TPU v7x, 256 devices: a whole 4x4x8 slice. The times are simulated.
256 devices in a mesh: outer: 32 (over z_hi, y, core), inner: 8 (over x, z_lo).
Axes of the slice: x: 4, y: 4, z: 8 (z_hi: 4, z_lo: 2; z = z_hi * 2 + z_lo), core: 2. Of those that a mesh axis runs over, the one named last changes fastest.
Arguments:
- tokens: bfloat16 [512, 512, 1024], P('outer', 'inner'), may hold values from -6 to 6
- gate: bfloat16 [512, 512, 1024], P('outer', 'inner'), may hold values from 0.25 to 2
- upstream: bfloat16 [512, 512, 1024], P('outer', 'inner'), may hold values from -6 to 6
- first_factor: bfloat16 [8, 512, 512], P('inner'), may hold values from -0.25 to 0.25
- second_factor: bfloat16 [8, 512, 512], P('inner'), may hold values from -0.25 to 0.25
Outputs:
- token_grad: bfloat16 [512, 512, 1024], P('outer', 'inner')
- first_grad: float32 [8, 512, 512], P('inner', 'outer')
- second_grad: float32 [8, 512, 512], P('inner', 'outer')
All inputs are finite; a program needn't handle non-finite values.
Results may differ from a plain program's by a relative error of at most 0.0057.
Values may be sent and summed in bfloat16 or wider, within the bound.
No kernel may reach another device: no remote copies, remote signals or barrier semaphores. Data moves between devices by JAX's collectives and lax.ppermute only.
A program may use at most 64 MiB of HBM per device.

v0:
```python
import jax
import jax.numpy as jnp
from jax import lax
from jax.sharding import PartitionSpec as P

ROWS = 512
COLS = 512
SLAB = 128


def as_slabs(array):
    return array.reshape(array.shape[0], array.shape[1], array.shape[2] // SLAB, SLAB)


def as_flat(array):
    return array.reshape(array.shape[0], array.shape[1], array.shape[2] * array.shape[3])


def local(tokens, gate, upstream, first_factor, second_factor):
    gated_grad = (gate.astype(jnp.float32) * upstream.astype(jnp.float32)).astype(jnp.bfloat16)
    tok_slab, grad_slab = (
        lax.all_to_all(tokens, "inner", split_axis=2, concat_axis=1, tiled=True),
        lax.all_to_all(gated_grad, "inner", split_axis=2, concat_axis=1, tiled=True),
    )
    tok_parts = as_slabs(tok_slab)
    mixed = jnp.einsum(
        "spq,rqsk->rpsk", first_factor, tok_parts, preferred_element_type=jnp.float32
    ).astype(jnp.bfloat16)
    mixed_cols, grad_cols = (
        lax.all_to_all(as_flat(mixed), "outer", split_axis=1, concat_axis=0, tiled=True),
        lax.all_to_all(grad_slab, "outer", split_axis=1, concat_axis=0, tiled=True),
    )
    mixed_parts = as_slabs(mixed_cols)
    grad_parts = as_slabs(grad_cols)
    second_part = jnp.einsum(
        "qcsk,rcsk->sqr", grad_parts, mixed_parts, preferred_element_type=jnp.float32
    )
    mixed_grad = jnp.einsum(
        "sqr,qcsk->rcsk", second_factor, grad_parts, preferred_element_type=jnp.float32
    ).astype(jnp.bfloat16)
    mixed_back = as_slabs(
        lax.all_to_all(as_flat(mixed_grad), "outer", split_axis=0, concat_axis=1, tiled=True)
    )
    first_part = jnp.einsum(
        "rpsk,rcsk->spc", mixed_back, tok_parts, preferred_element_type=jnp.float32
    )
    token_slab_grad = jnp.einsum(
        "spc,rpsk->rcsk", first_factor, mixed_back, preferred_element_type=jnp.float32
    ).astype(jnp.bfloat16)
    token_grad = lax.all_to_all(
        as_flat(token_slab_grad), "inner", split_axis=1, concat_axis=2, tiled=True
    )
    first_sum, second_sum = (
        lax.psum_scatter(first_part, "outer", scatter_dimension=1, tiled=True),
        lax.psum_scatter(second_part, "outer", scatter_dimension=1, tiled=True),
    )
    first_grad = first_sum * ROWS ** (-0.5) * SLAB ** (-0.5)
    second_grad = second_sum * COLS ** (-0.5) * SLAB ** (-0.5)
    return (token_grad, first_grad, second_grad)


def solution(mesh):
    in_specs = (
        P("outer", "inner", None),
        P("outer", "inner", None),
        P("outer", "inner", None),
        P("inner", None, None),
        P("inner", None, None),
    )
    out_specs = (P("outer", "inner", None), P("inner", "outer", None), P("inner", "outer", None))
    return jax.shard_map(local, mesh=mesh, in_specs=in_specs, out_specs=out_specs, check_vma=False)
```

profile of v0, /device:TPU:70, one launch (start us, length us, event | category | flops | bytes accessed | tf_op | source)
XLA Modules:
  0.0 469.4 jit_solution(14591417962425693312)
XLA Ops:
  7.2 0.0 copy-start
  7.2 3.4 multiply_convert_fusion
  10.6 4.9 %copy.60 = bf16[16,64,1024]{1,0,2:T(8,128)(2,1)} copy(bf16[16,64,1024]{2,1,0:T(8,128)(2,1)S(1)} %multiply_convert_fusion) | data formatting | bytes 4194304 | tf_op jit(solution)/shard_map/convert_element_type | solution.py:20
  15.4 7.6 %reshape.73 = bf16[8,2,65536]{2,1,0:T(2,128)(2,1)} reshape(bf16[1024,16,64]{2,1,0:T(8,128)(2,1)} %bitcast.70) | data formatting | bytes 4194304
  23.0 6.1 %all-to-all-start = ((bf16[8,2,65536]{2,1,0:T(2,128)(2,1)}), bf16[8,2,65536]{2,1,0:T(2,128)(2,1)S(1)}, u32[]{:S(2)}, u32[]{:S(2)}) async-start(bf16[8,2,65536]{2,1,0:T(2,128)(2,1)} %reshape.73), calls=%async_computation | async-start | bytes 4194304 | tf_op jit(solution)/shard_map/all_to_all | solution.py:23
  29.1 6.2 %copy.73 = bf16[16,64,1024]{1,0,2:T(8,128)(2,1)} copy(bf16[16,64,1024]{2,1,0:T(8,128)(2,1)} %param.5) | data formatting | bytes 4194304 | tf_op args[0]
  35.3 7.6 %reshape.75 = bf16[8,2,65536]{2,1,0:T(2,128)(2,1)} reshape(bf16[1024,16,64]{2,1,0:T(8,128)(2,1)} %bitcast.73) | data formatting | bytes 4194304
  42.9 11.4 %all-to-all-done = bf16[8,2,65536]{2,1,0:T(2,128)(2,1)S(1)} async-done(((bf16[8,2,65536]{2,1,0:T(2,128)(2,1)}), bf16[8,2,65536]{2,1,0:T(2,128)(2,1)S(1)}, u32[]{:S(2)}, u32[]{:S(2)}) %all-to-all-start) | async-done | bytes 2097184 | tf_op jit(solution)/shard_map/all_to_all | solution.py:23
  54.3 0.0 copy-start.1
  54.3 1.3 copy-done.1
  55.7 5.3 %all-to-all-start.4 = ((bf16[8,2,65536]{2,1,0:T(2,128)(2,1)}), bf16[8,2,65536]{2,1,0:T(2,128)(2,1)S(1)}, u32[]{:S(2)}, u32[]{:S(2)}) async-start(bf16[8,2,65536]{2,1,0:T(2,128)(2,1)} %reshape.75), calls=%async_computation.4 | async-start | bytes 4194304 | tf_op jit(solution)/shard_map/all_to_all | solution.py:22
  61.0 7.4 %reshape.74 = bf16[1024,16,64]{2,1,0:T(8,128)(2,1)} reshape(bf16[8,2,65536]{2,1,0:T(2,128)(2,1)} %copy-done.1) | data formatting | bytes 4194304
  68.4 6.7 %copy.84 = bf16[16,8,64,128]{3,0,2,1:T(8,128)(2,1)} copy(bf16[16,8,64,128]{2,0,3,1:T(8,128)(2,1)} %bitcast.71) | data formatting | bytes 4194304 | tf_op jit(solution)/shard_map/all_to_all | solution.py:23
  75.1 10.3 %all-to-all-done.4 = bf16[8,2,65536]{2,1,0:T(2,128)(2,1)S(1)} async-done(((bf16[8,2,65536]{2,1,0:T(2,128)(2,1)}), bf16[8,2,65536]{2,1,0:T(2,128)(2,1)S(1)}, u32[]{:S(2)}, u32[]{:S(2)}) %all-to-all-start.4) | async-done | bytes 2097184 | tf_op jit(solution)/shard_map/all_to_all | solution.py:22
  85.4 10.1 %all-to-all-start.1 = ((bf16[16,512,128]{2,0,1:T(8,128)(2,1)}), bf16[16,512,128]{2,0,1:T(8,128)(2,1)}, u32[]{:S(2)}, u32[]{:S(2)}) async-start(bf16[16,512,128]{2,0,1:T(8,128)(2,1)} %bitcast.74), calls=%async_computation.1 | async-start | bytes 4194304 | tf_op jit(solution)/shard_map/all_to_all | solution.py:31
  95.5 5.0 %reshape.76 = bf16[1024,16,64]{2,1,0:T(8,128)(2,1)} reshape(bf16[8,2,65536]{2,1,0:T(2,128)(2,1)S(1)} %all-to-all-done.4) | data formatting | bytes 4194304
  100.5 4.6 copy.74
  105.1 0.0 copy-start.4
  105.1 0.0 copy-done
  105.2 2.6 convert_bitcast_fusion
  107.8 0.0 copy-done.4
  107.8 4.5 copy.76
  112.3 34.0 %all-to-all-done.1 = bf16[16,512,128]{2,0,1:T(8,128)(2,1)} async-done(((bf16[16,512,128]{2,0,1:T(8,128)(2,1)}), bf16[16,512,128]{2,0,1:T(8,128)(2,1)}, u32[]{:S(2)}, u32[]{:S(2)}) %all-to-all-start.1) | async-done | bytes 2097184 | tf_op jit(solution)/shard_map/all_to_all | solution.py:31
  146.3 6.7 %all-to-all-start.5 = ((bf16[16,512,128]{2,0,1:T(8,128)(2,1)}), bf16[16,512,128]{2,0,1:T(8,128)(2,1)S(1)}, u32[]{:S(2)}, u32[]{:S(2)}) async-start(bf16[16,512,128]{2,0,1:T(8,128)(2,1)} %copy.76), calls=%async_computation.6 | async-start | bytes 4194304 | tf_op jit(solution)/shard_map/all_to_all | solution.py:30
  153.0 0.0 copy-start.5
  153.0 2.2 copy.65
  155.2 0.0 copy-start.2
  155.2 1.3 copy-done.2
  156.5 0.0 copy-done.5
  156.5 2.7 convert_bitcast_fusion.2
  159.2 4.5 copy.67
  163.7 38.9 %all-to-all-done.5 = bf16[16,512,128]{2,0,1:T(8,128)(2,1)S(1)} async-done(((bf16[16,512,128]{2,0,1:T(8,128)(2,1)}), bf16[16,512,128]{2,0,1:T(8,128)(2,1)S(1)}, u32[]{:S(2)}, u32[]{:S(2)}) %all-to-all-start.5) | async-done | bytes 2097184 | tf_op jit(solution)/shard_map/all_to_all | solution.py:30
  202.7 7.0 %all-to-all-start.2 = ((bf16[512,16,128]{2,1,0:T(8,128)(2,1)}), bf16[512,16,128]{2,1,0:T(8,128)(2,1)}, u32[]{:S(2)}, u32[]{:S(2)}) async-start(bf16[512,16,128]{2,1,0:T(8,128)(2,1)} %copy.67), calls=%async_computation.2 | async-start | bytes 4194304 | tf_op jit(solution)/shard_map/all_to_all | solution.py:42
  209.7 1.9 copy.78
  211.6 47.7 %all-to-all-done.2 = bf16[512,16,128]{2,1,0:T(8,128)(2,1)} async-done(((bf16[512,16,128]{2,1,0:T(8,128)(2,1)}), bf16[512,16,128]{2,1,0:T(8,128)(2,1)}, u32[]{:S(2)}, u32[]{:S(2)}) %all-to-all-start.2) | async-done | bytes 2097184 | tf_op jit(solution)/shard_map/all_to_all | solution.py:42
  259.3 2.1 copy.68
  261.4 0.0 copy-start.3
  261.4 1.4 copy-done.3
  262.8 1.3 convert_bitcast_fusion.1
  264.1 3.1 copy.70
  267.1 5.0 %all-to-all-start.3 = ((bf16[16,512,128]{2,0,1:T(8,128)(2,1)}), bf16[16,512,128]{2,0,1:T(8,128)(2,1)S(1)}, u32[]{:S(2)}, u32[]{:S(2)}) async-start(bf16[16,512,128]{2,0,1:T(8,128)(2,1)} %copy.70), calls=%async_computation.3 | async-start | bytes 4194304 | tf_op jit(solution)/shard_map/all_to_all | solution.py:50
  272.1 0.0 reduce-scatter.5.cloned.1.call-start
  272.1 4.5 fusion.3
  276.6 0.0 reduce-scatter.5.cloned.1.call-update
  276.7 0.0 reduce-scatter.3.cloned.1.call-start
  276.7 4.5 convolution_bitcast_fusion
  281.2 0.0 reduce-scatter.3.cloned.1.call-update
  281.2 82.2 %reduce-scatter.5.cloned.1.call-done = f32[1,16,512]{2,1,0:T(8,128)} async-done(((f32[1,512,512]{2,1,0:T(8,128)}), f32[1,16,512]{2,1,0:T(8,128)}) %reduce-scatter.5.cloned.1.call-update) | async-done | bytes 32784 | tf_op jit(solution)/shard_map/reduce_scatter | solution.py:55
  363.5 1.4 broadcast_multiply_fusion
  364.8 89.5 %reduce-scatter.3.cloned.1.call-done = f32[1,16,512]{2,1,0:T(8,128)} async-done(((f32[1,512,512]{2,1,0:T(8,128)}), f32[1,16,512]{2,1,0:T(8,128)}) %reduce-scatter.3.cloned.1.call-update) | async-done | bytes 32784 | tf_op jit(solution)/shard_map/reduce_scatter | solution.py:54
  454.3 1.4 broadcast_multiply_fusion.1
  455.7 0.0 all-to-all-done.3
  455.7 2.7 copy.72
  458.4 4.2 all_to_all.83
Async XLA Ops:
  7.2 98.0 %copy-start = (bf16[1,512,512]{2,1,0:T(8,128)(2,1)S(1)}, bf16[1,512,512]{2,1,0:T(8,128)(2,1)}, u32[]{:S(2)}) copy-start(bf16[1,512,512]{2,1,0:T(8,128)(2,1)} %param.8) | copy-start | bytes 1572868
  23.0 31.3 %all-to-all-start = ((bf16[8,2,65536]{2,1,0:T(2,128)(2,1)}), bf16[8,2,65536]{2,1,0:T(2,128)(2,1)S(1)}, u32[]{:S(2)}, u32[]{:S(2)}) async-start(bf16[8,2,65536]{2,1,0:T(2,128)(2,1)} %reshape.73), calls=%async_computation | async-start | bytes 4194304 | tf_op jit(solution)/shard_map/all_to_all | solution.py:23
  54.3 1.3 copy-start.1
  55.7 29.7 %all-to-all-start.4 = ((bf16[8,2,65536]{2,1,0:T(2,128)(2,1)}), bf16[8,2,65536]{2,1,0:T(2,128)(2,1)S(1)}, u32[]{:S(2)}, u32[]{:S(2)}) async-start(bf16[8,2,65536]{2,1,0:T(2,128)(2,1)} %reshape.75), calls=%async_computation.4 | async-start | bytes 4194304 | tf_op jit(solution)/shard_map/all_to_all | solution.py:22
  85.4 60.9 %all-to-all-start.1 = ((bf16[16,512,128]{2,0,1:T(8,128)(2,1)}), bf16[16,512,128]{2,0,1:T(8,128)(2,1)}, u32[]{:S(2)}, u32[]{:S(2)}) async-start(bf16[16,512,128]{2,0,1:T(8,128)(2,1)} %bitcast.74), calls=%async_computation.1 | async-start | bytes 4194304 | tf_op jit(solution)/shard_map/all_to_all | solution.py:31
  105.1 2.7 copy-start.4
  146.3 56.4 %all-to-all-start.5 = ((bf16[16,512,128]{2,0,1:T(8,128)(2,1)}), bf16[16,512,128]{2,0,1:T(8,128)(2,1)S(1)}, u32[]{:S(2)}, u32[]{:S(2)}) async-start(bf16[16,512,128]{2,0,1:T(8,128)(2,1)} %copy.76), calls=%async_computation.6 | async-start | bytes 4194304 | tf_op jit(solution)/shard_map/all_to_all | solution.py:30
  153.0 3.5 copy-start.5
  155.2 1.3 copy-start.2
  202.7 56.6 %all-to-all-start.2 = ((bf16[512,16,128]{2,1,0:T(8,128)(2,1)}), bf16[512,16,128]{2,1,0:T(8,128)(2,1)}, u32[]{:S(2)}, u32[]{:S(2)}) async-start(bf16[512,16,128]{2,1,0:T(8,128)(2,1)} %copy.67), calls=%async_computation.2 | async-start | bytes 4194304 | tf_op jit(solution)/shard_map/all_to_all | solution.py:42
  261.4 1.4 copy-start.3
  267.1 188.5 %all-to-all-start.3 = ((bf16[16,512,128]{2,0,1:T(8,128)(2,1)}), bf16[16,512,128]{2,0,1:T(8,128)(2,1)S(1)}, u32[]{:S(2)}, u32[]{:S(2)}) async-start(bf16[16,512,128]{2,0,1:T(8,128)(2,1)} %copy.70), calls=%async_computation.3 | async-start | bytes 4194304 | tf_op jit(solution)/shard_map/all_to_all | solution.py:50
  272.1 91.4 %reduce-scatter.5.cloned.1.call-start = ((), (), s32[]{:S(2)}) async-start(), calls=%async_computation.9 | async-start | bytes 1081344 | tf_op jit(solution)/shard_map/reduce_scatter | solution.py:55
  276.7 177.6 %reduce-scatter.3.cloned.1.call-start = ((), (), s32[]{:S(2)}) async-start(), calls=%async_computation.8 | async-start | bytes 1081344 | tf_op jit(solution)/shard_map/reduce_scatter | solution.py:54
Sparse Core Ops, SparseCore 0:
  276.8 86.6 reduce-scatter.4
  367.7 86.5 reduce-scatter.2
where the time goes:
time: 473 us; the launch traced here: 469 us
  waiting for transfers between devices  314 us (66%)
  local copies, waits for them, and re-layouts  79.2 us (17%)
  starting transfers between devices  40.2 us (8%)
  matrix products  15.6 us (3%)
  between operations  14.2 us (3%)
  other arithmetic  6.13 us (1%)
    reduce_scatter x1, waiting for transfers between devices, local(): lax.psum_scatter(first_part, 'outer', scatter_dimension=1, tiled=True)  89.5 us
    reduce_scatter x1, waiting for transfers between devices, local(): lax.psum_scatter(second_part, 'outer', scatter_dimension=1, tiled=True)  82.2 us
    all_to_all x1, waiting for transfers between devices, local(): lax.all_to_all(as_flat(mixed_grad), 'outer', split_axis=0, concat_axis=1,...  47.7 us
    all_to_all x1, waiting for transfers between devices, local(): lax.all_to_all(as_flat(mixed), 'outer', split_axis=1, concat_axis=0, tile...  38.9 us
    unnamed x17, local copies, waits for them, and re-layouts  37.8 us
    all_to_all x1, waiting for transfers between devices, local(): lax.all_to_all(grad_slab, 'outer', split_axis=1, concat_axis=0, tiled=True)  34 us
    reshape x3, local copies, waits for them, and re-layouts, as_flat(): array.reshape(array.shape[0], array.shape[1], array.shape[2] * array.shap...  12.1 us
    all_to_all x1, waiting for transfers between devices, local(): lax.all_to_all(gated_grad, 'inner', split_axis=2, concat_axis=1, tiled=True)  11.4 us
  transfers between devices with their start and end apart: 8, of which 7 were waited for; matrix products, arithmetic and copies ran while one was open for 14% of the time, Pallas kernels for 0%

commit v1 on v0

v1 whole, which is shorter than its diff:
```python
import functools

import jax
import jax.numpy as jnp
from jax import lax
from jax.experimental import pallas as pl
from jax.experimental.pallas import tpu as pltpu
from jax.sharding import Mesh, PartitionSpec as P

ROWS = 512
COLS = 512
SLAB = 128
BF = jnp.bfloat16
F32 = jnp.float32
ZYC = ("zh", "y", "core", "zl")
PLANE = ("y", "core", "x")
PARAMS = pltpu.CompilerParams(vmem_limit_bytes=48 * 1024 * 1024)
VM = pl.BlockSpec(memory_space=pltpu.VMEM)
SM = pl.BlockSpec(memory_space=pltpu.SMEM)


def call(kernel, outs, scratch=(), n_in=1, flops=0, moved=4 << 20):
    return pl.pallas_call(
        kernel,
        out_shape=outs,
        in_specs=[SM] + [VM] * n_in,
        out_specs=jax.tree.map(lambda _: VM, outs),
        scratch_shapes=list(scratch),
        compiler_params=PARAMS,
        cost_estimate=pl.CostEstimate(flops=flops, bytes_accessed=moved, transcendentals=0),
    )


def shape(*dims, dtype=BF):
    return jax.ShapeDtypeStruct(dims, dtype)


def gate_kernel(gate, up, out):
    prod = gate[...].astype(F32) * up[...].astype(F32)
    out[0, :, 0] = jnp.swapaxes(prod, 0, 1).astype(BF).reshape(8, 8, 16, SLAB)


def gate_call(gate, up):
    return pl.pallas_call(
        gate_kernel,
        grid=(8,),
        out_shape=shape(4, 8, 2, 8, 16, SLAB),
        in_specs=[pl.BlockSpec((16, 64, SLAB), lambda s: (0, 0, s))] * 2,
        out_specs=pl.BlockSpec((1, 8, 1, 8, 16, SLAB), lambda s: (s // 2, 0, s % 2, 0, 0, 0)),
        compiler_params=PARAMS,
        cost_estimate=pl.CostEstimate(flops=1 << 20, bytes_accessed=6 << 20, transcendentals=0),
    )(gate, up)


def factor_kernel(pos, *refs):
    yc = pos[2]
    f1, f2t, f1tp, full = refs[8:]
    for s in range(8):
        rows = pl.ds(pl.multiple_of(lax.rem(yc + 8 - s, 8) * 64, 64), 64)
        full[:, rows, :] = refs[s][...].astype(F32)
    f1[...] = full[0].astype(BF)
    f2t[...] = full[1].T.astype(BF)
    ordered = jnp.concatenate(
        [full[0, k * 64 + c * 8 : k * 64 + c * 8 + 8, :] for c in range(8) for k in range(8)], axis=0
    )
    f1tp[...] = ordered.T.astype(BF)


def second_apply_kernel(pos, f2t, g, out, flat, swap):
    for k in range(16):
        flat[:, k * SLAB : (k + 1) * SLAB] = g[:, :, k // 8, k % 8].reshape(ROWS, SLAB)

    def body(zh, _):
        rows = pl.ds(pl.multiple_of(zh * 128, 128), 128)
        for k in range(0, 16, 2):
            part = jnp.dot(f2t[rows, :], flat[:, k * SLAB : (k + 2) * SLAB], preferred_element_type=F32)
            swap[pl.ds(k, 128, stride=16), :] = part[:, :SLAB]
            swap[pl.ds(k + 1, 128, stride=16), :] = part[:, SLAB:]
        for yc in range(8):
            tile = swap[yc * 256 : (yc + 1) * 256, :].astype(BF).reshape(4, 4, 16, SLAB)
            for x in range(4):
                out[yc, x, zh] = tile[x]
        return 0

    lax.fori_loop(0, 4, body, 0)


def first_apply_kernel(pos, f1tp, m, o0, o1, o2, o3):
    x = pos[0]
    for s, out in enumerate((o0, o1, o2, o3)):
        rows = pl.ds(pl.multiple_of(lax.rem(x + s, 4) * 128, 128), 128)
        left = f1tp[rows, :]
        for zh in range(4):
            for r in range(0, 4, 2):
                right = jnp.concatenate(
                    [m[:, :, zh, r].reshape(COLS, SLAB), m[:, :, zh, r + 1].reshape(COLS, SLAB)], axis=1
                )
                part = jnp.dot(left, right, preferred_element_type=F32).astype(BF)
                out[zh, r] = part[:, :SLAB].reshape(2, 64, SLAB)
                out[zh, r + 1] = part[:, SLAB:].reshape(2, 64, SLAB)


def token_cut_kernel(pos, x0, x1, x2, x3, *outs):
    x, z = pos[0], pos[1]
    for s, block in enumerate((x0, x1, x2, x3)):
        source = lax.rem(x + 4 - s, 4)
        for t, out in enumerate(outs):
            lanes = pl.ds(pl.multiple_of(lax.rem(z + t, 8) * SLAB, SLAB), SLAB)
            out[source] = block[:, :, lanes]


def grad_cut_kernel(pos, x0, x1, x2, x3, *outs):
    x, z = pos[0], pos[1]
    for s, block in enumerate((x0, x1, x2, x3)):
        source = lax.rem(x + 4 - s, 4)
        for t, out in enumerate(outs):
            owner = lax.rem(z + t, 8)
            for r in range(4):
                out[source, r] = block[owner // 2, r, lax.rem(owner, 2)]


def grad_join_kernel(pos, *refs):
    z = pos[1]
    out = refs[8]
    for t in range(8):
        lanes = pl.ds(pl.multiple_of(lax.rem(z + 8 - t, 8) * SLAB, SLAB), SLAB)
        out[:, :, lanes] = refs[t][...].reshape(16, 64, SLAB)


def mix_kernel(pos, f1, p0, p1, p2, p3, p4, p5, p6, p7, mixed, tokw, tok, swap):
    z = pos[1]
    for t, block in enumerate((p0, p1, p2, p3, p4, p5, p6, p7)):
        source = lax.rem(z + 8 - t, 8)
        for r in range(4):
            for x in range(4):
                tok[source // 2, r, x, lax.rem(source, 2)] = block[x, r]
    for k in range(16):
        tokw[:, k * SLAB : (k + 1) * SLAB] = tok[k // 4, k % 4].reshape(COLS, SLAB)

    def body(b, _):
        rows = pl.ds(pl.multiple_of(b * 128, 128), 128)
        for k in range(0, 16, 2):
            part = jnp.dot(f1[rows, :], tokw[:, k * SLAB : (k + 2) * SLAB], preferred_element_type=F32)
            swap[pl.ds(k, 128, stride=16), :] = part[:, :SLAB]
            swap[pl.ds(k + 1, 128, stride=16), :] = part[:, SLAB:]
        for zl in range(2):
            tile = swap[zl * 1024 : (zl + 1) * 1024, :].astype(BF).reshape(8, 8, 16, SLAB)
            for yc in range(8):
                mixed[yc, b, zl] = tile[yc]
        return 0

    lax.fori_loop(0, 4, body, 0)


def first_kernel(pos, m, tokw, first, mgw):
    for k in range(16):
        mgw[:, k * SLAB : (k + 1) * SLAB] = m[:, :, k // 4, k % 4].reshape(COLS, SLAB)
    for yc in range(8):
        left = mgw[yc * 64 : (yc + 1) * 64, :]
        part = lax.dot_general(left, tokw[...], (((1,), (1,)), ((), ())), preferred_element_type=F32)
        for x in range(4):
            for zl in range(2):
                at = (x * 2 + zl) * 8
                half = (yc % 2) * 8
                first[zl * 2 + yc // 4, (yc // 2) % 2, x, half : half + 8, :] = part[at : at + 8, :]


def second_kernel(pos, g, mixed, first, parts, flat, mixw):
    parts[:, :, :, 0] = first[...]
    for k in range(16):
        lanes = slice(k * SLAB, (k + 1) * SLAB)
        flat[:, lanes] = g[:, :, k // 8, k % 8].reshape(ROWS, SLAB)
        mixw[:, lanes] = mixed[:, :, k // 8, k % 8].reshape(ROWS, SLAB)
    for zh in range(4):
        part = lax.dot_general(
            flat[zh * 128 : (zh + 1) * 128, :], mixw[...], (((1,), (1,)), ((), ())), preferred_element_type=F32
        )
        for y in range(4):
            for core in range(2):
                at = (y * 2 + core) * 16
                parts[y, core, zh, 1] = part[at : at + 16, :]


def sum_kernel(pos, parts, out):
    total = parts[0]
    for k in range(1, 32):
        total = total + parts[k]
    place = lax.broadcasted_iota(jnp.int32, (ROWS, ROWS), 0)
    row = lax.broadcasted_iota(jnp.int32, (ROWS, ROWS), 1)
    want = ((row >> 4) & 7) * 64 + ((row >> 2) & 3) * 16 + (row >> 7) * 4 + (row & 3)
    order = (place == want).astype(F32)
    out[0] = total[0] * (ROWS**-0.5 * SLAB**-0.5)
    second = jnp.dot(total[1], order, precision=lax.Precision.HIGHEST, preferred_element_type=F32)
    out[1] = second * (COLS**-0.5 * SLAB**-0.5)


def shifts(count):
    return lambda s: [(k, (k + s) % count) for k in range(count)]


def local(tokens, gate, upstream, first_factor, second_factor):
    zh, zl = lax.axis_index("zh"), lax.axis_index("zl")
    x, yc = lax.axis_index("x"), lax.axis_index("y") * 2 + lax.axis_index("core")
    z = zh * 2 + zl
    pos = jnp.stack([x, z, yc]).astype(jnp.int32)

    sent = gate_call(gate, upstream)
    grad = lax.all_to_all(sent.reshape(64, 8, 16, SLAB), ZYC, 0, 0, tiled=True).reshape(4, 8, 2, 8, 16, SLAB)

    x_step, yc_step, z_step = shifts(4), shifts(8), shifts(8)
    both = jnp.concatenate([first_factor, second_factor], 0)
    eighth = lax.dynamic_slice_in_dim(both, yc * 64, 64, 1)
    got = eighth
    for s in range(1, 4):
        came = lax.ppermute(eighth, ("zh", "x"), [(k * 4 + k, k * 4 + (k + s) % 4) for k in range(4)])
        got = jnp.where(x == (zh + s) % 4, came, got)
    eighths = [got] + [lax.ppermute(got, ("y", "core"), yc_step(s)) for s in range(1, 8)]
    f1, f2t, f1tp = call(
        factor_kernel,
        [shape(COLS, COLS), shape(ROWS, ROWS), shape(COLS, COLS)],
        [pltpu.VMEM((2, COLS, COLS), F32)],
        n_in=8,
    )(pos, *eighths)

    tok_x = []
    for s in range(4):
        piece = lax.dynamic_slice_in_dim(tokens, ((x + s) % 4) * 4, 4, 0)
        tok_x.append(piece if s == 0 else lax.ppermute(piece, "x", x_step(s)))
    tok_cut = call(token_cut_kernel, [shape(4, 4, 64, SLAB)] * 8, n_in=4)(pos, *tok_x)

    tok_cut, grad, f2t, f1tp, f1 = lax.optimization_barrier((tok_cut, grad, f2t, f1tp, f1))
    mg_sent = call(
        second_apply_kernel,
        shape(8, 4, 4, 4, 16, SLAB),
        [pltpu.VMEM((ROWS, 16 * SLAB), BF), pltpu.VMEM((128 * 16, SLAB), F32)],
        n_in=2,
        flops=1 << 30,
    )(pos, f2t, grad)
    tok_z = [tok_cut[0]] + [lax.ppermute(tok_cut[t], ("zh", "zl"), z_step(t)) for t in range(1, 8)]
    mg = lax.all_to_all(mg_sent.reshape(32, 16, 16, SLAB), PLANE, 0, 0, tiled=True).reshape(8, 4, 4, 4, 16, SLAB)

    tg_sent = call(first_apply_kernel, [shape(4, 4, 2, 64, SLAB)] * 4, n_in=2, flops=1 << 30)(pos, f1tp, mg)
    tg_sent, mg = lax.optimization_barrier((tg_sent, mg))
    tg_x = [tg_sent[0]] + [lax.ppermute(tg_sent[s], "x", x_step(s)) for s in range(1, 4)]
    tg_cut = call(grad_cut_kernel, [shape(4, 4, 64, SLAB)] * 8, n_in=4)(pos, *tg_x)
    wide = pltpu.VMEM((ROWS, 16 * SLAB), BF)
    mixed_sent, tokw = call(
        mix_kernel,
        [shape(8, 4, 2, 8, 16, SLAB), shape(COLS, 16 * SLAB)],
        [pltpu.VMEM((4, 4, 4, 2, 64, SLAB), BF), pltpu.VMEM((128 * 16, SLAB), F32)],
        n_in=9,
        flops=1 << 30,
    )(pos, f1, *tok_z)
    tg_cut, mixed_sent = lax.optimization_barrier((tg_cut, mixed_sent))
    tg_z = [tg_cut[0]] + [lax.ppermute(tg_cut[t], ("zh", "zl"), z_step(t)) for t in range(1, 8)]
    mixed = lax.all_to_all(mixed_sent.reshape(32, 16, 16, SLAB), PLANE, 0, 0, tiled=True).reshape(8, 4, 2, 8, 16, SLAB)
    first_part = call(first_kernel, shape(4, 2, 4, 16, COLS, dtype=F32), [wide], n_in=2, flops=1 << 30)(pos, mg, tokw)
    mixed, first_part, tg_z[3:6] = lax.optimization_barrier((mixed, first_part, tg_z[3:6]))
    parts = call(
        second_kernel, shape(4, 2, 4, 2, 16, ROWS, dtype=F32), [wide, wide], n_in=3, flops=1 << 30
    )(pos, grad, mixed, first_part)
    parts = lax.all_to_all(parts.reshape(32, 2, 16, 512), PLANE, 0, 0, tiled=True)
    parts, tg_z = lax.optimization_barrier((parts, tg_z))
    sums = call(sum_kernel, shape(2, 16, 512, dtype=F32))(pos, parts)
    sums = lax.ppermute(sums, ("zh", "x"), [(a * 4 + b, b * 4 + a) for a in range(4) for b in range(4)])
    token_grad = call(grad_join_kernel, shape(16, 64, 1024), n_in=8)(pos, *tg_z)
    return token_grad, sums[:1], sums[1:]


def solution(mesh):
    fine = Mesh(mesh.devices.reshape(4, 4, 2, 4, 2), ("zh", "y", "core", "x", "zl"))
    outer, inner = ("zh", "y", "core"), ("x", "zl")
    grid = P(outer, inner, None)
    factor = P(inner, None, None)
    return jax.shard_map(
        local,
        mesh=fine,
        in_specs=(grid, grid, grid, factor, factor),
        out_specs=(grid, P(inner, outer, None), P(inner, outer, None)),
        check_vma=False,
    )
```

time: 473 us -> 274 us (0.58)
  waiting for transfers between devices: 314 us -> 114 us
  starting transfers between devices: 40.2 us -> 88.1 us
  local copies, waits for them, and re-layouts: 79.2 us -> 32 us
  Pallas kernels: 0 us -> 37.1 us
  matrix products: 15.6 us -> 0 us
  between operations: 14.2 us -> 1.01 us
  other arithmetic: 6.13 us -> 0.16 us
    reduce_scatter x2 -> x0, waiting for transfers between devices: 172 us -> none  [the longest x1 89.5 us: local(): lax.psum_scatter(first_part, 'outer', scatter_dimension=1, tiled=True)]
    all_to_all x6 -> x4, waiting for transfers between devices: 142 us -> 19.7 us  [the longest x1 15.7 us: local(): lax.all_to_all(mg_sent.reshape(32, 16, 16, SLAB), PLANE, 0, 0, tiled=True)]
    ppermute x0 -> x31, waiting for transfers between devices: none -> 94.6 us  [the longest x7 32.6 us: local(): lax.ppermute(tg_cut[t], ('zh', 'zl'), z_step(t))]
    ppermute x0 -> x31, starting transfers between devices: none -> 55.5 us  [the longest x7 17.1 us: local(): lax.ppermute(tok_cut[t], ('zh', 'zl'), z_step(t))]
    pallas_call x0 -> x11, Pallas kernels: none -> 37.1 us  [the longest x1 6.85 us: local(): call(first_kernel, shape(4, 2, 4, 16, COLS, dtype=F32), [wide], n_in=2, f...]
    all_to_all x7 -> x0, local copies, waits for them, and re-layouts: 24.5 us -> none  [the longest x2 6.84 us: local(): lax.all_to_all(as_flat(token_slab_grad), 'inner', split_axis=1, concat_ax...]
    dot_general x5 -> x0, matrix products: 15.6 us -> none  [the longest x1 4.55 us: local(): jnp.einsum('qcsk,rcsk->sqr', grad_parts, mixed_parts, preferred_element_t...]
    reshape x3 -> x0, local copies, waits for them, and re-layouts: 12.1 us -> none  [as_flat(): array.reshape(array.shape[0], array.shape[1], array.shape[2] * array.shap...]
  transfers between devices with their start and end apart: 8 -> 35, of which waited for: 7 -> 17; matrix products, arithmetic and copies ran while one was open for 14% -> 1% of each run, Pallas kernels for 0% -> 8%
where the time goes in v1:
time: 274 us; the launch traced here: 273 us
  waiting for transfers between devices  114 us (42%)
  starting transfers between devices  88.1 us (32%)
  Pallas kernels  37.1 us (14%)
  local copies, waits for them, and re-layouts  32 us (12%)
    ppermute x7, waiting for transfers between devices, local(): lax.ppermute(tg_cut[t], ('zh', 'zl'), z_step(t))  32.6 us
    unnamed x90, local copies, waits for them, and re-layouts  28.7 us
    ppermute x7, waiting for transfers between devices, local(): lax.ppermute(tok_cut[t], ('zh', 'zl'), z_step(t))  26.1 us
    ppermute x7, waiting for transfers between devices, local(): lax.ppermute(got, ('y', 'core'), yc_step(s))  23.1 us
    ppermute x7, starting transfers between devices, local(): lax.ppermute(tok_cut[t], ('zh', 'zl'), z_step(t))  17.1 us
    all_to_all x1, waiting for transfers between devices, local(): lax.all_to_all(mg_sent.reshape(32, 16, 16, SLAB), PLANE, 0, 0, tiled=True)  15.7 us
    ppermute x7, starting transfers between devices, local(): lax.ppermute(tg_cut[t], ('zh', 'zl'), z_step(t))  13.2 us
    all_to_all x1, starting transfers between devices, local(): lax.all_to_all(sent.reshape(64, 8, 16, SLAB), ZYC, 0, 0, tiled=True)  11.4 us
  transfers between devices with their start and end apart: 35, of which 17 were waited for; matrix products, arithmetic and copies ran while one was open for 1% of the time, Pallas kernels for 8%

profile of v1, /device:TPU:70, one launch (start us, length us, event | category | flops | bytes accessed | tf_op | source)
XLA Modules:
  0.0 272.6 jit_solution(8657795918808106072)
XLA Ops:
  0.6 1.6 copy-done.3
  2.2 5.3 %shard_map.77 = bf16[4,8,2,8,16,128]{5,4,3,2,1,0:T(8,128)(2,1)S(1)} custom-call(bf16[16,64,1024]{2,1,0:T(8,128)(2,1)S(1)} %copy-done.3, bf16[16,64,1024]{2,1,0:T(8,128)(2,1)} %up.1), custom_call_target="tpu_custom_call" | custom-call | flops 1048576 | bytes 6291456 | tf_op jit(solution)/shard_map/pallas_call | solution.py:44
  7.5 1.3 copy-done
  8.8 11.4 %all-to-all-start = ((bf16[64,8,16,128]{3,2,1,0:T(8,128)(2,1)}), bf16[64,8,16,128]{3,2,1,0:T(8,128)(2,1)S(1)}, u32[]{:S(2)}, u32[]{:S(2)}) async-start(bf16[64,8,16,128]{3,2,1,0:T(8,128)(2,1)} %bitcast.12), calls=%async_computation | async-start | bytes 4194304 | tf_op jit(solution)/shard_map/all_to_all | solution.py:208
  20.3 1.3 collective-permute-start.4
  22.3 1.3 collective-permute-start.5
  23.6 6.5 %collective-permute-done.4 = bf16[2,64,512]{2,1,0:T(8,128)(2,1)S(1)} collective-permute-done((bf16[2,64,512]{2,1,0:T(8,128)(2,1)S(1)}, bf16[2,64,512]{2,1,0:T(8,128)(2,1)S(1)}, u32[]{:S(2)}, u32[]{:S(2)}) %collective-permute-start.4) | collective-permute-done | bytes 131104 | tf_op jit(solution)/shard_map/ppermute | solution.py:215
  30.1 0.9 collective-permute-start.12
  31.0 2.7 constant_dynamic-slice_fusion
  33.7 3.6 %collective-permute-start.2 = (bf16[4,64,1024]{2,1,0:T(8,128)(2,1)}, bf16[4,64,1024]{2,1,0:T(8,128)(2,1)S(1)}, u32[]{:S(2)}, u32[]{:S(2)}) collective-permute-start(bf16[4,64,1024]{2,1,0:T(8,128)(2,1)} %get-tuple-element.133), channel_id=1, source_target_pairs={{0,6},{2,0},{4,2},{6,4},{1,7},{3,1},{5,3},{7,5},{8,14},{10,8},{12,... | collective-permute-start | bytes 1572872 | tf_op jit(solution)/shard_map/ppermute | solution.py:228
  37.3 2.1 collective-permute-start.1
  39.4 1.1 collective-permute-start.11
  40.5 9.3 %collective-permute-done.11.refs_6_ = bf16[2,64,512]{2,1,0:T(8,128)(2,1)S(1)} collective-permute-done((bf16[2,64,512]{2,1,0:T(8,128)(2,1)S(1)}, bf16[2,64,512]{2,1,0:T(8,128)(2,1)S(1)}, u32[]{:S(2)}, u32[]{:S(2)}) %collective-permute-start.11) | collective-permute-done | bytes 131104 | tf_op jit(solution)/shard_map/ppermute | solution.py:217
  50.5 3.1 %collective-permute-start.8 = (bf16[2,64,512]{2,1,0:T(8,128)(2,1)S(1)}, bf16[2,64,512]{2,1,0:T(8,128)(2,1)S(1)}, u32[]{:S(2)}, u32[]{:S(2)}) collective-permute-start(bf16[2,64,512]{2,1,0:T(8,128)(2,1)S(1)} %select_select_fusion.refs_0_), channel_id=1, source_target_pairs={{0,24},{8,32},{16,40},{24,48},{32,56},{40,0},{48,8},{56,16},{1,25}... | collective-permute-start | bytes 393224 | tf_op jit(solution)/shard_map/ppermute | solution.py:217
  53.6 8.7 %collective-permute-done.9.refs_4_ = bf16[2,64,512]{2,1,0:T(8,128)(2,1)S(1)} collective-permute-done((bf16[2,64,512]{2,1,0:T(8,128)(2,1)S(1)}, bf16[2,64,512]{2,1,0:T(8,128)(2,1)S(1)}, u32[]{:S(2)}, u32[]{:S(2)}) %collective-permute-start.9) | collective-permute-done | bytes 131104 | tf_op jit(solution)/shard_map/ppermute | solution.py:217
  63.7 2.3 collective-permute-start.6
  66.1 5.1 %collective-permute-done.7.refs_2_ = bf16[2,64,512]{2,1,0:T(8,128)(2,1)} collective-permute-done((bf16[2,64,512]{2,1,0:T(8,128)(2,1)S(1)}, bf16[2,64,512]{2,1,0:T(8,128)(2,1)}, u32[]{:S(2)}, u32[]{:S(2)}) %collective-permute-start.7) | collective-permute-done | bytes 131104 | tf_op jit(solution)/shard_map/ppermute | solution.py:217
  71.2 0.9 copy-done.21
  72.1 0.9 copy-done.23
  73.0 0.9 copy-done.25
  73.9 1.5 shard_map.78
  76.1 0.8 copy-done.26
  77.7 1.8 shard_map.76
  84.5 1.0 copy-done.7
  85.5 3.6 %shard_map.79 = bf16[8,4,4,4,16,128]{5,4,3,2,1,0:T(8,128)(2,1)S(1)} custom-call(s32[3]{0:T(128)S(1)} %pad_add_fusion.pos, bf16[512,512]{1,0:T(8,128)(2,1)S(1)} %copy-done.7, bf16[4,8,2,8,16,128]{5,4,3,2,1,0:T(8,128)(2,1)S(1)} %bitcast.10), custom_call_target="tpu_custom_call" | custom-call | flops 1073741824 | bytes 4194304 | tf_op jit(solution)/shard_map/pallas_call | solution.py:232
  89.1 1.3 copy-done.1
  90.4 6.8 %all-to-all-start.1 = ((bf16[32,16,16,128]{3,2,1,0:T(8,128)(2,1)}), bf16[32,16,16,128]{3,2,1,0:T(8,128)(2,1)}, u32[]{:S(2)}, u32[]{:S(2)}) async-start(bf16[32,16,16,128]{3,2,1,0:T(8,128)(2,1)} %bitcast.13), calls=%async_computation.1 | async-start | bytes 4194304 | tf_op jit(solution)/shard_map/all_to_all | solution.py:240
  97.3 4.2 %collective-permute-start.17 = (bf16[4,4,64,128]{3,2,1,0:T(8,128)(2,1)}, bf16[4,4,64,128]{3,2,1,0:T(8,128)(2,1)}, u32[]{:S(2)}, u32[]{:S(2)}) collective-permute-start(bf16[4,4,64,128]{3,2,1,0:T(8,128)(2,1)} %copy-done.41), channel_id=1, source_target_pairs={{0,64},{1,65},{64,128},{65,129},{128,192},{129,193},{192,0},{193,1... | collective-permute-start | bytes 786440 | tf_op jit(solution)/shard_map/ppermute | solution.py:239
  101.5 0.9 collective-permute-start.18
  102.4 1.9 collective-permute-start.19
  104.4 3.1 %collective-permute-start.20 = (bf16[4,4,64,128]{3,2,1,0:T(8,128)(2,1)}, bf16[4,4,64,128]{3,2,1,0:T(8,128)(2,1)}, u32[]{:S(2)}, u32[]{:S(2)}) collective-permute-start(bf16[4,4,64,128]{3,2,1,0:T(8,128)(2,1)} %copy-done.34), channel_id=1, source_target_pairs={{0,129},{1,192},{64,193},{65,0},{128,1},{129,64},{192,65},{193,128... | collective-permute-start | bytes 786440 | tf_op jit(solution)/shard_map/ppermute | solution.py:239
  107.4 15.7 %all-to-all-done.1 = bf16[32,16,16,128]{3,2,1,0:T(8,128)(2,1)} async-done(((bf16[32,16,16,128]{3,2,1,0:T(8,128)(2,1)}), bf16[32,16,16,128]{3,2,1,0:T(8,128)(2,1)}, u32[]{:S(2)}, u32[]{:S(2)}) %all-to-all-start.1) | async-done | bytes 2097184 | tf_op jit(solution)/shard_map/all_to_all | solution.py:240
  123.1 2.9 %shard_map.80 = (bf16[4,4,2,64,128]{4,3,2,1,0:T(8,128)(2,1)S(1)}, bf16[4,4,2,64,128]{4,3,2,1,0:T(8,128)(2,1)S(1)}, bf16[4,4,2,64,128]{4,3,2,1,0:T(8,128)(2,1)S(1)}, bf16[4,4,2,64,128]{4,3,2,1,0:T(8,128)(2,1)S(1)}) custom-call(s32[3]{0:T(128)S(1)} %pad_add_fusion.pos, bf16[512,512]{1,0:T(8,128)(2,1)S(1)} %copy-done.29, bf16[8,4,4,4,16,128]{5,4,3,2,1,0:T(8,128)(2,1)} %bitcast.6.m), custom_call_target="tpu_custom_call" | custom-call | flops 1073741824 | bytes 4194304 | tf_op jit(solution)/shard_map/pallas_call | solution.py:242
  126.1 1.9 collective-permute-start.13
  128.0 1.8 collective-permute-start.14
  129.9 4.4 %collective-permute-done.18.p3 = bf16[4,4,64,128]{3,2,1,0:T(8,128)(2,1)} collective-permute-done((bf16[4,4,64,128]{3,2,1,0:T(8,128)(2,1)}, bf16[4,4,64,128]{3,2,1,0:T(8,128)(2,1)}, u32[]{:S(2)}, u32[]{:S(2)}) %collective-permute-start.18) | collective-permute-done | bytes 262176 | tf_op jit(solution)/shard_map/ppermute | solution.py:239
  134.2 0.8 collective-permute-start.15
  135.1 8.0 %collective-permute-done.19.p4 = bf16[4,4,64,128]{3,2,1,0:T(8,128)(2,1)} collective-permute-done((bf16[4,4,64,128]{3,2,1,0:T(8,128)(2,1)}, bf16[4,4,64,128]{3,2,1,0:T(8,128)(2,1)}, u32[]{:S(2)}, u32[]{:S(2)}) %collective-permute-start.19) | collective-permute-done | bytes 262176 | tf_op jit(solution)/shard_map/ppermute | solution.py:239
  143.0 6.9 %collective-permute-start.21 = (bf16[4,4,64,128]{3,2,1,0:T(8,128)(2,1)S(1)}, bf16[4,4,64,128]{3,2,1,0:T(8,128)(2,1)S(1)}, u32[]{:S(2)}, u32[]{:S(2)}) collective-permute-start(bf16[4,4,64,128]{3,2,1,0:T(8,128)(2,1)S(1)} %copy-done.33), channel_id=1, source_target_pairs={{0,192},{1,193},{64,0},{65,1},{128,64},{129,65},{192,128},{193,129... | collective-permute-start | bytes 786440 | tf_op jit(solution)/shard_map/ppermute | solution.py:239
  149.9 9.3 %collective-permute-done.21.p6 = bf16[4,4,64,128]{3,2,1,0:T(8,128)(2,1)S(1)} collective-permute-done((bf16[4,4,64,128]{3,2,1,0:T(8,128)(2,1)S(1)}, bf16[4,4,64,128]{3,2,1,0:T(8,128)(2,1)S(1)}, u32[]{:S(2)}, u32[]{:S(2)}) %collective-permute-start.21) | collective-permute-done | bytes 262176 | tf_op jit(solution)/shard_map/ppermute | solution.py:239
  159.2 4.5 %collective-permute-done.22.p7 = bf16[4,4,64,128]{3,2,1,0:T(8,128)(2,1)S(1)} collective-permute-done((bf16[4,4,64,128]{3,2,1,0:T(8,128)(2,1)S(1)}, bf16[4,4,64,128]{3,2,1,0:T(8,128)(2,1)S(1)}, u32[]{:S(2)}, u32[]{:S(2)}) %collective-permute-start.22) | collective-permute-done | bytes 262176 | tf_op jit(solution)/shard_map/ppermute | solution.py:239
  163.7 5.2 %shard_map.82 = (bf16[8,4,2,8,16,128]{5,4,3,2,1,0:T(8,128)(2,1)S(1)}, bf16[512,2048]{1,0:T(8,128)(2,1)}) custom-call(s32[3]{0:T(128)S(1)} %pad_add_fusion.pos, bf16[512,512]{1,0:T(8,128)(2,1)S(1)} %copy-done.27, bf16[4,4,64,128]{3,2,1,0:T(8,128)(2,1)S(1)} %get-tuple-element.99.p0, bf16[4,4,64,128]{3,2,1,0:T(8,128)(2,1)} %collective-permute-done.16.p1, ...), custom_call_target="tpu_custom_call" | custom-call | flops 1073741824 | bytes 4194304 | tf_op jit(solution)/shard_map/pallas_call | solution.py:247
  168.8 1.4 copy-done.4
  170.2 1.6 shard_map.81
  174.7 7.0 %all-to-all-start.2 = ((bf16[32,16,16,128]{3,2,1,0:T(8,128)(2,1)}), bf16[32,16,16,128]{3,2,1,0:T(8,128)(2,1)}, u32[]{:S(2)}, u32[]{:S(2)}) async-start(bf16[32,16,16,128]{3,2,1,0:T(8,128)(2,1)} %bitcast.15), calls=%async_computation.2 | async-start | bytes 4194304 | tf_op jit(solution)/shard_map/all_to_all | solution.py:256
  181.8 6.8 %collective-permute-start.24 = (bf16[4,4,64,128]{3,2,1,0:T(8,128)(2,1)}, bf16[4,4,64,128]{3,2,1,0:T(8,128)(2,1)S(1)}, u32[]{:S(2)}, u32[]{:S(2)}) collective-permute-start(bf16[4,4,64,128]{3,2,1,0:T(8,128)(2,1)} %get-tuple-element.112), channel_id=1, source_target_pairs={{0,128},{1,129},{64,192},{65,193},{128,0},{129,1},{192,64},{193,65... | collective-permute-start | bytes 786440 | tf_op jit(solution)/shard_map/ppermute | solution.py:255
  188.7 1.6 copy-done.5
  190.3 6.8 %shard_map.83.first = f32[4,2,4,16,512]{4,3,2,1,0:T(8,128)S(1)} custom-call(s32[3]{0:T(128)S(1)} %pad_add_fusion.pos, bf16[8,4,4,4,16,128]{5,4,3,2,1,0:T(8,128)(2,1)} %bitcast.6.m, bf16[512,2048]{1,0:T(8,128)(2,1)S(1)} %copy-done.5), custom_call_target="tpu_custom_call" | custom-call | flops 1073741824 | bytes 4194304 | tf_op jit(solution)/shard_map/pallas_call | solution.py:257
  197.1 8.6 %collective-permute-done.23.refs_3_ = bf16[4,4,64,128]{3,2,1,0:T(8,128)(2,1)S(1)} collective-permute-done((bf16[4,4,64,128]{3,2,1,0:T(8,128)(2,1)}, bf16[4,4,64,128]{3,2,1,0:T(8,128)(2,1)S(1)}, u32[]{:S(2)}, u32[]{:S(2)}) %collective-permute-start.23) | collective-permute-done | bytes 262176 | tf_op jit(solution)/shard_map/ppermute | solution.py:255
  206.4 9.3 %collective-permute-done.24.refs_4_ = bf16[4,4,64,128]{3,2,1,0:T(8,128)(2,1)S(1)} collective-permute-done((bf16[4,4,64,128]{3,2,1,0:T(8,128)(2,1)}, bf16[4,4,64,128]{3,2,1,0:T(8,128)(2,1)S(1)}, u32[]{:S(2)}, u32[]{:S(2)}) %collective-permute-start.24) | collective-permute-done | bytes 262176 | tf_op jit(solution)/shard_map/ppermute | solution.py:255
  216.4 1.3 collective-permute-done.25.refs_5_
  218.4 4.7 %shard_map.84 = f32[4,2,4,2,16,512]{5,4,3,2,1,0:T(8,128)S(1)} custom-call(s32[3]{0:T(128)S(1)} %pad_add_fusion.pos, bf16[4,8,2,8,16,128]{5,4,3,2,1,0:T(8,128)(2,1)S(1)} %bitcast.11, bf16[8,4,2,8,16,128]{5,4,3,2,1,0:T(8,128)(2,1)} %bitcast.8.mixed, f32[4,2,4,16,512]{4,3,2,1,0:T(8,128)S(1)} %shard_map.83.first), custom_call_target="tpu_custom_call" | custom-call | flops 1073741824 | bytes 4194304 | tf_op jit(solution)/shard_map/pallas_call | solution.py:259
  223.1 1.3 copy-done.2
  224.4 7.4 %all-to-all-start.3 = ((f32[32,2,16,512]{3,2,1,0:T(8,128)}), f32[32,2,16,512]{3,2,1,0:T(8,128)S(1)}, u32[]{:S(2)}, u32[]{:S(2)}) async-start(f32[32,2,16,512]{3,2,1,0:T(8,128)} %bitcast.14), calls=%async_computation.3 | async-start | bytes 4194304 | tf_op jit(solution)/shard_map/all_to_all | solution.py:262
  231.9 1.9 collective-permute-start.27
  233.8 1.1 collective-permute-start.28
  234.9 3.1 %collective-permute-start.29 = (bf16[4,4,64,128]{3,2,1,0:T(8,128)(2,1)}, bf16[4,4,64,128]{3,2,1,0:T(8,128)(2,1)S(1)}, u32[]{:S(2)}, u32[]{:S(2)}) collective-permute-start(bf16[4,4,64,128]{3,2,1,0:T(8,128)(2,1)} %copy-done.35), channel_id=1, source_target_pairs={{0,193},{1,0},{64,1},{65,64},{128,65},{129,128},{192,129},{193,192... | collective-permute-start | bytes 786440 | tf_op jit(solution)/shard_map/ppermute | solution.py:255
  238.1 5.9 %collective-permute-done.26.refs_1_ = bf16[4,4,64,128]{3,2,1,0:T(8,128)(2,1)S(1)} collective-permute-done((bf16[4,4,64,128]{3,2,1,0:T(8,128)(2,1)}, bf16[4,4,64,128]{3,2,1,0:T(8,128)(2,1)S(1)}, u32[]{:S(2)}, u32[]{:S(2)}) %collective-permute-start.26) | collective-permute-done | bytes 262176 | tf_op jit(solution)/shard_map/ppermute | solution.py:255
  244.0 7.2 %collective-permute-done.27.refs_2_ = bf16[4,4,64,128]{3,2,1,0:T(8,128)(2,1)S(1)} collective-permute-done((bf16[4,4,64,128]{3,2,1,0:T(8,128)(2,1)}, bf16[4,4,64,128]{3,2,1,0:T(8,128)(2,1)S(1)}, u32[]{:S(2)}, u32[]{:S(2)}) %collective-permute-start.27) | collective-permute-done | bytes 262176 | tf_op jit(solution)/shard_map/ppermute | solution.py:255
  253.6 4.0 %all-to-all-done.3.parts = f32[32,2,16,512]{3,2,1,0:T(8,128)S(1)} async-done(((f32[32,2,16,512]{3,2,1,0:T(8,128)}), f32[32,2,16,512]{3,2,1,0:T(8,128)S(1)}, u32[]{:S(2)}, u32[]{:S(2)}) %all-to-all-start.3) | async-done | bytes 2097184 | tf_op jit(solution)/shard_map/all_to_all | solution.py:262
  257.6 1.3 shard_map.86
  259.0 4.2 %collective-permute-start.30 = (f32[2,16,512]{2,1,0:T(8,128)S(1)}, f32[2,16,512]{2,1,0:T(8,128)S(1)}, u32[]{:S(2)}, u32[]{:S(2)}) collective-permute-start(f32[2,16,512]{2,1,0:T(8,128)S(1)} %shard_map.86), channel_id=1, source_target_pairs={{0,0},{2,64},{4,128},{6,192},{64,2},{66,66},{68,130},{70,194},{128... | collective-permute-start | bytes 196616 | tf_op jit(solution)/shard_map/ppermute | solution.py:265
  263.3 2.5 shard_map.85
  265.7 6.3 %collective-permute-done.30 = f32[2,16,512]{2,1,0:T(8,128)S(1)} collective-permute-done((f32[2,16,512]{2,1,0:T(8,128)S(1)}, f32[2,16,512]{2,1,0:T(8,128)S(1)}, u32[]{:S(2)}, u32[]{:S(2)}) %collective-permute-start.30) | collective-permute-done | bytes 65568 | tf_op jit(solution)/shard_map/ppermute | solution.py:265
  (112 shorter events, 17.8 us)
Async XLA Ops:
  0.6 1.6 copy-start.3
  7.5 1.3 copy-start
  8.8 11.5 %copy-start.43 = (bf16[1,512,512]{2,1,0:T(8,128)(2,1)S(1)}, bf16[1,512,512]{2,1,0:T(8,128)(2,1)}, u32[]{:S(2)}) copy-start(bf16[1,512,512]{2,1,0:T(8,128)(2,1)} %param.8) | copy-start | bytes 1572868
  8.8 11.5 %copy-start.44 = (bf16[1,512,512]{2,1,0:T(8,128)(2,1)S(1)}, bf16[1,512,512]{2,1,0:T(8,128)(2,1)}, u32[]{:S(2)}) copy-start(bf16[1,512,512]{2,1,0:T(8,128)(2,1)} %param.9) | copy-start | bytes 1572868
  8.8 75.7 %all-to-all-start = ((bf16[64,8,16,128]{3,2,1,0:T(8,128)(2,1)}), bf16[64,8,16,128]{3,2,1,0:T(8,128)(2,1)S(1)}, u32[]{:S(2)}, u32[]{:S(2)}) async-start(bf16[64,8,16,128]{3,2,1,0:T(8,128)(2,1)} %bitcast.12), calls=%async_computation | async-start | bytes 4194304 | tf_op jit(solution)/shard_map/all_to_all | solution.py:208
  20.3 9.7 %collective-permute-start.4 = (bf16[2,64,512]{2,1,0:T(8,128)(2,1)S(1)}, bf16[2,64,512]{2,1,0:T(8,128)(2,1)S(1)}, u32[]{:S(2)}, u32[]{:S(2)}) collective-permute-start(bf16[2,64,512]{2,1,0:T(8,128)(2,1)S(1)} %fusion), channel_id=1, source_target_pairs={{0,4},{66,70},{132,128},{198,194},{1,5},{67,71},{133,129},{199,195... | collective-permute-start | bytes 393224 | tf_op jit(solution)/shard_map/ppermute | solution.py:215
  21.6 8.4 %collective-permute-start.3 = (bf16[2,64,512]{2,1,0:T(8,128)(2,1)S(1)}, bf16[2,64,512]{2,1,0:T(8,128)(2,1)S(1)}, u32[]{:S(2)}, u32[]{:S(2)}) collective-permute-start(bf16[2,64,512]{2,1,0:T(8,128)(2,1)S(1)} %fusion), channel_id=1, source_target_pairs={{0,6},{66,64},{132,130},{198,196},{1,7},{67,65},{133,131},{199,197... | collective-permute-start | bytes 393224 | tf_op jit(solution)/shard_map/ppermute | solution.py:215
  22.3 7.8 %collective-permute-start.5 = (bf16[2,64,512]{2,1,0:T(8,128)(2,1)S(1)}, bf16[2,64,512]{2,1,0:T(8,128)(2,1)}, u32[]{:S(2)}, u32[]{:S(2)}) collective-permute-start(bf16[2,64,512]{2,1,0:T(8,128)(2,1)S(1)} %fusion), channel_id=1, source_target_pairs={{0,2},{66,68},{132,134},{198,192},{1,3},{67,69},{133,135},{199,193... | collective-permute-start | bytes 393224 | tf_op jit(solution)/shard_map/ppermute | solution.py:215
  30.1 10.3 %collective-permute-start.12 = (bf16[2,64,512]{2,1,0:T(8,128)(2,1)S(1)}, bf16[2,64,512]{2,1,0:T(8,128)(2,1)S(1)}, u32[]{:S(2)}, u32[]{:S(2)}) collective-permute-start(bf16[2,64,512]{2,1,0:T(8,128)(2,1)S(1)} %select_select_fusion.refs_0_), channel_id=1, source_target_pairs={{0,56},{8,0},{16,8},{24,16},{32,24},{40,32},{48,40},{56,48},{1,57}... | collective-permute-start | bytes 393224 | tf_op jit(solution)/shard_map/ppermute | solution.py:217
  33.7 44.0 %collective-permute-start.2 = (bf16[4,64,1024]{2,1,0:T(8,128)(2,1)}, bf16[4,64,1024]{2,1,0:T(8,128)(2,1)S(1)}, u32[]{:S(2)}, u32[]{:S(2)}) collective-permute-start(bf16[4,64,1024]{2,1,0:T(8,128)(2,1)} %get-tuple-element.133), channel_id=1, source_target_pairs={{0,6},{2,0},{4,2},{6,4},{1,7},{3,1},{5,3},{7,5},{8,14},{10,8},{12,... | collective-permute-start | bytes 1572872 | tf_op jit(solution)/shard_map/ppermute | solution.py:228
  37.3 40.4 %collective-permute-start = (bf16[4,64,1024]{2,1,0:T(8,128)(2,1)}, bf16[4,64,1024]{2,1,0:T(8,128)(2,1)}, u32[]{:S(2)}, u32[]{:S(2)}) collective-permute-start(bf16[4,64,1024]{2,1,0:T(8,128)(2,1)} %get-tuple-element.134), channel_id=1, source_target_pairs={{0,2},{2,4},{4,6},{6,0},{1,3},{3,5},{5,7},{7,1},{8,10},{10,12},{12... | collective-permute-start | bytes 1572872 | tf_op jit(solution)/shard_map/ppermute | solution.py:228
  37.3 40.4 %collective-permute-start.1 = (bf16[4,64,1024]{2,1,0:T(8,128)(2,1)}, bf16[4,64,1024]{2,1,0:T(8,128)(2,1)}, u32[]{:S(2)}, u32[]{:S(2)}) collective-permute-start(bf16[4,64,1024]{2,1,0:T(8,128)(2,1)} %get-tuple-element.136), channel_id=1, source_target_pairs={{0,4},{2,6},{4,0},{6,2},{1,5},{3,7},{5,1},{7,3},{8,12},{10,14},{12... | collective-permute-start | bytes 1572872 | tf_op jit(solution)/shard_map/ppermute | solution.py:228
  39.4 10.5 %collective-permute-start.11 = (bf16[2,64,512]{2,1,0:T(8,128)(2,1)S(1)}, bf16[2,64,512]{2,1,0:T(8,128)(2,1)S(1)}, u32[]{:S(2)}, u32[]{:S(2)}) collective-permute-start(bf16[2,64,512]{2,1,0:T(8,128)(2,1)S(1)} %select_select_fusion.refs_0_), channel_id=1, source_target_pairs={{0,48},{8,56},{16,0},{24,8},{32,16},{40,24},{48,32},{56,40},{1,49}... | collective-permute-start | bytes 393224 | tf_op jit(solution)/shard_map/ppermute | solution.py:217
  40.5 9.4 %collective-permute-start.10 = (bf16[2,64,512]{2,1,0:T(8,128)(2,1)S(1)}, bf16[2,64,512]{2,1,0:T(8,128)(2,1)S(1)}, u32[]{:S(2)}, u32[]{:S(2)}) collective-permute-start(bf16[2,64,512]{2,1,0:T(8,128)(2,1)S(1)} %select_select_fusion.refs_0_), channel_id=1, source_target_pairs={{0,40},{8,48},{16,56},{24,0},{32,8},{40,16},{48,24},{56,32},{1,41}... | collective-permute-start | bytes 393224 | tf_op jit(solution)/shard_map/ppermute | solution.py:217
  49.8 12.5 %collective-permute-start.9 = (bf16[2,64,512]{2,1,0:T(8,128)(2,1)S(1)}, bf16[2,64,512]{2,1,0:T(8,128)(2,1)S(1)}, u32[]{:S(2)}, u32[]{:S(2)}) collective-permute-start(bf16[2,64,512]{2,1,0:T(8,128)(2,1)S(1)} %select_select_fusion.refs_0_), channel_id=1, source_target_pairs={{0,32},{8,40},{16,48},{24,56},{32,0},{40,8},{48,16},{56,24},{1,33}... | collective-permute-start | bytes 393224 | tf_op jit(solution)/shard_map/ppermute | solution.py:217
  50.5 12.5 %collective-permute-start.8 = (bf16[2,64,512]{2,1,0:T(8,128)(2,1)S(1)}, bf16[2,64,512]{2,1,0:T(8,128)(2,1)S(1)}, u32[]{:S(2)}, u32[]{:S(2)}) collective-permute-start(bf16[2,64,512]{2,1,0:T(8,128)(2,1)S(1)} %select_select_fusion.refs_0_), channel_id=1, source_target_pairs={{0,24},{8,32},{16,40},{24,48},{32,56},{40,0},{48,8},{56,16},{1,25}... | collective-permute-start | bytes 393224 | tf_op jit(solution)/shard_map/ppermute | solution.py:217
  63.0 8.1 %collective-permute-start.7 = (bf16[2,64,512]{2,1,0:T(8,128)(2,1)S(1)}, bf16[2,64,512]{2,1,0:T(8,128)(2,1)}, u32[]{:S(2)}, u32[]{:S(2)}) collective-permute-start(bf16[2,64,512]{2,1,0:T(8,128)(2,1)S(1)} %select_select_fusion.refs_0_), channel_id=1, source_target_pairs={{0,16},{8,24},{16,32},{24,40},{32,48},{40,56},{48,0},{56,8},{1,17}... | collective-permute-start | bytes 393224 | tf_op jit(solution)/shard_map/ppermute | solution.py:217
  63.7 7.5 %collective-permute-start.6 = (bf16[2,64,512]{2,1,0:T(8,128)(2,1)S(1)}, bf16[2,64,512]{2,1,0:T(8,128)(2,1)}, u32[]{:S(2)}, u32[]{:S(2)}) collective-permute-start(bf16[2,64,512]{2,1,0:T(8,128)(2,1)S(1)} %select_select_fusion.refs_0_), channel_id=1, source_target_pairs={{0,8},{8,16},{16,24},{24,32},{32,40},{40,48},{48,56},{56,0},{1,9},... | collective-permute-start | bytes 393224 | tf_op jit(solution)/shard_map/ppermute | solution.py:217
  71.2 0.9 copy-start.21
  72.1 0.9 copy-start.23
  73.0 0.9 copy-start.25
  75.3 0.8 copy-start.6
  76.1 0.8 copy-start.26
  76.9 0.8 copy-start.28
  79.5 0.7 copy-start.30
  80.2 0.7 copy-start.32
  84.5 1.0 copy-start.7
  89.1 1.3 copy-start.1
  90.4 32.7 %copy-start.29 = (bf16[512,512]{1,0:T(8,128)(2,1)S(1)}, bf16[512,512]{1,0:T(8,128)(2,1)}, u32[]{:S(2)}) copy-start(bf16[512,512]{1,0:T(8,128)(2,1)} %copy-done.28) | copy-start | bytes 1572868
  90.4 32.7 %all-to-all-start.1 = ((bf16[32,16,16,128]{3,2,1,0:T(8,128)(2,1)}), bf16[32,16,16,128]{3,2,1,0:T(8,128)(2,1)}, u32[]{:S(2)}, u32[]{:S(2)}) async-start(bf16[32,16,16,128]{3,2,1,0:T(8,128)(2,1)} %bitcast.13), calls=%async_computation.1 | async-start | bytes 4194304 | tf_op jit(solution)/shard_map/all_to_all | solution.py:240
  97.2 66.4 %copy-start.27 = (bf16[512,512]{1,0:T(8,128)(2,1)S(1)}, bf16[512,512]{1,0:T(8,128)(2,1)}, u32[]{:S(2)}) copy-start(bf16[512,512]{1,0:T(8,128)(2,1)} %copy-done.26) | copy-start | bytes 1572868
  97.2 28.8 %collective-permute-start.16 = (bf16[4,4,64,128]{3,2,1,0:T(8,128)(2,1)}, bf16[4,4,64,128]{3,2,1,0:T(8,128)(2,1)}, u32[]{:S(2)}, u32[]{:S(2)}) collective-permute-start(bf16[4,4,64,128]{3,2,1,0:T(8,128)(2,1)} %copy-done.42), channel_id=1, source_target_pairs={{0,1},{1,64},{64,65},{65,128},{128,129},{129,192},{192,193},{193,0... | collective-permute-start | bytes 786440 | tf_op jit(solution)/shard_map/ppermute | solution.py:239
  97.3 30.7 %collective-permute-start.17 = (bf16[4,4,64,128]{3,2,1,0:T(8,128)(2,1)}, bf16[4,4,64,128]{3,2,1,0:T(8,128)(2,1)}, u32[]{:S(2)}, u32[]{:S(2)}) collective-permute-start(bf16[4,4,64,128]{3,2,1,0:T(8,128)(2,1)} %copy-done.41), channel_id=1, source_target_pairs={{0,64},{1,65},{64,128},{65,129},{128,192},{129,193},{192,0},{193,1... | collective-permute-start | bytes 786440 | tf_op jit(solution)/shard_map/ppermute | solution.py:239
  101.5 32.7 %collective-permute-start.18 = (bf16[4,4,64,128]{3,2,1,0:T(8,128)(2,1)}, bf16[4,4,64,128]{3,2,1,0:T(8,128)(2,1)}, u32[]{:S(2)}, u32[]{:S(2)}) collective-permute-start(bf16[4,4,64,128]{3,2,1,0:T(8,128)(2,1)} %copy-done.40), channel_id=1, source_target_pairs={{0,65},{1,128},{64,129},{65,192},{128,193},{129,0},{192,1},{193,64... | collective-permute-start | bytes 786440 | tf_op jit(solution)/shard_map/ppermute | solution.py:239
  102.4 40.6 %collective-permute-start.19 = (bf16[4,4,64,128]{3,2,1,0:T(8,128)(2,1)}, bf16[4,4,64,128]{3,2,1,0:T(8,128)(2,1)}, u32[]{:S(2)}, u32[]{:S(2)}) collective-permute-start(bf16[4,4,64,128]{3,2,1,0:T(8,128)(2,1)} %copy-done.36), channel_id=1, source_target_pairs={{0,128},{1,129},{64,192},{65,193},{128,0},{129,1},{192,64},{193,65... | collective-permute-start | bytes 786440 | tf_op jit(solution)/shard_map/ppermute | solution.py:239
  104.4 45.6 %collective-permute-start.20 = (bf16[4,4,64,128]{3,2,1,0:T(8,128)(2,1)}, bf16[4,4,64,128]{3,2,1,0:T(8,128)(2,1)}, u32[]{:S(2)}, u32[]{:S(2)}) collective-permute-start(bf16[4,4,64,128]{3,2,1,0:T(8,128)(2,1)} %copy-done.34), channel_id=1, source_target_pairs={{0,129},{1,192},{64,193},{65,0},{128,1},{129,64},{192,65},{193,128... | collective-permute-start | bytes 786440 | tf_op jit(solution)/shard_map/ppermute | solution.py:239
  123.1 19.9 %copy-start.33 = (bf16[4,4,64,128]{3,2,1,0:T(8,128)(2,1)S(1)}, bf16[4,4,64,128]{3,2,1,0:T(8,128)(2,1)}, u32[]{:S(2)}) copy-start(bf16[4,4,64,128]{3,2,1,0:T(8,128)(2,1)} %copy-done.32) | copy-start | bytes 786436
  123.1 26.8 %copy-start.31 = (bf16[4,4,64,128]{3,2,1,0:T(8,128)(2,1)S(1)}, bf16[4,4,64,128]{3,2,1,0:T(8,128)(2,1)}, u32[]{:S(2)}) copy-start(bf16[4,4,64,128]{3,2,1,0:T(8,128)(2,1)} %copy-done.30) | copy-start | bytes 786436
  126.1 44.1 %collective-permute-start.13 = (bf16[4,4,2,64,128]{4,3,2,1,0:T(8,128)(2,1)S(1)}, bf16[4,4,2,64,128]{4,3,2,1,0:T(8,128)(2,1)S(1)}, u32[]{:S(2)}, u32[]{:S(2)}) collective-permute-start(bf16[4,4,2,64,128]{4,3,2,1,0:T(8,128)(2,1)S(1)} %get-tuple-element.87), channel_id=1, source_target_pairs={{0,2},{2,4},{4,6},{6,0},{1,3},{3,5},{5,7},{7,1},{8,10},{10,12},{12... | collective-permute-start | bytes 1572872 | tf_op jit(solution)/shard_map/ppermute | solution.py:244
  128.0 42.2 %collective-permute-start.14 = (bf16[4,4,2,64,128]{4,3,2,1,0:T(8,128)(2,1)S(1)}, bf16[4,4,2,64,128]{4,3,2,1,0:T(8,128)(2,1)S(1)}, u32[]{:S(2)}, u32[]{:S(2)}) collective-permute-start(bf16[4,4,2,64,128]{4,3,2,1,0:T(8,128)(2,1)S(1)} %get-tuple-element.88), channel_id=1, source_target_pairs={{0,4},{2,6},{4,0},{6,2},{1,5},{3,7},{5,1},{7,3},{8,12},{10,14},{12... | collective-permute-start | bytes 1572872 | tf_op jit(solution)/shard_map/ppermute | solution.py:244
  134.2 36.0 %collective-permute-start.15 = (bf16[4,4,2,64,128]{4,3,2,1,0:T(8,128)(2,1)S(1)}, bf16[4,4,2,64,128]{4,3,2,1,0:T(8,128)(2,1)S(1)}, u32[]{:S(2)}, u32[]{:S(2)}) collective-permute-start(bf16[4,4,2,64,128]{4,3,2,1,0:T(8,128)(2,1)S(1)} %get-tuple-element.89), channel_id=1, source_target_pairs={{0,6},{2,0},{4,2},{6,4},{1,7},{3,1},{5,3},{7,5},{8,14},{10,8},{12,... | collective-permute-start | bytes 1572872 | tf_op jit(solution)/shard_map/ppermute | solution.py:244
  143.0 16.1 %collective-permute-start.21 = (bf16[4,4,64,128]{3,2,1,0:T(8,128)(2,1)S(1)}, bf16[4,4,64,128]{3,2,1,0:T(8,128)(2,1)S(1)}, u32[]{:S(2)}, u32[]{:S(2)}) collective-permute-start(bf16[4,4,64,128]{3,2,1,0:T(8,128)(2,1)S(1)} %copy-done.33), channel_id=1, source_target_pairs={{0,192},{1,193},{64,0},{65,1},{128,64},{129,65},{192,128},{193,129... | collective-permute-start | bytes 786440 | tf_op jit(solution)/shard_map/ppermute | solution.py:239
  149.9 13.7 %collective-permute-start.22 = (bf16[4,4,64,128]{3,2,1,0:T(8,128)(2,1)S(1)}, bf16[4,4,64,128]{3,2,1,0:T(8,128)(2,1)S(1)}, u32[]{:S(2)}, u32[]{:S(2)}) collective-permute-start(bf16[4,4,64,128]{3,2,1,0:T(8,128)(2,1)S(1)} %copy-done.31), channel_id=1, source_target_pairs={{0,193},{1,0},{64,1},{65,64},{128,65},{129,128},{192,129},{193,192... | collective-permute-start | bytes 786440 | tf_op jit(solution)/shard_map/ppermute | solution.py:239
  168.8 1.4 copy-start.4
  173.2 0.7 copy-start.38
  174.7 43.7 %all-to-all-start.2 = ((bf16[32,16,16,128]{3,2,1,0:T(8,128)(2,1)}), bf16[32,16,16,128]{3,2,1,0:T(8,128)(2,1)}, u32[]{:S(2)}, u32[]{:S(2)}) async-start(bf16[32,16,16,128]{3,2,1,0:T(8,128)(2,1)} %bitcast.15), calls=%async_computation.2 | async-start | bytes 4194304 | tf_op jit(solution)/shard_map/all_to_all | solution.py:256
  181.7 24.0 %collective-permute-start.23 = (bf16[4,4,64,128]{3,2,1,0:T(8,128)(2,1)}, bf16[4,4,64,128]{3,2,1,0:T(8,128)(2,1)S(1)}, u32[]{:S(2)}, u32[]{:S(2)}) collective-permute-start(bf16[4,4,64,128]{3,2,1,0:T(8,128)(2,1)} %get-tuple-element.111), channel_id=1, source_target_pairs={{0,65},{1,128},{64,129},{65,192},{128,193},{129,0},{192,1},{193,64... | collective-permute-start | bytes 786440 | tf_op jit(solution)/shard_map/ppermute | solution.py:255
  181.8 33.8 %collective-permute-start.24 = (bf16[4,4,64,128]{3,2,1,0:T(8,128)(2,1)}, bf16[4,4,64,128]{3,2,1,0:T(8,128)(2,1)S(1)}, u32[]{:S(2)}, u32[]{:S(2)}) collective-permute-start(bf16[4,4,64,128]{3,2,1,0:T(8,128)(2,1)} %get-tuple-element.112), channel_id=1, source_target_pairs={{0,128},{1,129},{64,192},{65,193},{128,0},{129,1},{192,64},{193,65... | collective-permute-start | bytes 786440 | tf_op jit(solution)/shard_map/ppermute | solution.py:255
  188.7 29.0 %collective-permute-start.25 = (bf16[4,4,64,128]{3,2,1,0:T(8,128)(2,1)}, bf16[4,4,64,128]{3,2,1,0:T(8,128)(2,1)S(1)}, u32[]{:S(2)}, u32[]{:S(2)}) collective-permute-start(bf16[4,4,64,128]{3,2,1,0:T(8,128)(2,1)} %get-tuple-element.113), channel_id=1, source_target_pairs={{0,129},{1,192},{64,193},{65,0},{128,1},{129,64},{192,65},{193,128... | collective-permute-start | bytes 786440 | tf_op jit(solution)/shard_map/ppermute | solution.py:255
  188.7 1.6 copy-start.5
  217.7 0.7 copy-start.12
  223.1 1.3 copy-start.2
  224.4 33.2 %all-to-all-start.3 = ((f32[32,2,16,512]{3,2,1,0:T(8,128)}), f32[32,2,16,512]{3,2,1,0:T(8,128)S(1)}, u32[]{:S(2)}, u32[]{:S(2)}) async-start(f32[32,2,16,512]{3,2,1,0:T(8,128)} %bitcast.14), calls=%async_computation.3 | async-start | bytes 4194304 | tf_op jit(solution)/shard_map/all_to_all | solution.py:262
  231.8 31.4 %copy-start.9 = (bf16[4,4,64,128]{3,2,1,0:T(8,128)(2,1)S(1)}, bf16[4,4,64,128]{3,2,1,0:T(8,128)(2,1)}, u32[]{:S(2)}) copy-start(bf16[4,4,64,128]{3,2,1,0:T(8,128)(2,1)} %copy-done.8) | copy-start | bytes 786436
  231.8 31.4 %copy-start.11 = (bf16[4,4,64,128]{3,2,1,0:T(8,128)(2,1)S(1)}, bf16[4,4,64,128]{3,2,1,0:T(8,128)(2,1)}, u32[]{:S(2)}) copy-start(bf16[4,4,64,128]{3,2,1,0:T(8,128)(2,1)} %copy-done.10) | copy-start | bytes 786436
  231.8 31.4 %copy-start.13 = (bf16[4,4,64,128]{3,2,1,0:T(8,128)(2,1)S(1)}, bf16[4,4,64,128]{3,2,1,0:T(8,128)(2,1)}, u32[]{:S(2)}) copy-start(bf16[4,4,64,128]{3,2,1,0:T(8,128)(2,1)} %copy-done.12) | copy-start | bytes 786436
  231.8 12.2 %collective-permute-start.26 = (bf16[4,4,64,128]{3,2,1,0:T(8,128)(2,1)}, bf16[4,4,64,128]{3,2,1,0:T(8,128)(2,1)S(1)}, u32[]{:S(2)}, u32[]{:S(2)}) collective-permute-start(bf16[4,4,64,128]{3,2,1,0:T(8,128)(2,1)} %copy-done.39), channel_id=1, source_target_pairs={{0,1},{1,64},{64,65},{65,128},{128,129},{129,192},{192,193},{193,0... | collective-permute-start | bytes 786440 | tf_op jit(solution)/shard_map/ppermute | solution.py:255
  231.9 19.3 %collective-permute-start.27 = (bf16[4,4,64,128]{3,2,1,0:T(8,128)(2,1)}, bf16[4,4,64,128]{3,2,1,0:T(8,128)(2,1)S(1)}, u32[]{:S(2)}, u32[]{:S(2)}) collective-permute-start(bf16[4,4,64,128]{3,2,1,0:T(8,128)(2,1)} %copy-done.38), channel_id=1, source_target_pairs={{0,64},{1,65},{64,128},{65,129},{128,192},{129,193},{192,0},{193,1... | collective-permute-start | bytes 786440 | tf_op jit(solution)/shard_map/ppermute | solution.py:255
  233.8 18.2 %collective-permute-start.28 = (bf16[4,4,64,128]{3,2,1,0:T(8,128)(2,1)}, bf16[4,4,64,128]{3,2,1,0:T(8,128)(2,1)S(1)}, u32[]{:S(2)}, u32[]{:S(2)}) collective-permute-start(bf16[4,4,64,128]{3,2,1,0:T(8,128)(2,1)} %copy-done.37), channel_id=1, source_target_pairs={{0,192},{1,193},{64,0},{65,1},{128,64},{129,65},{192,128},{193,129... | collective-permute-start | bytes 786440 | tf_op jit(solution)/shard_map/ppermute | solution.py:255
  234.9 18.0 %collective-permute-start.29 = (bf16[4,4,64,128]{3,2,1,0:T(8,128)(2,1)}, bf16[4,4,64,128]{3,2,1,0:T(8,128)(2,1)S(1)}, u32[]{:S(2)}, u32[]{:S(2)}) collective-permute-start(bf16[4,4,64,128]{3,2,1,0:T(8,128)(2,1)} %copy-done.35), channel_id=1, source_target_pairs={{0,193},{1,0},{64,1},{65,64},{128,65},{129,128},{192,129},{193,192... | collective-permute-start | bytes 786440 | tf_op jit(solution)/shard_map/ppermute | solution.py:255
  257.6 5.6 %copy-start.15 = (bf16[4,4,64,128]{3,2,1,0:T(8,128)(2,1)S(1)}, bf16[4,4,64,128]{3,2,1,0:T(8,128)(2,1)}, u32[]{:S(2)}) copy-start(bf16[4,4,64,128]{3,2,1,0:T(8,128)(2,1)} %copy-done.14) | copy-start | bytes 786436
  257.6 5.6 %copy-start.17 = (bf16[4,4,64,128]{3,2,1,0:T(8,128)(2,1)S(1)}, bf16[4,4,64,128]{3,2,1,0:T(8,128)(2,1)}, u32[]{:S(2)}) copy-start(bf16[4,4,64,128]{3,2,1,0:T(8,128)(2,1)} %copy-done.16) | copy-start | bytes 786436
  257.6 5.6 %copy-start.19 = (bf16[4,4,64,128]{3,2,1,0:T(8,128)(2,1)S(1)}, bf16[4,4,64,128]{3,2,1,0:T(8,128)(2,1)}, u32[]{:S(2)}) copy-start(bf16[4,4,64,128]{3,2,1,0:T(8,128)(2,1)} %copy-done.18) | copy-start | bytes 786436
  259.0 13.1 %collective-permute-start.30 = (f32[2,16,512]{2,1,0:T(8,128)S(1)}, f32[2,16,512]{2,1,0:T(8,128)S(1)}, u32[]{:S(2)}, u32[]{:S(2)}) collective-permute-start(f32[2,16,512]{2,1,0:T(8,128)S(1)} %shard_map.86), channel_id=1, source_target_pairs={{0,0},{2,64},{4,128},{6,192},{64,2},{66,66},{68,130},{70,194},{128... | collective-permute-start | bytes 196616 | tf_op jit(solution)/shard_map/ppermute | solution.py:265
  (16 other events, 11.1 us)

commit v2 on v1

v2 whole, which is shorter than its diff:
```python
import functools

import jax
import jax.numpy as jnp
from jax import lax
from jax.experimental import pallas as pl
from jax.experimental.pallas import tpu as pltpu
from jax.sharding import Mesh, PartitionSpec as P

ROWS = 512
COLS = 512
SLAB = 128
BF = jnp.bfloat16
F32 = jnp.float32
ZYC = ("zh", "y", "core", "zl")
ZX = ("zh", "x", "zl")
PLANE = ("y", "core", "x")
PARAMS = pltpu.CompilerParams(vmem_limit_bytes=48 * 1024 * 1024)
VM = pl.BlockSpec(memory_space=pltpu.VMEM)
SM = pl.BlockSpec(memory_space=pltpu.SMEM)


def call(kernel, outs, scratch=(), n_in=1, flops=0, moved=4 << 20):
    return pl.pallas_call(
        kernel,
        out_shape=outs,
        in_specs=[SM] + [VM] * n_in,
        out_specs=jax.tree.map(lambda _: VM, outs),
        scratch_shapes=list(scratch),
        compiler_params=PARAMS,
        cost_estimate=pl.CostEstimate(flops=flops, bytes_accessed=moved, transcendentals=0),
    )


def shape(*dims, dtype=BF):
    return jax.ShapeDtypeStruct(dims, dtype)


def gate_kernel(gate, up, out):
    for k in range(8):
        lanes = slice(k * SLAB, (k + 1) * SLAB)
        prod = gate[:, :, lanes].astype(F32) * up[:, :, lanes].astype(F32)
        out[k // 2, :, k % 2] = jnp.swapaxes(prod, 0, 1).astype(BF).reshape(2, 8, 16, SLAB)


def gate_call(gate, up):
    return pl.pallas_call(
        gate_kernel,
        grid=(4,),
        out_shape=shape(4, 8, 2, 8, 16, SLAB),
        in_specs=[pl.BlockSpec((16, 16, 1024), lambda c: (0, c, 0))] * 2,
        out_specs=pl.BlockSpec((4, 2, 2, 8, 16, SLAB), lambda c: (0, c, 0, 0, 0, 0)),
        compiler_params=PARAMS,
        cost_estimate=pl.CostEstimate(flops=1 << 20, bytes_accessed=6 << 20, transcendentals=0),
    )(gate, up)


def factor_kernel(pos, *refs):
    f1, f2t, f1tp, full = refs[4:]
    for k in range(4):
        rows = pl.ds(pl.multiple_of((pos[2] ^ k) * 128, 128), 128)
        full[:, rows, :] = refs[k][...].astype(F32)
    f1[...] = full[0].astype(BF)
    f2t[...] = full[1].T.astype(BF)
    ordered = jnp.concatenate(
        [
            full[0, x * 128 + zl * 64 + c * 8 : x * 128 + zl * 64 + c * 8 + 8, :]
            for x in range(4)
            for c in range(8)
            for zl in range(2)
        ],
        axis=0,
    )
    f1tp[...] = ordered.T.astype(BF)


def second_apply_kernel(pos, f2t, g, *refs):
    outs, flat, swap = refs[:8], refs[8], refs[9]
    for k in range(16):
        flat[:, k * SLAB : (k + 1) * SLAB] = g[:, :, k // 8, k % 8].reshape(ROWS, SLAB)

    def body(zh, _):
        rows = pl.ds(pl.multiple_of(zh * 128, 128), 128)
        for k in range(0, 16, 2):
            part = jnp.dot(f2t[rows, :], flat[:, k * SLAB : (k + 2) * SLAB], preferred_element_type=F32)
            swap[pl.ds(k, 128, stride=16), :] = part[:, :SLAB]
            swap[pl.ds(k + 1, 128, stride=16), :] = part[:, SLAB:]
        for t, out in enumerate(outs):
            at = pl.multiple_of(lax.rem(pos[3] + t, 8) * 256, 256)
            tile = swap[pl.ds(at, 256), :].astype(BF).reshape(4, 4, 16, SLAB)
            for x in range(4):
                out[x, zh] = tile[x]
        return 0

    lax.fori_loop(0, 4, body, 0)


def second_cut_kernel(pos, *refs):
    for s, out in enumerate(refs[8:]):
        owner = lax.rem(pos[0] + s, 4)
        for t in range(8):
            out[lax.rem(pos[3] + 8 - t, 8)] = refs[t][owner]


def first_apply_kernel(pos, f1t, m0, m1, m2, m3, out, mgw):
    for k in range(16):
        for s, block in enumerate((m0, m1, m2, m3)):
            rows = pl.ds(pl.multiple_of(lax.rem(pos[0] + 4 - s, 4) * 128, 128), 128)
            mgw[rows, k * SLAB : (k + 1) * SLAB] = block[:, k // 4, k % 4].reshape(128, SLAB)
    for k in range(0, 16, 2):
        part = jnp.dot(f1t[...], mgw[:, k * SLAB : (k + 2) * SLAB], preferred_element_type=F32).astype(BF)
        out[k // 4, :, :, k % 4] = part[:, :SLAB].reshape(4, 2, 64, SLAB)
        out[k // 4, :, :, k % 4 + 1] = part[:, SLAB:].reshape(4, 2, 64, SLAB)


def token_cut_kernel(tok, out, sem):
    copies = [
        pltpu.make_async_copy(
            tok.at[pl.ds(4 * x, 4), :, pl.ds(SLAB * k, SLAB)], out.at[k // 2, x, k % 2], sem.at[k, x]
        )
        for k in range(8)
        for x in range(4)
    ]
    for copy in copies:
        copy.start()
    for copy in copies:
        copy.wait()


def grad_join_kernel(part, out):
    for k in range(8):
        out[:, :, k * SLAB : (k + 1) * SLAB] = part[k // 2, 0, k % 2]


def grad_join(parts):
    return pl.pallas_call(
        grad_join_kernel,
        grid=(4,),
        out_shape=shape(16, 64, 1024),
        in_specs=[pl.BlockSpec((4, 1, 2, 4, 64, SLAB), lambda x: (0, x, 0, 0, 0, 0))],
        out_specs=pl.BlockSpec((4, 64, 1024), lambda x: (x, 0, 0)),
        compiler_params=PARAMS,
        cost_estimate=pl.CostEstimate(flops=0, bytes_accessed=4 << 20, transcendentals=0),
    )(parts)


def move(kernel, out, operand):
    return pl.pallas_call(
        kernel,
        out_shape=out,
        in_specs=[pl.BlockSpec(memory_space=pl.ANY)],
        out_specs=pl.BlockSpec(memory_space=pl.ANY),
        scratch_shapes=[pltpu.SemaphoreType.DMA((8, 4))],
        compiler_params=PARAMS,
        cost_estimate=pl.CostEstimate(flops=0, bytes_accessed=4 << 20, transcendentals=0),
    )(operand)


def mix_kernel(pos, f1, tok, mixed, tokw, swap):
    for k in range(16):
        tokw[:, k * SLAB : (k + 1) * SLAB] = tok[k // 4, :, :, k % 4].reshape(COLS, SLAB)

    def body(b, _):
        rows = pl.ds(pl.multiple_of(b * 128, 128), 128)
        for k in range(0, 16, 2):
            part = jnp.dot(f1[rows, :], tokw[:, k * SLAB : (k + 2) * SLAB], preferred_element_type=F32)
            swap[pl.ds(k, 128, stride=16), :] = part[:, :SLAB]
            swap[pl.ds(k + 1, 128, stride=16), :] = part[:, SLAB:]
        for zl in range(2):
            tile = swap[zl * 1024 : (zl + 1) * 1024, :].astype(BF).reshape(8, 8, 16, SLAB)
            for yc in range(8):
                mixed[yc, b, zl] = tile[yc]
        return 0

    lax.fori_loop(0, 4, body, 0)


def first_kernel(pos, mgw, tok, keep, give, tokw):
    for k in range(16):
        tokw[:, k * SLAB : (k + 1) * SLAB] = tok[k // 4, :, :, k % 4].reshape(COLS, SLAB)
    for x in range(4):
        left = mgw[x * 128 : (x + 1) * 128, :]
        part = lax.dot_general(left, tokw[...], (((1,), (1,)), ((), ())), preferred_element_type=F32)

        def put(cores):
            for yc in range(8):
                for zl in range(2):
                    at, half = yc * 16 + zl * 8, (yc % 2) * 8
                    cores[(yc // 2) % 2][zl * 2 + yc // 4, x, half : half + 8, :] = part[at : at + 8, :]

        @pl.when(pos[5] == 0)
        def _():
            put((keep, give))

        @pl.when(pos[5] == 1)
        def _():
            put((give, keep))


def second_kernel(pos, g, mixed, keep, give, flat, mixw):
    core = pos[5]
    for k in range(16):
        lanes = slice(k * SLAB, (k + 1) * SLAB)
        flat[:, lanes] = g[:, :, k // 8, k % 8].reshape(ROWS, SLAB)
        mixw[:, lanes] = mixed[:, :, k // 8, k % 8].reshape(ROWS, SLAB)
    for zh in range(4):
        part = lax.dot_general(
            flat[zh * 128 : (zh + 1) * 128, :], mixw[...], (((1,), (1,)), ((), ())), preferred_element_type=F32
        )

        def put(keep, give):
            for y in range(4):
                keep[y, zh] = part[y * 32 : y * 32 + 16, :]
                give[y, zh] = part[y * 32 + 16 : y * 32 + 32, :]

        @pl.when(core == 0)
        def _():
            put(keep, give)

        @pl.when(core == 1)
        def _():
            put(give, keep)


def core_sum_kernel(pos, f, fo, s, so, *outs):
    for t, out in enumerate(outs):
        y = lax.rem(pos[4] + t, 4)
        out[:, 0] = f[y] + fo[y]
        out[:, 1] = s[y] + so[y]


def y_sum_kernel(pos, a, b, c, d, *outs):
    for s, out in enumerate(outs):
        x = lax.rem(pos[0] + s, 4)
        out[...] = (a[x] + b[x]) + (c[x] + d[x])


def sum_kernel(pos, a, b, c, d, out):
    place = lax.broadcasted_iota(jnp.int32, (ROWS, ROWS), 0)
    row = lax.broadcasted_iota(jnp.int32, (ROWS, ROWS), 1)
    want = ((row >> 4) & 7) * 64 + ((row >> 2) & 3) * 16 + (row >> 7) * 4 + (row & 3)
    order = (place == want).astype(F32)
    out[0] = ((a[0] + b[0]) + (c[0] + d[0])) * (ROWS**-0.5 * SLAB**-0.5)
    total = (a[1] + b[1]) + (c[1] + d[1])
    second = jnp.dot(total, order, precision=lax.Precision.HIGHEST, preferred_element_type=F32)
    out[1] = second * (COLS**-0.5 * SLAB**-0.5)


def shifts(count):
    return lambda s: [(k, (k + s) % count) for k in range(count)]


def local(tokens, gate, upstream, first_factor, second_factor):
    zh, zl = lax.axis_index("zh"), lax.axis_index("zl")
    x, y, core = lax.axis_index("x"), lax.axis_index("y"), lax.axis_index("core")
    z, yc, part = zh * 2 + zl, y * 2 + core, (y % 2) * 2 + core
    pos = jnp.stack([x, z, part, yc, y, core]).astype(jnp.int32)
    four, eight = shifts(4), shifts(8)
    wide = pltpu.VMEM((ROWS, 16 * SLAB), BF)
    swap = pltpu.VMEM((128 * 16, SLAB), F32)
    f32 = functools.partial(shape, dtype=F32)

    gated = gate_call(gate, upstream)
    grad = lax.all_to_all(gated.reshape(64, 8, 16, SLAB), ZYC, 0, 0, tiled=True).reshape(4, 8, 2, 8, 16, SLAB)
    sent = move(token_cut_kernel, shape(4, 4, 2, 4, 64, SLAB), tokens)

    both = jnp.concatenate([first_factor, second_factor], 0)
    quarter = lax.dynamic_slice_in_dim(both, part * 128, 128, 1)
    got = quarter
    for s in range(1, 4):
        came = lax.ppermute(quarter, ("zh", "x"), [(k * 4 + k, k * 4 + (k + s) % 4) for k in range(4)])
        got = jnp.where(x == (zh + s) % 4, came, got)
    quarters = [got] + [lax.ppermute(got, ("y", "core"), [(k, k ^ s) for k in range(8)]) for s in range(1, 4)]
    f1, f2t, f1tp = call(
        factor_kernel,
        [shape(COLS, COLS), shape(ROWS, ROWS), shape(COLS, COLS)],
        [pltpu.VMEM((2, COLS, COLS), F32)],
        n_in=4,
    )(pos, *quarters)
    sent, grad, f1, f2t, f1tp = lax.optimization_barrier((sent, grad, f1, f2t, f1tp))

    tok = lax.all_to_all(sent.reshape(32, 4, 64, SLAB), ZX, 0, 0, tiled=True).reshape(4, 4, 2, 4, 64, SLAB)
    mg = call(second_apply_kernel, [shape(4, 4, 4, 16, SLAB)] * 8, [wide, swap], n_in=2, flops=1 << 30)(pos, f2t, grad)
    mg = [mg[0]] + [lax.ppermute(mg[t], ("y", "core"), eight(t)) for t in range(1, 8)]
    mg = call(second_cut_kernel, [shape(8, 4, 4, 16, SLAB)] * 4, n_in=8)(pos, *mg)
    mg = [mg[0]] + [lax.ppermute(mg[s], "x", four(s)) for s in range(1, 4)]
    tok, mg = lax.optimization_barrier((tok, mg))

    mixed = call(mix_kernel, shape(8, 4, 2, 8, 16, SLAB), [wide, swap], n_in=2, flops=1 << 30)(pos, f1, tok)
    mixed = lax.all_to_all(mixed.reshape(32, 16, 16, SLAB), PLANE, 0, 0, tiled=True).reshape(8, 4, 2, 8, 16, SLAB)
    sent, mgw = call(
        first_apply_kernel, [shape(4, 4, 2, 4, 64, SLAB), shape(COLS, 16 * SLAB)], n_in=5, flops=1 << 30
    )(pos, f1tp, *mg)
    mixed, sent = lax.optimization_barrier((mixed, sent))

    home = lax.all_to_all(sent.reshape(32, 4, 64, SLAB), ZX, 0, 0, tiled=True)
    halves = [f32(4, 4, 16, 512)] * 2
    second_keep, second_give = call(second_kernel, halves, [wide, wide], n_in=2, flops=1 << 30)(pos, grad, mixed)
    first_keep, first_give = call(first_kernel, halves, [wide], n_in=2, flops=1 << 30)(pos, mgw, tok)
    other = [(0, 1), (1, 0)]
    first_came, second_came = lax.ppermute(first_give, "core", other), lax.ppermute(second_give, "core", other)
    sums = call(core_sum_kernel, [f32(4, 2, 16, 512)] * 4, n_in=4)(
        pos, first_keep, first_came, second_keep, second_came
    )
    sums = [sums[0]] + [lax.ppermute(sums[t], "y", four(t)) for t in range(1, 4)]
    sums = call(y_sum_kernel, [f32(2, 16, 512)] * 4, n_in=4, moved=1 << 20)(pos, *sums)
    sums = [sums[0]] + [lax.ppermute(sums[s], "x", four(s)) for s in range(1, 4)]
    sums = call(sum_kernel, f32(2, 16, 512), n_in=4, moved=1 << 19)(pos, *sums)
    sums = lax.ppermute(sums, ("zh", "x"), [(a * 4 + b, b * 4 + a) for a in range(4) for b in range(4)])
    home, sums = lax.optimization_barrier((home, sums))
    token_grad = grad_join(home.reshape(4, 4, 2, 4, 64, SLAB))
    return token_grad, sums[:1], sums[1:]


def solution(mesh):
    fine = Mesh(mesh.devices.reshape(4, 4, 2, 4, 2), ("zh", "y", "core", "x", "zl"))
    outer, inner = ("zh", "y", "core"), ("x", "zl")
    grid = P(outer, inner, None)
    factor = P(inner, None, None)
    return jax.shard_map(
        local,
        mesh=fine,
        in_specs=(grid, grid, grid, factor, factor),
        out_specs=(grid, P(inner, outer, None), P(inner, outer, None)),
        check_vma=False,
    )
```

time: 274 us -> 253 us (0.923)
  starting transfers between devices: 88.1 us -> 65.3 us
  waiting for transfers between devices: 114 us -> 129 us
  local copies, waits for them, and re-layouts: 32 us -> 21.2 us
  Pallas kernels: 37.1 us -> 33 us
    ppermute x30 -> x24, starting transfers between devices: 51.3 us -> 22.9 us  [the longest x7 6.14 us: local(): lax.ppermute(mg[t], ('y', 'core'), eight(t))]
    ppermute x30 -> x24, waiting for transfers between devices: 88.3 us -> 96.6 us  [the longest x3 27 us: local(): mg = [mg[0]] + [lax.ppermute(mg[s], 'x', four(s)) for s in range(1, 4)]]
    unnamed x90 -> x46, local copies, waits for them, and re-layouts: 28.7 us -> 20.5 us
    all_to_all x4, starting transfers between devices: 32.6 us -> 38.6 us  [the longest x1 11.4 us: local(): lax.all_to_all(gated.reshape(64, 8, 16, SLAB), ZYC, 0, 0, tiled=True)]
    all_to_all x4, waiting for transfers between devices: 19.7 us -> 24 us  [the longest x1 18.4 us: local(): lax.all_to_all(mixed.reshape(32, 16, 16, SLAB), PLANE, 0, 0, tiled=True)]
    pallas_call x10 -> x12, Pallas kernels: 35.6 us -> 32 us  [the longest x1 5.41 us: local(): call(second_kernel, halves, [wide, wide], n_in=2, flops=1 << 30)]
  transfers between devices with their start and end apart: 35 -> 29, of which waited for: 17 -> 19; matrix products, arithmetic and copies ran while one was open for 1% -> 0% of each run, Pallas kernels for 8% -> 8%
where the time goes in v2:
time: 253 us; the launch traced here: 251 us
  waiting for transfers between devices  129 us (51%)
  starting transfers between devices  65.3 us (26%)
  Pallas kernels  33 us (13%)
  local copies, waits for them, and re-layouts  21.2 us (8%)
    ppermute x3, waiting for transfers between devices, local(): mg = [mg[0]] + [lax.ppermute(mg[s], 'x', four(s)) for s in range(1, 4)]  27 us
    unnamed x46, local copies, waits for them, and re-layouts  20.5 us
    ppermute x7, waiting for transfers between devices, local(): lax.ppermute(mg[t], ('y', 'core'), eight(t))  18.7 us
    all_to_all x1, waiting for transfers between devices, local(): lax.all_to_all(mixed.reshape(32, 16, 16, SLAB), PLANE, 0, 0, tiled=True)  18.4 us
    ppermute x3, waiting for transfers between devices, local(): lax.ppermute(got, ('y', 'core'), [(k, k ^ s) for k in range(8)])  16.7 us
    ppermute x3, waiting for transfers between devices, local(): lax.ppermute(sums[t], 'y', four(t))  12 us
    ppermute x3, waiting for transfers between devices, local(): lax.ppermute(quarter, ('zh', 'x'), [(k * 4 + k, k * 4 + (k + s) % 4) for...  11.9 us
    all_to_all x1, starting transfers between devices, local(): lax.all_to_all(gated.reshape(64, 8, 16, SLAB), ZYC, 0, 0, tiled=True)  11.4 us
  transfers between devices with their start and end apart: 29, of which 19 were waited for; matrix products, arithmetic and copies ran while one was open for 0% of the time, Pallas kernels for 8%

profile of v2, /device:TPU:70, one launch (start us, length us, event | category | flops | bytes accessed | tf_op | source)
XLA Modules:
  0.0 250.9 jit_solution(14627367628920260126)
XLA Ops:
  0.6 1.6 copy-done.5
  2.2 4.4 %shard_map.77 = bf16[4,8,2,8,16,128]{5,4,3,2,1,0:T(8,128)(2,1)} custom-call(bf16[16,64,1024]{2,1,0:T(8,128)(2,1)S(1)} %copy-done.5, bf16[16,64,1024]{2,1,0:T(8,128)(2,1)} %up.1), custom_call_target="tpu_custom_call" | custom-call | flops 1048576 | bytes 6291456 | tf_op jit(solution)/shard_map/pallas_call | solution.py:47
  6.6 11.4 %all-to-all-start = ((bf16[64,8,16,128]{3,2,1,0:T(8,128)(2,1)}), bf16[64,8,16,128]{3,2,1,0:T(8,128)(2,1)S(1)}, u32[]{:S(2)}, u32[]{:S(2)}) async-start(bf16[64,8,16,128]{3,2,1,0:T(8,128)(2,1)} %bitcast.6), calls=%async_computation | async-start | bytes 4194304 | tf_op jit(solution)/shard_map/all_to_all | solution.py:264
  18.2 1.4 collective-permute-start
  19.5 1.3 collective-permute-start.1
  20.8 1.4 collective-permute-start.2
  22.2 11.9 %collective-permute-done.1 = bf16[2,128,512]{2,1,0:T(8,128)(2,1)} collective-permute-done((bf16[2,128,512]{2,1,0:T(8,128)(2,1)S(1)}, bf16[2,128,512]{2,1,0:T(8,128)(2,1)}, u32[]{:S(2)}, u32[]{:S(2)}) %collective-permute-start.1) | collective-permute-done | bytes 262176 | tf_op jit(solution)/shard_map/ppermute | solution.py:271
  34.1 1.1 select_select_fusion.refs_0_
  35.2 1.6 collective-permute-start.4
  37.1 1.6 copy-done.6
  38.7 0.9 shard_map.76
  39.6 1.3 copy-done.4
  41.0 6.1 %collective-permute-done.4.refs_2_ = bf16[2,128,512]{2,1,0:T(8,128)(2,1)S(1)} collective-permute-done((bf16[2,128,512]{2,1,0:T(8,128)(2,1)S(1)}, bf16[2,128,512]{2,1,0:T(8,128)(2,1)S(1)}, u32[]{:S(2)}, u32[]{:S(2)}) %collective-permute-start.4) | collective-permute-done | bytes 262176 | tf_op jit(solution)/shard_map/ppermute | solution.py:273
  47.2 10.5 %collective-permute-done.5.refs_3_ = bf16[2,128,512]{2,1,0:T(8,128)(2,1)S(1)} collective-permute-done((bf16[2,128,512]{2,1,0:T(8,128)(2,1)S(1)}, bf16[2,128,512]{2,1,0:T(8,128)(2,1)S(1)}, u32[]{:S(2)}, u32[]{:S(2)}) %collective-permute-start.5) | collective-permute-done | bytes 262176 | tf_op jit(solution)/shard_map/ppermute | solution.py:273
  57.7 0.7 copy-done.9
  58.5 0.9 copy-done.10
  59.4 1.0 shard_map.78
  60.4 0.8 copy-done.11
  61.2 0.8 copy-done.19
  62.0 5.5 %all-to-all-done = bf16[64,8,16,128]{3,2,1,0:T(8,128)(2,1)S(1)} async-done(((bf16[64,8,16,128]{3,2,1,0:T(8,128)(2,1)}), bf16[64,8,16,128]{3,2,1,0:T(8,128)(2,1)S(1)}, u32[]{:S(2)}, u32[]{:S(2)}) %all-to-all-start) | async-done | bytes 2097184 | tf_op jit(solution)/shard_map/all_to_all | solution.py:264
  67.5 1.3 copy-done.1
  68.9 9.0 %all-to-all-start.1 = ((bf16[32,4,64,128]{3,2,1,0:T(8,128)(2,1)}), bf16[32,4,64,128]{3,2,1,0:T(8,128)(2,1)S(1)}, u32[]{:S(2)}, u32[]{:S(2)}) async-start(bf16[32,4,64,128]{3,2,1,0:T(8,128)(2,1)} %bitcast.19), calls=%async_computation.1 | async-start | bytes 4194304 | tf_op jit(solution)/shard_map/all_to_all | solution.py:282
  77.9 1.6 copy-done.2
  79.5 3.6 %shard_map.79 = (bf16[4,4,4,16,128]{4,3,2,1,0:T(8,128)(2,1)S(1)}, bf16[4,4,4,16,128]{4,3,2,1,0:T(8,128)(2,1)S(1)}, bf16[4,4,4,16,128]{4,3,2,1,0:T(8,128)(2,1)S(1...) custom-call(s32[6]{0:T(128)S(1)} %stack.27.pos, ...), custom_call_target="tpu_custom_call" | custom-call | flops 1073741824 | bytes 4194304 | tf_op jit(solution)/shard_map/pallas_call | solution.py:283
  83.3 1.7 collective-permute-start.11
  86.2 5.7 %collective-permute-done.10.refs_5_ = bf16[4,4,4,16,128]{4,3,2,1,0:T(8,128)(2,1)S(1)} collective-permute-done((bf16[4,4,4,16,128]{4,3,2,1,0:T(8,128)(2,1)S(1)}, bf16[4,4,4,16,128]{4,3,2,1,0:T(8,128)(2,1)S(1)}, u32[]{:S(2)}, u32[]{:S(2)}) %collective-permute-start.10) | collective-permute-done | bytes 262176 | tf_op jit(solution)/shard_map/ppermute | solution.py:284
  91.9 0.9 collective-permute-start.8
  92.7 4.2 %collective-permute-done.11.refs_6_ = bf16[4,4,4,16,128]{4,3,2,1,0:T(8,128)(2,1)S(1)} collective-permute-done((bf16[4,4,4,16,128]{4,3,2,1,0:T(8,128)(2,1)S(1)}, bf16[4,4,4,16,128]{4,3,2,1,0:T(8,128)(2,1)S(1)}, u32[]{:S(2)}, u32[]{:S(2)}) %collective-permute-start.11) | collective-permute-done | bytes 262176 | tf_op jit(solution)/shard_map/ppermute | solution.py:284
  96.9 2.3 collective-permute-start.9
  99.2 1.2 collective-permute-done.12.refs_7_
  100.4 4.8 %collective-permute-done.8.refs_3_ = bf16[4,4,4,16,128]{4,3,2,1,0:T(8,128)(2,1)S(1)} collective-permute-done((bf16[4,4,4,16,128]{4,3,2,1,0:T(8,128)(2,1)S(1)}, bf16[4,4,4,16,128]{4,3,2,1,0:T(8,128)(2,1)S(1)}, u32[]{:S(2)}, u32[]{:S(2)}) %collective-permute-start.8) | collective-permute-done | bytes 262176 | tf_op jit(solution)/shard_map/ppermute | solution.py:284
  105.2 2.8 %collective-permute-done.9.refs_4_ = bf16[4,4,4,16,128]{4,3,2,1,0:T(8,128)(2,1)S(1)} collective-permute-done((bf16[4,4,4,16,128]{4,3,2,1,0:T(8,128)(2,1)S(1)}, bf16[4,4,4,16,128]{4,3,2,1,0:T(8,128)(2,1)S(1)}, u32[]{:S(2)}, u32[]{:S(2)}) %collective-permute-start.9) | collective-permute-done | bytes 262176 | tf_op jit(solution)/shard_map/ppermute | solution.py:284
  108.0 0.7 shard_map.80
  109.3 2.4 collective-permute-start.14
  111.7 15.1 %collective-permute-done.13.m1 = bf16[8,4,4,16,128]{4,3,2,1,0:T(8,128)(2,1)S(1)} collective-permute-done((bf16[8,4,4,16,128]{4,3,2,1,0:T(8,128)(2,1)S(1)}, bf16[8,4,4,16,128]{4,3,2,1,0:T(8,128)(2,1)S(1)}, u32[]{:S(2)}, u32[]{:S(2)}) %collective-permute-start.13) | collective-permute-done | bytes 524320 | tf_op jit(solution)/shard_map/ppermute | solution.py:286
  126.8 0.8 copy-done.13
  127.6 2.8 %collective-permute-done.14.m2 = bf16[8,4,4,16,128]{4,3,2,1,0:T(8,128)(2,1)S(1)} collective-permute-done((bf16[8,4,4,16,128]{4,3,2,1,0:T(8,128)(2,1)S(1)}, bf16[8,4,4,16,128]{4,3,2,1,0:T(8,128)(2,1)S(1)}, u32[]{:S(2)}, u32[]{:S(2)}) %collective-permute-start.14) | collective-permute-done | bytes 524320 | tf_op jit(solution)/shard_map/ppermute | solution.py:286
  130.5 0.8 copy-done.15
  131.2 9.1 %collective-permute-done.15.m3 = bf16[8,4,4,16,128]{4,3,2,1,0:T(8,128)(2,1)S(1)} collective-permute-done((bf16[8,4,4,16,128]{4,3,2,1,0:T(8,128)(2,1)S(1)}, bf16[8,4,4,16,128]{4,3,2,1,0:T(8,128)(2,1)S(1)}, u32[]{:S(2)}, u32[]{:S(2)}) %collective-permute-start.15) | collective-permute-done | bytes 524320 | tf_op jit(solution)/shard_map/ppermute | solution.py:286
  140.3 0.8 copy-done.17
  141.1 3.6 %shard_map.81 = bf16[8,4,2,8,16,128]{5,4,3,2,1,0:T(8,128)(2,1)S(1)} custom-call(s32[6]{0:T(128)S(1)} %stack.27.pos, bf16[512,512]{1,0:T(8,128)(2,1)S(1)} %get-tuple-element.49.f1, bf16[4,4,2,4,64,128]{5,4,3,2,1,0:T(8,128)(2,1)S(1)} %bitcast.14), custom_call_target="tpu_custom_call" | custom-call | flops 1073741824 | bytes 4194304 | tf_op jit(solution)/shard_map/pallas_call | solution.py:289
  144.7 1.4 copy-done
  146.1 7.6 %all-to-all-start.2 = ((bf16[32,16,16,128]{3,2,1,0:T(8,128)(2,1)}), bf16[32,16,16,128]{3,2,1,0:T(8,128)(2,1)}, u32[]{:S(2)}, u32[]{:S(2)}) async-start(bf16[32,16,16,128]{3,2,1,0:T(8,128)(2,1)} %bitcast.16), calls=%async_computation.2 | async-start | bytes 4194304 | tf_op jit(solution)/shard_map/all_to_all | solution.py:290
  153.7 1.0 copy-done.14
  154.8 1.0 copy-done.16
  155.8 1.0 copy-done.18
  156.9 2.9 %shard_map.82 = (bf16[4,4,2,4,64,128]{5,4,3,2,1,0:T(8,128)(2,1)S(1)}, bf16[512,2048]{1,0:T(8,128)(2,1)}) custom-call(s32[6]{0:T(128)S(1)} %stack.27.pos, bf16[512,512]{1,0:T(8,128)(2,1)S(1)} %copy-done.12, bf16[8,4,4,16,128]{4,3,2,1,0:T(8,128)(2,1)S(1)} %get-tuple-element.67.m0, bf16[8,4,4,16,128]{4,3,2,1,0:T(8,128)(2,1)S(1)} %copy-done.14, ...), custom_call_target="tpu_custom_call" | custom-call | flops 1073741824 | bytes 4194304 | tf_op jit(solution)/shard_map/pallas_call | solution.py:291
  159.8 1.4 copy-done.7
  161.2 18.4 %all-to-all-done.2 = bf16[32,16,16,128]{3,2,1,0:T(8,128)(2,1)} async-done(((bf16[32,16,16,128]{3,2,1,0:T(8,128)(2,1)}), bf16[32,16,16,128]{3,2,1,0:T(8,128)(2,1)}, u32[]{:S(2)}, u32[]{:S(2)}) %all-to-all-start.2) | async-done | bytes 2097184 | tf_op jit(solution)/shard_map/all_to_all | solution.py:290
  179.6 10.5 %all-to-all-start.3 = ((bf16[32,4,64,128]{3,2,1,0:T(8,128)(2,1)}), bf16[32,4,64,128]{3,2,1,0:T(8,128)(2,1)}, u32[]{:S(2)}, u32[]{:S(2)}) async-start(bf16[32,4,64,128]{3,2,1,0:T(8,128)(2,1)} %bitcast.20), calls=%async_computation.3 | async-start | bytes 4194304 | tf_op jit(solution)/shard_map/all_to_all | solution.py:296
  190.2 1.6 copy-done.8
  191.7 3.9 %shard_map.83 = (f32[4,4,16,512]{3,2,1,0:T(8,128)S(1)}, f32[4,4,16,512]{3,2,1,0:T(8,128)S(1)}) custom-call(s32[6]{0:T(128)S(1)} %stack.27.pos, bf16[512,2048]{1,0:T(8,128)(2,1)S(1)} %copy-done.8, bf16[4,4,2,4,64,128]{5,4,3,2,1,0:T(8,128)(2,1)S(1)} %bitcast.15), custom_call_target="tpu_custom_call" | custom-call | flops 1073741824 | bytes 4194304 | tf_op jit(solution)/shard_map/pallas_call | solution.py:299
  195.8 5.4 %shard_map.84 = (f32[4,4,16,512]{3,2,1,0:T(8,128)S(1)}, f32[4,4,16,512]{3,2,1,0:T(8,128)S(1)}) custom-call(s32[6]{0:T(128)S(1)} %stack.27.pos, bf16[4,8,2,8,16,128]{5,4,3,2,1,0:T(8,128)(2,1)S(1)} %bitcast.18, bf16[8,4,2,8,16,128]{5,4,3,2,1,0:T(8,128)(2,1)} %bitcast.11.mixed), custom_call_target="tpu_custom_call" | custom-call | flops 1073741824 | bytes 4194304 | tf_op jit(solution)/shard_map/pallas_call | solution.py:298
  201.8 1.5 collective-permute-done.17.so
  204.7 1.7 collective-permute-start.19
  206.4 1.7 collective-permute-start.20
  208.1 11.4 %collective-permute-done.18.b = f32[4,2,16,512]{3,2,1,0:T(8,128)S(1)} collective-permute-done((f32[4,2,16,512]{3,2,1,0:T(8,128)S(1)}, f32[4,2,16,512]{3,2,1,0:T(8,128)S(1)}, u32[]{:S(2)}, u32[]{:S(2)}) %collective-permute-start.18) | collective-permute-done | bytes 262176 | tf_op jit(solution)/shard_map/ppermute | solution.py:305
  221.4 2.4 collective-permute-start.22
  223.8 1.5 collective-permute-done.21.b
  225.2 7.3 %collective-permute-done.22.c = f32[2,16,512]{2,1,0:T(8,128)S(1)} collective-permute-done((f32[2,16,512]{2,1,0:T(8,128)S(1)}, f32[2,16,512]{2,1,0:T(8,128)S(1)}, u32[]{:S(2)}, u32[]{:S(2)}) %collective-permute-start.22) | collective-permute-done | bytes 65568 | tf_op jit(solution)/shard_map/ppermute | solution.py:307
  232.6 1.2 shard_map.87
  233.8 3.7 %collective-permute-start.24 = (f32[2,16,512]{2,1,0:T(8,128)S(1)}, f32[2,16,512]{2,1,0:T(8,128)S(1)}, u32[]{:S(2)}, u32[]{:S(2)}) collective-permute-start(f32[2,16,512]{2,1,0:T(8,128)S(1)} %shard_map.87), channel_id=1, source_target_pairs={{0,0},{2,64},{4,128},{6,192},{64,2},{66,66},{68,130},{70,194},{128... | collective-permute-start | bytes 196616 | tf_op jit(solution)/shard_map/ppermute | solution.py:309
  237.5 8.8 %collective-permute-done.24 = f32[2,16,512]{2,1,0:T(8,128)S(1)} collective-permute-done((f32[2,16,512]{2,1,0:T(8,128)S(1)}, f32[2,16,512]{2,1,0:T(8,128)S(1)}, u32[]{:S(2)}, u32[]{:S(2)}) %collective-permute-start.24) | collective-permute-done | bytes 65568 | tf_op jit(solution)/shard_map/ppermute | solution.py:309
  246.3 4.0 %shard_map.88 = bf16[16,64,1024]{2,1,0:T(8,128)(2,1)} custom-call(bf16[4,4,2,4,64,128]{5,4,3,2,1,0:T(8,128)(2,1)} %bitcast.13.part), custom_call_target="tpu_custom_call" | custom-call | bytes 4194304 | tf_op jit(solution)/shard_map/pallas_call | solution.py:136
  (57 shorter events, 7.0 us)
Async XLA Ops:
  0.6 1.6 copy-start.5
  6.6 11.5 %copy-start.21 = (bf16[1,512,512]{2,1,0:T(8,128)(2,1)S(1)}, bf16[1,512,512]{2,1,0:T(8,128)(2,1)}, u32[]{:S(2)}) copy-start(bf16[1,512,512]{2,1,0:T(8,128)(2,1)} %param.8) | copy-start | bytes 1572868
  6.6 11.5 %copy-start.22 = (bf16[1,512,512]{2,1,0:T(8,128)(2,1)S(1)}, bf16[1,512,512]{2,1,0:T(8,128)(2,1)}, u32[]{:S(2)}) copy-start(bf16[1,512,512]{2,1,0:T(8,128)(2,1)} %param.9) | copy-start | bytes 1572868
  6.6 60.9 %all-to-all-start = ((bf16[64,8,16,128]{3,2,1,0:T(8,128)(2,1)}), bf16[64,8,16,128]{3,2,1,0:T(8,128)(2,1)S(1)}, u32[]{:S(2)}, u32[]{:S(2)}) async-start(bf16[64,8,16,128]{3,2,1,0:T(8,128)(2,1)} %bitcast.6), calls=%async_computation | async-start | bytes 4194304 | tf_op jit(solution)/shard_map/all_to_all | solution.py:264
  18.2 4.0 %collective-permute-start = (bf16[2,128,512]{2,1,0:T(8,128)(2,1)S(1)}, bf16[2,128,512]{2,1,0:T(8,128)(2,1)}, u32[]{:S(2)}, u32[]{:S(2)}) collective-permute-start(bf16[2,128,512]{2,1,0:T(8,128)(2,1)S(1)} %fusion), channel_id=1, source_target_pairs={{0,6},{66,64},{132,130},{198,196},{1,7},{67,65},{133,131},{199,197... | collective-permute-start | bytes 786440 | tf_op jit(solution)/shard_map/ppermute | solution.py:271
  19.5 14.5 %collective-permute-start.1 = (bf16[2,128,512]{2,1,0:T(8,128)(2,1)S(1)}, bf16[2,128,512]{2,1,0:T(8,128)(2,1)}, u32[]{:S(2)}, u32[]{:S(2)}) collective-permute-start(bf16[2,128,512]{2,1,0:T(8,128)(2,1)S(1)} %fusion), channel_id=1, source_target_pairs={{0,4},{66,70},{132,128},{198,194},{1,5},{67,71},{133,129},{199,195... | collective-permute-start | bytes 786440 | tf_op jit(solution)/shard_map/ppermute | solution.py:271
  20.8 13.2 %collective-permute-start.2 = (bf16[2,128,512]{2,1,0:T(8,128)(2,1)S(1)}, bf16[2,128,512]{2,1,0:T(8,128)(2,1)}, u32[]{:S(2)}, u32[]{:S(2)}) collective-permute-start(bf16[2,128,512]{2,1,0:T(8,128)(2,1)S(1)} %fusion), channel_id=1, source_target_pairs={{0,2},{66,68},{132,134},{198,192},{1,3},{67,69},{133,135},{199,193... | collective-permute-start | bytes 786440 | tf_op jit(solution)/shard_map/ppermute | solution.py:271
  35.1 5.9 %collective-permute-start.3 = (bf16[2,128,512]{2,1,0:T(8,128)(2,1)S(1)}, bf16[2,128,512]{2,1,0:T(8,128)(2,1)S(1)}, u32[]{:S(2)}, u32[]{:S(2)}) collective-permute-start(bf16[2,128,512]{2,1,0:T(8,128)(2,1)S(1)} %select_select_fusion.refs_0_), channel_id=1, source_target_pairs={{0,8},{8,0},{16,24},{24,16},{32,40},{40,32},{48,56},{56,48},{1,9},... | collective-permute-start | bytes 786440 | tf_op jit(solution)/shard_map/ppermute | solution.py:273
  35.2 11.9 %collective-permute-start.4 = (bf16[2,128,512]{2,1,0:T(8,128)(2,1)S(1)}, bf16[2,128,512]{2,1,0:T(8,128)(2,1)S(1)}, u32[]{:S(2)}, u32[]{:S(2)}) collective-permute-start(bf16[2,128,512]{2,1,0:T(8,128)(2,1)S(1)} %select_select_fusion.refs_0_), channel_id=1, source_target_pairs={{0,16},{8,24},{16,0},{24,8},{32,48},{40,56},{48,32},{56,40},{1,17}... | collective-permute-start | bytes 786440 | tf_op jit(solution)/shard_map/ppermute | solution.py:273
  36.8 20.9 %collective-permute-start.5 = (bf16[2,128,512]{2,1,0:T(8,128)(2,1)S(1)}, bf16[2,128,512]{2,1,0:T(8,128)(2,1)S(1)}, u32[]{:S(2)}, u32[]{:S(2)}) collective-permute-start(bf16[2,128,512]{2,1,0:T(8,128)(2,1)S(1)} %select_select_fusion.refs_0_), channel_id=1, source_target_pairs={{0,24},{8,16},{16,8},{24,0},{32,56},{40,48},{48,40},{56,32},{1,25}... | collective-permute-start | bytes 786440 | tf_op jit(solution)/shard_map/ppermute | solution.py:273
  37.1 1.6 copy-start.6
  39.6 1.3 copy-start.4
  57.7 0.7 copy-start.9
  58.4 0.9 copy-start.10
  60.4 0.8 copy-start.11
  61.2 0.8 copy-start.19
  67.5 1.3 copy-start.1
  68.9 9.0 %copy-start.20 = (bf16[512,512]{1,0:T(8,128)(2,1)S(1)}, bf16[512,512]{1,0:T(8,128)(2,1)}, u32[]{:S(2)}) copy-start(bf16[512,512]{1,0:T(8,128)(2,1)} %copy-done.19) | copy-start | bytes 1572868
  68.9 72.3 %all-to-all-start.1 = ((bf16[32,4,64,128]{3,2,1,0:T(8,128)(2,1)}), bf16[32,4,64,128]{3,2,1,0:T(8,128)(2,1)S(1)}, u32[]{:S(2)}, u32[]{:S(2)}) async-start(bf16[32,4,64,128]{3,2,1,0:T(8,128)(2,1)} %bitcast.19), calls=%async_computation.1 | async-start | bytes 4194304 | tf_op jit(solution)/shard_map/all_to_all | solution.py:282
  77.9 1.6 copy-start.2
  83.2 8.7 %collective-permute-start.10 = (bf16[4,4,4,16,128]{4,3,2,1,0:T(8,128)(2,1)S(1)}, bf16[4,4,4,16,128]{4,3,2,1,0:T(8,128)(2,1)S(1)}, u32[]{:S(2)}, u32[]{:S(2)}) collective-permute-start(bf16[4,4,4,16,128]{4,3,2,1,0:T(8,128)(2,1)S(1)} %get-tuple-element.58), channel_id=1, source_target_pairs={{0,40},{8,48},{16,56},{24,0},{32,8},{40,16},{48,24},{56,32},{1,41}... | collective-permute-start | bytes 786440 | tf_op jit(solution)/shard_map/ppermute | solution.py:284
  83.3 13.7 %collective-permute-start.11 = (bf16[4,4,4,16,128]{4,3,2,1,0:T(8,128)(2,1)S(1)}, bf16[4,4,4,16,128]{4,3,2,1,0:T(8,128)(2,1)S(1)}, u32[]{:S(2)}, u32[]{:S(2)}) collective-permute-start(bf16[4,4,4,16,128]{4,3,2,1,0:T(8,128)(2,1)S(1)} %get-tuple-element.59), channel_id=1, source_target_pairs={{0,48},{8,56},{16,0},{24,8},{32,16},{40,24},{48,32},{56,40},{1,49}... | collective-permute-start | bytes 786440 | tf_op jit(solution)/shard_map/ppermute | solution.py:284
  85.0 15.4 %collective-permute-start.12 = (bf16[4,4,4,16,128]{4,3,2,1,0:T(8,128)(2,1)S(1)}, bf16[4,4,4,16,128]{4,3,2,1,0:T(8,128)(2,1)S(1)}, u32[]{:S(2)}, u32[]{:S(2)}) collective-permute-start(bf16[4,4,4,16,128]{4,3,2,1,0:T(8,128)(2,1)S(1)} %get-tuple-element.60), channel_id=1, source_target_pairs={{0,56},{8,0},{16,8},{24,16},{32,24},{40,32},{48,40},{56,48},{1,57}... | collective-permute-start | bytes 786440 | tf_op jit(solution)/shard_map/ppermute | solution.py:284
  85.0 15.4 %collective-permute-start.6 = (bf16[4,4,4,16,128]{4,3,2,1,0:T(8,128)(2,1)S(1)}, bf16[4,4,4,16,128]{4,3,2,1,0:T(8,128)(2,1)S(1)}, u32[]{:S(2)}, u32[]{:S(2)}) collective-permute-start(bf16[4,4,4,16,128]{4,3,2,1,0:T(8,128)(2,1)S(1)} %get-tuple-element.54), channel_id=1, source_target_pairs={{0,8},{8,16},{16,24},{24,32},{32,40},{40,48},{48,56},{56,0},{1,9},... | collective-permute-start | bytes 786440 | tf_op jit(solution)/shard_map/ppermute | solution.py:284
  85.5 14.9 %collective-permute-start.7 = (bf16[4,4,4,16,128]{4,3,2,1,0:T(8,128)(2,1)S(1)}, bf16[4,4,4,16,128]{4,3,2,1,0:T(8,128)(2,1)S(1)}, u32[]{:S(2)}, u32[]{:S(2)}) collective-permute-start(bf16[4,4,4,16,128]{4,3,2,1,0:T(8,128)(2,1)S(1)} %get-tuple-element.55), channel_id=1, source_target_pairs={{0,16},{8,24},{16,32},{24,40},{32,48},{40,56},{48,0},{56,8},{1,17}... | collective-permute-start | bytes 786440 | tf_op jit(solution)/shard_map/ppermute | solution.py:284
  91.9 13.4 %collective-permute-start.8 = (bf16[4,4,4,16,128]{4,3,2,1,0:T(8,128)(2,1)S(1)}, bf16[4,4,4,16,128]{4,3,2,1,0:T(8,128)(2,1)S(1)}, u32[]{:S(2)}, u32[]{:S(2)}) collective-permute-start(bf16[4,4,4,16,128]{4,3,2,1,0:T(8,128)(2,1)S(1)} %get-tuple-element.56), channel_id=1, source_target_pairs={{0,24},{8,32},{16,40},{24,48},{32,56},{40,0},{48,8},{56,16},{1,25}... | collective-permute-start | bytes 786440 | tf_op jit(solution)/shard_map/ppermute | solution.py:284
  96.9 11.1 %collective-permute-start.9 = (bf16[4,4,4,16,128]{4,3,2,1,0:T(8,128)(2,1)S(1)}, bf16[4,4,4,16,128]{4,3,2,1,0:T(8,128)(2,1)S(1)}, u32[]{:S(2)}, u32[]{:S(2)}) collective-permute-start(bf16[4,4,4,16,128]{4,3,2,1,0:T(8,128)(2,1)S(1)} %get-tuple-element.57), channel_id=1, source_target_pairs={{0,32},{8,40},{16,48},{24,56},{32,0},{40,8},{48,16},{56,24},{1,33}... | collective-permute-start | bytes 786440 | tf_op jit(solution)/shard_map/ppermute | solution.py:284
  108.7 18.1 %collective-permute-start.13 = (bf16[8,4,4,16,128]{4,3,2,1,0:T(8,128)(2,1)S(1)}, bf16[8,4,4,16,128]{4,3,2,1,0:T(8,128)(2,1)S(1)}, u32[]{:S(2)}, u32[]{:S(2)}) collective-permute-start(bf16[8,4,4,16,128]{4,3,2,1,0:T(8,128)(2,1)S(1)} %get-tuple-element.62), channel_id=1, source_target_pairs={{0,2},{2,4},{4,6},{6,0},{1,3},{3,5},{5,7},{7,1},{8,10},{10,12},{12... | collective-permute-start | bytes 1572872 | tf_op jit(solution)/shard_map/ppermute | solution.py:286
  109.3 21.1 %collective-permute-start.14 = (bf16[8,4,4,16,128]{4,3,2,1,0:T(8,128)(2,1)S(1)}, bf16[8,4,4,16,128]{4,3,2,1,0:T(8,128)(2,1)S(1)}, u32[]{:S(2)}, u32[]{:S(2)}) collective-permute-start(bf16[8,4,4,16,128]{4,3,2,1,0:T(8,128)(2,1)S(1)} %get-tuple-element.63), channel_id=1, source_target_pairs={{0,4},{2,6},{4,0},{6,2},{1,5},{3,7},{5,1},{7,3},{8,12},{10,14},{12... | collective-permute-start | bytes 1572872 | tf_op jit(solution)/shard_map/ppermute | solution.py:286
  111.7 28.6 %collective-permute-start.15 = (bf16[8,4,4,16,128]{4,3,2,1,0:T(8,128)(2,1)S(1)}, bf16[8,4,4,16,128]{4,3,2,1,0:T(8,128)(2,1)S(1)}, u32[]{:S(2)}, u32[]{:S(2)}) collective-permute-start(bf16[8,4,4,16,128]{4,3,2,1,0:T(8,128)(2,1)S(1)} %get-tuple-element.64), channel_id=1, source_target_pairs={{0,6},{2,0},{4,2},{6,4},{1,7},{3,1},{5,3},{7,5},{8,14},{10,8},{12,... | collective-permute-start | bytes 1572872 | tf_op jit(solution)/shard_map/ppermute | solution.py:286
  126.8 0.8 copy-start.13
  130.5 0.8 copy-start.15
  140.3 0.8 copy-start.17
  144.7 1.4 copy-start
  146.1 7.6 %copy-start.12 = (bf16[512,512]{1,0:T(8,128)(2,1)S(1)}, bf16[512,512]{1,0:T(8,128)(2,1)}, u32[]{:S(2)}) copy-start(bf16[512,512]{1,0:T(8,128)(2,1)} %copy-done.11) | copy-start | bytes 1572868
  146.1 33.5 %all-to-all-start.2 = ((bf16[32,16,16,128]{3,2,1,0:T(8,128)(2,1)}), bf16[32,16,16,128]{3,2,1,0:T(8,128)(2,1)}, u32[]{:S(2)}, u32[]{:S(2)}) async-start(bf16[32,16,16,128]{3,2,1,0:T(8,128)(2,1)} %bitcast.16), calls=%async_computation.2 | async-start | bytes 4194304 | tf_op jit(solution)/shard_map/all_to_all | solution.py:290
  153.7 1.0 copy-start.14
  154.8 1.0 copy-start.16
  155.8 1.0 copy-start.18
  159.8 1.4 copy-start.7
  179.6 66.7 %all-to-all-start.3 = ((bf16[32,4,64,128]{3,2,1,0:T(8,128)(2,1)}), bf16[32,4,64,128]{3,2,1,0:T(8,128)(2,1)}, u32[]{:S(2)}, u32[]{:S(2)}) async-start(bf16[32,4,64,128]{3,2,1,0:T(8,128)(2,1)} %bitcast.20), calls=%async_computation.3 | async-start | bytes 4194304 | tf_op jit(solution)/shard_map/all_to_all | solution.py:296
  190.1 1.6 copy-start.8
  191.7 4.0 %copy-start.3 = (bf16[64,8,16,128]{3,2,1,0:T(8,128)(2,1)S(1)}, bf16[64,8,16,128]{3,2,1,0:T(8,128)(2,1)}, u32[]{:S(2)}) copy-start(bf16[64,8,16,128]{3,2,1,0:T(8,128)(2,1)} %copy-done.1) | copy-start | bytes 6291460
  195.7 6.2 %collective-permute-start.16 = (f32[4,4,16,512]{3,2,1,0:T(8,128)S(1)}, f32[4,4,16,512]{3,2,1,0:T(8,128)S(1)}, u32[]{:S(2)}, u32[]{:S(2)}) collective-permute-start(f32[4,4,16,512]{3,2,1,0:T(8,128)S(1)} %get-tuple-element.75), channel_id=1, source_target_pairs={{0,8},{8,0},{1,9},{9,1},{2,10},{10,2},{3,11},{11,3},{4,12},{12,4},... | collective-permute-start | bytes 1572872 | tf_op jit(solution)/shard_map/ppermute | solution.py:301
  201.2 2.2 collective-permute-start.17
  204.0 15.5 %collective-permute-start.18 = (f32[4,2,16,512]{3,2,1,0:T(8,128)S(1)}, f32[4,2,16,512]{3,2,1,0:T(8,128)S(1)}, u32[]{:S(2)}, u32[]{:S(2)}) collective-permute-start(f32[4,2,16,512]{3,2,1,0:T(8,128)S(1)} %get-tuple-element.80), channel_id=1, source_target_pairs={{0,16},{16,32},{32,48},{48,0},{1,17},{17,33},{33,49},{49,1},{2,18}... | collective-permute-start | bytes 786440 | tf_op jit(solution)/shard_map/ppermute | solution.py:305
  204.7 14.9 %collective-permute-start.19 = (f32[4,2,16,512]{3,2,1,0:T(8,128)S(1)}, f32[4,2,16,512]{3,2,1,0:T(8,128)S(1)}, u32[]{:S(2)}, u32[]{:S(2)}) collective-permute-start(f32[4,2,16,512]{3,2,1,0:T(8,128)S(1)} %get-tuple-element.81), channel_id=1, source_target_pairs={{0,32},{16,48},{32,0},{48,16},{1,33},{17,49},{33,1},{49,17},{2,34}... | collective-permute-start | bytes 786440 | tf_op jit(solution)/shard_map/ppermute | solution.py:305
  206.4 13.7 %collective-permute-start.20 = (f32[4,2,16,512]{3,2,1,0:T(8,128)S(1)}, f32[4,2,16,512]{3,2,1,0:T(8,128)S(1)}, u32[]{:S(2)}, u32[]{:S(2)}) collective-permute-start(f32[4,2,16,512]{3,2,1,0:T(8,128)S(1)} %get-tuple-element.82), channel_id=1, source_target_pairs={{0,48},{16,0},{32,16},{48,32},{1,49},{17,1},{33,17},{49,33},{2,50}... | collective-permute-start | bytes 786440 | tf_op jit(solution)/shard_map/ppermute | solution.py:305
  220.8 4.5 %collective-permute-start.21 = (f32[2,16,512]{2,1,0:T(8,128)S(1)}, f32[2,16,512]{2,1,0:T(8,128)S(1)}, u32[]{:S(2)}, u32[]{:S(2)}) collective-permute-start(f32[2,16,512]{2,1,0:T(8,128)S(1)} %get-tuple-element.84), channel_id=1, source_target_pairs={{0,2},{2,4},{4,6},{6,0},{1,3},{3,5},{5,7},{7,1},{8,10},{10,12},{12... | collective-permute-start | bytes 196616 | tf_op jit(solution)/shard_map/ppermute | solution.py:307
  221.4 11.2 %collective-permute-start.22 = (f32[2,16,512]{2,1,0:T(8,128)S(1)}, f32[2,16,512]{2,1,0:T(8,128)S(1)}, u32[]{:S(2)}, u32[]{:S(2)}) collective-permute-start(f32[2,16,512]{2,1,0:T(8,128)S(1)} %get-tuple-element.85), channel_id=1, source_target_pairs={{0,4},{2,6},{4,0},{6,2},{1,5},{3,7},{5,1},{7,3},{8,12},{10,14},{12... | collective-permute-start | bytes 196616 | tf_op jit(solution)/shard_map/ppermute | solution.py:307
  223.8 8.8 %collective-permute-start.23 = (f32[2,16,512]{2,1,0:T(8,128)S(1)}, f32[2,16,512]{2,1,0:T(8,128)S(1)}, u32[]{:S(2)}, u32[]{:S(2)}) collective-permute-start(f32[2,16,512]{2,1,0:T(8,128)S(1)} %get-tuple-element.86), channel_id=1, source_target_pairs={{0,6},{2,0},{4,2},{6,4},{1,7},{3,1},{5,3},{7,5},{8,14},{10,8},{12,... | collective-permute-start | bytes 196616 | tf_op jit(solution)/shard_map/ppermute | solution.py:307
  233.8 12.5 %collective-permute-start.24 = (f32[2,16,512]{2,1,0:T(8,128)S(1)}, f32[2,16,512]{2,1,0:T(8,128)S(1)}, u32[]{:S(2)}, u32[]{:S(2)}) collective-permute-start(f32[2,16,512]{2,1,0:T(8,128)S(1)} %shard_map.87), channel_id=1, source_target_pairs={{0,0},{2,64},{4,128},{6,192},{64,2},{66,66},{68,130},{70,194},{128... | collective-permute-start | bytes 196616 | tf_op jit(solution)/shard_map/ppermute | solution.py:309

commit v3 on v2

v3 whole, which is shorter than its diff:
```python
import functools

import jax
import jax.numpy as jnp
from jax import lax
from jax.experimental import pallas as pl
from jax.experimental.pallas import tpu as pltpu
from jax.sharding import Mesh, PartitionSpec as P

ROWS = 512
COLS = 512
SLAB = 128
BF = jnp.bfloat16
F32 = jnp.float32
ZYC = ("zh", "y", "core", "zl")
ZX = ("zh", "x", "zl")
PLANE = ("y", "core", "x")
NEAR, FAR = (0, 1, 7, 2), (6, 3, 5, 4)
PARAMS = pltpu.CompilerParams(vmem_limit_bytes=48 * 1024 * 1024)
VM = pl.BlockSpec(memory_space=pltpu.VMEM)
SM = pl.BlockSpec(memory_space=pltpu.SMEM)
HB = pl.BlockSpec(memory_space=pltpu.HBM)


def call(kernel, outs, scratch=(), n_in=1, hbm=(), flops=0, moved=4 << 20):
    return pl.pallas_call(
        kernel,
        out_shape=outs,
        in_specs=[SM] + [HB if k in hbm else VM for k in range(n_in)],
        out_specs=jax.tree.map(lambda _: HB if "out" in hbm else VM, outs),
        scratch_shapes=list(scratch),
        compiler_params=PARAMS,
        cost_estimate=pl.CostEstimate(flops=flops, bytes_accessed=moved, transcendentals=0),
    )


def shape(*dims, dtype=BF):
    return jax.ShapeDtypeStruct(dims, dtype)


def gate_kernel(gate, up, out):
    for k in range(8):
        lanes = slice(k * SLAB, (k + 1) * SLAB)
        prod = gate[:, :, lanes].astype(F32) * up[:, :, lanes].astype(F32)
        out[k // 2, :, k % 2] = jnp.swapaxes(prod, 0, 1).astype(BF).reshape(2, 8, 16, SLAB)


def gate_call(gate, up):
    return pl.pallas_call(
        gate_kernel,
        grid=(4,),
        out_shape=shape(4, 8, 2, 8, 16, SLAB),
        in_specs=[pl.BlockSpec((16, 16, 1024), lambda c: (0, c, 0))] * 2,
        out_specs=pl.BlockSpec((4, 2, 2, 8, 16, SLAB), lambda c: (0, c, 0, 0, 0, 0)),
        compiler_params=PARAMS,
        cost_estimate=pl.CostEstimate(flops=1 << 20, bytes_accessed=6 << 20, transcendentals=0),
    )(gate, up)


def second_factor_kernel(pos, *refs):
    f2t, full = refs[4:]
    for k in range(4):
        rows = pl.ds(pl.multiple_of((pos[2] ^ k) * 128, 128), 128)
        full[rows, :] = refs[k][0].astype(F32)
    f2t[...] = full[...].T.astype(BF)


def first_factor_kernel(pos, *refs):
    f1, f1tp, full = refs[4:]
    for k in range(4):
        rows = pl.ds(pl.multiple_of((pos[2] ^ k) * 128, 128), 128)
        full[rows, :] = refs[k][0].astype(F32)
    f1[...] = full[...].astype(BF)
    ordered = jnp.concatenate(
        [
            full[x * 128 + zl * 64 + c * 8 : x * 128 + zl * 64 + c * 8 + 8, :]
            for x in range(4)
            for c in range(8)
            for zl in range(2)
        ],
        axis=0,
    )
    f1tp[...] = ordered.T.astype(BF)


def bring(g, flat, sem):
    copies = [
        pltpu.make_async_copy(
            g.at[:, :, k // 8, k % 8], flat.at[:, :, :, pl.ds(k * SLAB, SLAB)], sem.at[k]
        )
        for k in range(16)
    ]
    for copy in copies:
        copy.start()
    return copies


def second_apply_kernel(pos, f2t, g, *refs):
    outs, flat, swap, sem = refs[:8], refs[8], refs[9], refs[10]
    for copy in bring(g, flat, sem):
        copy.wait()

    def body(zh, _):
        rows = pl.ds(pl.multiple_of(zh * 128, 128), 128)
        for k in range(0, 16, 2):
            right = flat[:, :, :, k * SLAB : (k + 2) * SLAB].reshape(ROWS, 2 * SLAB)
            part = jnp.dot(f2t[rows, :], right, preferred_element_type=F32)
            swap[pl.ds(k, 128, stride=16), :] = part[:, :SLAB]
            swap[pl.ds(k + 1, 128, stride=16), :] = part[:, SLAB:]
        for t, out in enumerate(outs):
            at = pl.multiple_of(lax.rem(pos[3] + t, 8) * 256, 256)
            tile = swap[pl.ds(at, 256), :].astype(BF).reshape(4, 4, 16, SLAB)
            for x in range(4):
                out[x, zh] = tile[x]
        return 0

    lax.fori_loop(0, 4, body, 0)


def second_cut_kernel(pos, a, b, c, d, *outs):
    for s, out in enumerate(outs):
        owner = lax.rem(pos[0] + s, 4)
        for t, block in enumerate((a, b, c, d)):
            out[t] = block[owner]


def first_apply_kernel(pos, f1t, *refs):
    out, mgw = refs[8:]
    for i, steps in enumerate((NEAR, FAR)):
        for s in range(4):
            block = refs[i * 4 + s]
            for j, t in enumerate(steps):
                at = lax.rem(pos[0] + 4 - s, 4) * 128 + lax.rem(pos[3] + 8 - t, 8) * 16
                rows = pl.ds(pl.multiple_of(at, 16), 16)
                for k in range(16):
                    mgw[rows, k * SLAB : (k + 1) * SLAB] = block[j, k // 4, k % 4]
    for k in range(0, 16, 2):
        part = jnp.dot(f1t[...], mgw[:, k * SLAB : (k + 2) * SLAB], preferred_element_type=F32).astype(BF)
        out[k // 4, :, :, k % 4] = part[:, :SLAB].reshape(4, 2, 64, SLAB)
        out[k // 4, :, :, k % 4 + 1] = part[:, SLAB:].reshape(4, 2, 64, SLAB)


def token_cut_kernel(pos, x0, x1, x2, x3, out):
    for s, block in enumerate((x0, x1, x2, x3)):
        source = lax.rem(pos[0] + 4 - s, 4)
        for k in range(8):
            out[k // 2, k % 2, source] = block[:, :, k * SLAB : (k + 1) * SLAB]


def grad_join_kernel(pos, part, out, stage, arrive, leave):
    def into(x, k):
        return pltpu.make_async_copy(
            part.at[k // 2, x, k % 2], stage.at[pl.ds(4 * x, 4), :, pl.ds(SLAB * k, SLAB)], arrive.at[x, k]
        )

    def away(x):
        rows = pl.ds(4 * x, 4)
        return pltpu.make_async_copy(stage.at[rows], out.at[rows], leave.at[x])

    for x in range(4):
        for k in range(8):
            into(x, k).start()
    for x in range(4):
        for k in range(8):
            into(x, k).wait()
        away(x).start()
    for x in range(4):
        away(x).wait()


def mix_kernel(pos, f1, tok, mixed, tokw, swap, stage, sem):
    for k in range(16):
        for x in range(4):
            for zl in range(2):
                at = (x * 2 + zl) * 64
                tokw[at : at + 64, k * SLAB : (k + 1) * SLAB] = tok[k // 4, zl, x, k % 4]

    def copy(b):
        return pltpu.make_async_copy(stage.at[b], mixed.at[:, b], sem.at[b])

    for b in range(4):
        for k in range(0, 16, 2):
            part = jnp.dot(
                f1[b * 128 : (b + 1) * 128, :], tokw[:, k * SLAB : (k + 2) * SLAB], preferred_element_type=F32
            )
            swap[pl.ds(k, 128, stride=16), :] = part[:, :SLAB]
            swap[pl.ds(k + 1, 128, stride=16), :] = part[:, SLAB:]
        for zl in range(2):
            stage[b, :, zl] = swap[zl * 1024 : (zl + 1) * 1024, :].astype(BF).reshape(8, 8, 16, SLAB)
        copy(b).start()
    for b in range(4):
        copy(b).wait()


def first_kernel(pos, mgw, tok, keep, give, tokw):
    for k in range(16):
        for x in range(4):
            for zl in range(2):
                at = (x * 2 + zl) * 64
                tokw[at : at + 64, k * SLAB : (k + 1) * SLAB] = tok[k // 4, zl, x, k % 4]
    for x in range(4):
        left = mgw[x * 128 : (x + 1) * 128, :]
        part = lax.dot_general(left, tokw[...], (((1,), (1,)), ((), ())), preferred_element_type=F32)

        def put(cores):
            for yc in range(8):
                for zl in range(2):
                    at, half = yc * 16 + zl * 8, (yc % 2) * 8
                    cores[(yc // 2) % 2][zl * 2 + yc // 4, x, half : half + 8, :] = part[at : at + 8, :]

        @pl.when(pos[5] == 0)
        def _():
            put((keep, give))

        @pl.when(pos[5] == 1)
        def _():
            put((give, keep))


def second_kernel(pos, g, mixed, keep, give, flat, mixw, sem):
    core = pos[5]
    copies = bring(g, flat, sem)
    for k in range(16):
        lanes = slice(k * SLAB, (k + 1) * SLAB)
        mixw[:, lanes] = mixed[:, :, k // 8, k % 8].reshape(ROWS, SLAB)
    for copy in copies:
        copy.wait()
    for zh in range(4):
        part = lax.dot_general(
            flat[zh].reshape(128, 16 * SLAB), mixw[...], (((1,), (1,)), ((), ())), preferred_element_type=F32
        )

        def put(keep, give):
            for y in range(4):
                keep[y, zh] = part[y * 32 : y * 32 + 16, :]
                give[y, zh] = part[y * 32 + 16 : y * 32 + 32, :]

        @pl.when(core == 0)
        def _():
            put(keep, give)

        @pl.when(core == 1)
        def _():
            put(give, keep)


def core_sum_kernel(pos, f, fo, s, so, *outs):
    for t, out in enumerate(outs):
        y = lax.rem(pos[4] + t, 4)
        out[:, 0] = f[y] + fo[y]
        out[:, 1] = s[y] + so[y]


def y_sum_kernel(pos, a, b, c, d, *outs):
    for s, out in enumerate(outs):
        x = lax.rem(pos[0] + s, 4)
        out[...] = (a[x] + b[x]) + (c[x] + d[x])


def sum_kernel(pos, a, b, c, d, out):
    place = lax.broadcasted_iota(jnp.int32, (ROWS, ROWS), 0)
    row = lax.broadcasted_iota(jnp.int32, (ROWS, ROWS), 1)
    want = ((row >> 4) & 7) * 64 + ((row >> 2) & 3) * 16 + (row >> 7) * 4 + (row & 3)
    order = (place == want).astype(F32)
    out[0] = ((a[0] + b[0]) + (c[0] + d[0])) * (ROWS**-0.5 * SLAB**-0.5)
    total = (a[1] + b[1]) + (c[1] + d[1])
    second = jnp.dot(total, order, precision=lax.Precision.HIGHEST, preferred_element_type=F32)
    out[1] = second * (COLS**-0.5 * SLAB**-0.5)


def shifts(count):
    return lambda s: [(k, (k + s) % count) for k in range(count)]


def local(tokens, gate, upstream, first_factor, second_factor):
    zh, zl = lax.axis_index("zh"), lax.axis_index("zl")
    x, y, core = lax.axis_index("x"), lax.axis_index("y"), lax.axis_index("core")
    z, yc, part = zh * 2 + zl, y * 2 + core, (y % 2) * 2 + core
    pos = jnp.stack([x, z, part, yc, y, core]).astype(jnp.int32)
    four, eight = shifts(4), shifts(8)
    wide = pltpu.VMEM((ROWS, 16 * SLAB), BF)
    swap = pltpu.VMEM((128 * 16, SLAB), F32)
    cols, dma = pltpu.VMEM((4, 8, 16, 16 * SLAB), BF), pltpu.SemaphoreType.DMA((16,))
    f32 = functools.partial(shape, dtype=F32)

    gated = gate_call(gate, upstream)
    grad = lax.all_to_all(gated.reshape(64, 8, 16, SLAB), ZYC, 0, 0, tiled=True).reshape(4, 8, 2, 8, 16, SLAB)
    tok_x = []
    for s in range(4):
        piece = lax.dynamic_slice_in_dim(tokens, ((x + s) % 4) * 4, 4, 0)
        tok_x.append(piece if s == 0 else lax.ppermute(piece, "x", four(s)))
    sent = call(token_cut_kernel, shape(4, 2, 4, 4, 64, SLAB), n_in=4)(pos, *tok_x)

    both = jnp.concatenate([first_factor, second_factor], 0)
    quarter = lax.dynamic_slice_in_dim(both, part * 128, 128, 1)
    got = quarter
    for s in range(1, 4):
        came = lax.ppermute(quarter, ("zh", "x"), [(k * 4 + k, k * 4 + (k + s) % 4) for k in range(4)])
        got = jnp.where(x == (zh + s) % 4, came, got)

    def gathered(own):
        return [own] + [lax.ppermute(own, ("y", "core"), [(k, k ^ s) for k in range(8)]) for s in range(1, 4)]

    full = pltpu.VMEM((COLS, COLS), F32)
    f2t = call(second_factor_kernel, shape(ROWS, ROWS), [full], n_in=4, moved=1 << 20)(pos, *gathered(got[1:]))
    got, sent, grad, f2t = lax.optimization_barrier((got, sent, grad, f2t))

    tok = lax.all_to_all(sent.reshape(8, 16, 64, SLAB), ("zh", "zl"), 0, 0, tiled=True).reshape(4, 2, 4, 4, 64, SLAB)
    f1, f1tp = call(first_factor_kernel, [shape(COLS, COLS)] * 2, [full], n_in=4, moved=1 << 20)(
        pos, *gathered(got[:1])
    )
    mg = call(second_apply_kernel, [shape(4, 4, 4, 16, SLAB)] * 8, [cols, swap, dma], n_in=2, hbm=(1,), flops=1 << 30)(
        pos, f2t, grad
    )
    crossed = []
    for steps in (NEAR, FAR):
        group = [mg[t] if t == 0 else lax.ppermute(mg[t], ("y", "core"), eight(t)) for t in steps]
        group = call(second_cut_kernel, [shape(4, 4, 4, 16, SLAB)] * 4, n_in=4, moved=1 << 21)(pos, *group)
        crossed += [group[0]] + [lax.ppermute(group[s], "x", four(s)) for s in (2, 1, 3)]
    mg = [crossed[i] for i in (0, 2, 1, 3, 4, 6, 5, 7)]
    tok, mg = lax.optimization_barrier((tok, mg))

    stage = pltpu.VMEM((4, 8, 2, 8, 16, SLAB), BF)
    mixed = call(
        mix_kernel, shape(8, 4, 2, 8, 16, SLAB), [wide, swap, stage, dma], n_in=2, hbm=("out",), flops=1 << 30
    )(pos, f1, tok)
    mixed = lax.all_to_all(mixed.reshape(32, 16, 16, SLAB), PLANE, 0, 0, tiled=True).reshape(8, 4, 2, 8, 16, SLAB)
    sent, mgw = call(
        first_apply_kernel, [shape(4, 4, 2, 4, 64, SLAB), shape(COLS, 16 * SLAB)], n_in=9, flops=1 << 30
    )(pos, f1tp, *mg)
    mixed, sent = lax.optimization_barrier((mixed, sent))

    home = lax.all_to_all(sent.reshape(32, 4, 64, SLAB), ZX, 0, 0, tiled=True)
    halves = [f32(4, 4, 16, 512)] * 2
    second_keep, second_give = call(second_kernel, halves, [cols, wide, dma], n_in=2, hbm=(0,), flops=1 << 30)(
        pos, grad, mixed
    )
    first_keep, first_give = call(first_kernel, halves, [wide], n_in=2, flops=1 << 30)(pos, mgw, tok)
    other = [(0, 1), (1, 0)]
    first_came, second_came = lax.ppermute(first_give, "core", other), lax.ppermute(second_give, "core", other)
    sums = call(core_sum_kernel, [f32(4, 2, 16, 512)] * 4, n_in=4)(
        pos, first_keep, first_came, second_keep, second_came
    )
    sums = [sums[0]] + [lax.ppermute(sums[t], "y", four(t)) for t in range(1, 4)]
    sums = call(y_sum_kernel, [f32(2, 16, 512)] * 4, n_in=4, moved=1 << 20)(pos, *sums)
    sums = [sums[0]] + [lax.ppermute(sums[s], "x", four(s)) for s in range(1, 4)]
    sums = call(sum_kernel, f32(2, 16, 512), n_in=4, moved=1 << 19)(pos, *sums)
    sums = lax.ppermute(sums, ("zh", "x"), [(a * 4 + b, b * 4 + a) for a in range(4) for b in range(4)])
    home, sums = lax.optimization_barrier((home, sums))
    token_grad = call(
        grad_join_kernel,
        shape(16, 64, 1024),
        [pltpu.VMEM((16, 64, 1024), BF), pltpu.SemaphoreType.DMA((4, 8)), pltpu.SemaphoreType.DMA((4,))],
        hbm=(0, "out"),
    )(pos, home.reshape(4, 4, 2, 4, 64, SLAB))
    return token_grad, sums[:1], sums[1:]


def solution(mesh):
    fine = Mesh(mesh.devices.reshape(4, 4, 2, 4, 2), ("zh", "y", "core", "x", "zl"))
    outer, inner = ("zh", "y", "core"), ("x", "zl")
    grid = P(outer, inner, None)
    factor = P(inner, None, None)
    return jax.shard_map(
        local,
        mesh=fine,
        in_specs=(grid, grid, grid, factor, factor),
        out_specs=(grid, P(inner, outer, None), P(inner, outer, None)),
        check_vma=False,
    )
```

time: 253 us -> 246 us (0.972)
  waiting for transfers between devices: 129 us -> 107 us
  starting transfers between devices: 65.3 us -> 76.8 us
    ppermute x6 -> x15, starting transfers between devices: 4.97 us -> 20.6 us  [the longest x6 7.94 us: local(): lax.ppermute(group[s], 'x', four(s))]
    ppermute x6 -> x15, waiting for transfers between devices: 43.7 us -> 31.6 us  [the longest x6 14.3 us: local(): lax.ppermute(group[s], 'x', four(s))]
    ppermute x3, waiting for transfers between devices: 11.9 us -> 4.03 us  [local(): lax.ppermute(quarter, ('zh', 'x'), [(k * 4 + k, k * 4 + (k + s) % 4) for...]
    ppermute x7, waiting for transfers between devices: 18.7 us -> 13.8 us  [local(): lax.ppermute(mg[t], ('y', 'core'), eight(t))]
    pallas_call x7 -> x9, Pallas kernels: 19.2 us -> 22 us  [the longest x1 6.3 us: local(): call(second_kernel, halves, [cols, wide, dma], n_in=2, hbm=(0,), flops=1...]
    dynamic_slice x0 -> x1, local copies, waits for them, and re-layouts: none -> 2.73 us  [local(): piece = lax.dynamic_slice_in_dim(tokens, (x + s) % 4 * 4, 4, 0)]
    all_to_all x1, starting transfers between devices: 9.04 us -> 6.5 us  [local(): lax.all_to_all(sent.reshape(8, 16, 64, SLAB), ('zh', 'zl'), 0, 0, tiled=T...]
    unnamed x46 -> x56, local copies, waits for them, and re-layouts: 20.5 us -> 19.2 us
  transfers between devices with their start and end apart: 29 -> 38, of which waited for: 19 -> 21; matrix products, arithmetic and copies ran while one was open for 0% -> 2% of each run, Pallas kernels for 8% -> 10%
where the time goes in v3:
time: 246 us; the launch traced here: 245 us
  waiting for transfers between devices  107 us (43%)
  starting transfers between devices  76.8 us (31%)
  Pallas kernels  35.3 us (14%)
  local copies, waits for them, and re-layouts  22.7 us (9%)
    unnamed x56, local copies, waits for them, and re-layouts  19.2 us
    all_to_all x1, waiting for transfers between devices, local(): lax.all_to_all(mixed.reshape(32, 16, 16, SLAB), PLANE, 0, 0, tiled=True)  17.4 us
    ppermute x6, waiting for transfers between devices, local(): lax.ppermute(group[s], 'x', four(s))  14.3 us
    ppermute x7, waiting for transfers between devices, local(): lax.ppermute(mg[t], ('y', 'core'), eight(t))  13.8 us
    ppermute x3, waiting for transfers between devices, local(): lax.ppermute(sums[t], 'y', four(t))  12 us
    all_to_all x1, starting transfers between devices, local(): lax.all_to_all(gated.reshape(64, 8, 16, SLAB), ZYC, 0, 0, tiled=True)  11.4 us
    ppermute x6, waiting for transfers between devices, gathered(): lax.ppermute(own, ('y', 'core'), [(k, k ^ s) for k in range(8)])  11.1 us
    all_to_all x1, starting transfers between devices, local(): home = lax.all_to_all(sent.reshape(32, 4, 64, SLAB), ZX, 0, 0, tiled=True)  10.6 us
  transfers between devices with their start and end apart: 38, of which 21 were waited for; matrix products, arithmetic and copies ran while one was open for 2% of the time, Pallas kernels for 10%

profile of v3, /device:TPU:70, one launch (start us, length us, event | category | flops | bytes accessed | tf_op | source)
XLA Modules:
  0.0 244.9 jit_solution(18228807567514588943)
XLA Ops:
  0.6 1.6 copy-done.5
  2.2 4.4 %shard_map.77 = bf16[4,8,2,8,16,128]{5,4,3,2,1,0:T(8,128)(2,1)} custom-call(bf16[16,64,1024]{2,1,0:T(8,128)(2,1)S(1)} %copy-done.5, bf16[16,64,1024]{2,1,0:T(8,128)(2,1)} %up.1), custom_call_target="tpu_custom_call" | custom-call | flops 1048576 | bytes 6291456 | tf_op jit(solution)/shard_map/pallas_call | solution.py:49
  6.6 11.4 %all-to-all-start = ((bf16[64,8,16,128]{3,2,1,0:T(8,128)(2,1)}), bf16[64,8,16,128]{3,2,1,0:T(8,128)(2,1)S(1)}, u32[]{:S(2)}, u32[]{:S(2)}) async-start(bf16[64,8,16,128]{3,2,1,0:T(8,128)(2,1)} %bitcast.6), calls=%async_computation | async-start | bytes 4194304 | tf_op jit(solution)/shard_map/all_to_all | solution.py:287
  19.5 1.3 collective-permute-start.1
  20.8 1.4 collective-permute-start.2
  22.2 2.7 %constant_dynamic-slice_fusion = (bf16[4,64,1024]{2,1,0:T(8,128)(2,1)}, bf16[4,64,1024]{2,1,0:T(8,128)(2,1)}, bf16[4,64,1024]{2,1,0:T(8,128)(2,1)S(1)}, bf16[4,64,1024]{2,1,0:T(8,128)(2,1)}) fusion(bf16[16,64,1024]{2,1,0:T(8,128)(2,1)} %param.5, s32[]{:T(128)S(6)} %select_n.88, s32[]{:T(128)S(6)} %select_n.84, s32[]{:T(128)S(6)} %select_n.82, s32[]{:T(128)S(6)} %select_n.86), kind=kLoop, calls=%fused_computation.4 | loop fusion | bytes 4194320 | tf_op jit(solution)/shard_map/dynamic_slice | solution.py:290
  24.9 1.1 collective-permute-start.3
  26.1 4.3 %collective-permute-start.4 = (bf16[4,64,1024]{2,1,0:T(8,128)(2,1)}, bf16[4,64,1024]{2,1,0:T(8,128)(2,1)}, u32[]{:S(2)}, u32[]{:S(2)}) collective-permute-start(bf16[4,64,1024]{2,1,0:T(8,128)(2,1)} %get-tuple-element.104), channel_id=1, source_target_pairs={{0,4},{2,6},{4,0},{6,2},{1,5},{3,7},{5,1},{7,3},{8,12},{10,14},{12... | collective-permute-start | bytes 1572872 | tf_op jit(solution)/shard_map/ppermute | solution.py:291
  30.4 1.4 collective-permute-start.5
  31.8 4.0 %collective-permute-done.1 = bf16[2,128,512]{2,1,0:T(8,128)(2,1)} collective-permute-done((bf16[2,128,512]{2,1,0:T(8,128)(2,1)}, bf16[2,128,512]{2,1,0:T(8,128)(2,1)}, u32[]{:S(2)}, u32[]{:S(2)}) %collective-permute-start.1) | collective-permute-done | bytes 262176 | tf_op jit(solution)/shard_map/ppermute | solution.py:298
  35.8 1.2 select_select_fusion
  37.2 1.6 collective-permute-start.7
  38.7 1.0 collective-permute-start.8
  39.8 5.5 %collective-permute-done.7.refs_2_ = bf16[1,128,512]{2,1,0:T(8,128)(2,1)S(1)} collective-permute-done((bf16[1,128,512]{2,1,0:T(8,128)(2,1)S(1)}, bf16[1,128,512]{2,1,0:T(8,128)(2,1)S(1)}, u32[]{:S(2)}, u32[]{:S(2)}) %collective-permute-start.7) | collective-permute-done | bytes 131104 | tf_op jit(solution)/shard_map/ppermute | solution.py:302
  45.3 3.9 %collective-permute-done.8.refs_3_ = bf16[1,128,512]{2,1,0:T(8,128)(2,1)} collective-permute-done((bf16[1,128,512]{2,1,0:T(8,128)(2,1)S(1)}, bf16[1,128,512]{2,1,0:T(8,128)(2,1)}, u32[]{:S(2)}, u32[]{:S(2)}) %collective-permute-start.8) | collective-permute-done | bytes 131104 | tf_op jit(solution)/shard_map/ppermute | solution.py:302
  49.3 1.2 shard_map.78.f2t
  51.3 6.2 %collective-permute-done.5.x3 = bf16[4,64,1024]{2,1,0:T(8,128)(2,1)} collective-permute-done((bf16[4,64,1024]{2,1,0:T(8,128)(2,1)}, bf16[4,64,1024]{2,1,0:T(8,128)(2,1)}, u32[]{:S(2)}, u32[]{:S(2)}) %collective-permute-start.5) | collective-permute-done | bytes 524320 | tf_op jit(solution)/shard_map/ppermute | solution.py:291
  57.4 1.6 shard_map.76
  59.0 1.3 copy-done.4
  60.3 7.2 %all-to-all-done = bf16[64,8,16,128]{3,2,1,0:T(8,128)(2,1)S(1)} async-done(((bf16[64,8,16,128]{3,2,1,0:T(8,128)(2,1)}), bf16[64,8,16,128]{3,2,1,0:T(8,128)(2,1)S(1)}, u32[]{:S(2)}, u32[]{:S(2)}) %all-to-all-start) | async-done | bytes 2097184 | tf_op jit(solution)/shard_map/all_to_all | solution.py:287
  67.5 1.3 copy-done.1
  68.9 6.5 %all-to-all-start.1 = ((bf16[8,16,64,128]{3,2,1,0:T(8,128)(2,1)}), bf16[8,16,64,128]{3,2,1,0:T(8,128)(2,1)S(1)}, u32[]{:S(2)}, u32[]{:S(2)}) async-start(bf16[8,16,64,128]{3,2,1,0:T(8,128)(2,1)} %bitcast.19), calls=%async_computation.1 | async-start | bytes 4194304 | tf_op jit(solution)/shard_map/all_to_all | solution.py:308
  75.4 1.6 copy-done.2
  77.0 3.9 %shard_map.80 = (bf16[4,4,4,16,128]{4,3,2,1,0:T(8,128)(2,1)S(1)}, bf16[4,4,4,16,128]{4,3,2,1,0:T(8,128)(2,1)S(1)}, bf16[4,4,4,16,128]{4,3,2,1,0:T(8,128)(2,1)S(1...) custom-call(s32[6]{0:T(128)S(1)} %stack.27.pos, ...), custom_call_target="tpu_custom_call" | custom-call | flops 1073741824 | bytes 4194304 | tf_op jit(solution)/shard_map/pallas_call | solution.py:312
  80.9 1.2 collective-permute-start.18
  82.1 3.2 %collective-permute-start.20 = (bf16[4,4,4,16,128]{4,3,2,1,0:T(8,128)(2,1)S(1)}, bf16[4,4,4,16,128]{4,3,2,1,0:T(8,128)(2,1)S(1)}, u32[]{:S(2)}, u32[]{:S(2)}) collective-permute-start(bf16[4,4,4,16,128]{4,3,2,1,0:T(8,128)(2,1)S(1)} %get-tuple-element.67), channel_id=1, source_target_pairs={{0,40},{8,48},{16,56},{24,0},{32,8},{40,16},{48,24},{56,32},{1,41}... | collective-permute-start | bytes 786440 | tf_op jit(solution)/shard_map/ppermute | solution.py:317
  85.4 1.8 collective-permute-start.21
  87.2 7.3 %collective-permute-done.18.a = bf16[4,4,4,16,128]{4,3,2,1,0:T(8,128)(2,1)S(1)} collective-permute-done((bf16[4,4,4,16,128]{4,3,2,1,0:T(8,128)(2,1)S(1)}, bf16[4,4,4,16,128]{4,3,2,1,0:T(8,128)(2,1)S(1)}, u32[]{:S(2)}, u32[]{:S(2)}) %collective-permute-start.18) | collective-permute-done | bytes 262176 | tf_op jit(solution)/shard_map/ppermute | solution.py:317
  95.3 1.9 collective-permute-done.20.c
  97.2 4.0 %collective-permute-done.21.d = bf16[4,4,4,16,128]{4,3,2,1,0:T(8,128)(2,1)S(1)} collective-permute-done((bf16[4,4,4,16,128]{4,3,2,1,0:T(8,128)(2,1)S(1)}, bf16[4,4,4,16,128]{4,3,2,1,0:T(8,128)(2,1)S(1)}, u32[]{:S(2)}, u32[]{:S(2)}) %collective-permute-start.21) | collective-permute-done | bytes 262176 | tf_op jit(solution)/shard_map/ppermute | solution.py:317
  102.6 2.3 collective-permute-start.10
  106.4 1.8 collective-permute-start.23
  109.0 1.5 collective-permute-start.24
  110.5 1.6 collective-permute-done.11.refs_3_
  112.1 1.5 collective-permute-start.15
  113.6 2.1 collective-permute-start.16
  117.5 5.9 %collective-permute-done.24.refs_7_ = bf16[4,4,4,16,128]{4,3,2,1,0:T(8,128)(2,1)S(1)} collective-permute-done((bf16[4,4,4,16,128]{4,3,2,1,0:T(8,128)(2,1)S(1)}, bf16[4,4,4,16,128]{4,3,2,1,0:T(8,128)(2,1)S(1)}, u32[]{:S(2)}, u32[]{:S(2)}) %collective-permute-start.24) | collective-permute-done | bytes 262176 | tf_op jit(solution)/shard_map/ppermute | solution.py:319
  124.9 2.8 %collective-permute-done.16.refs_2_ = bf16[4,4,4,16,128]{4,3,2,1,0:T(8,128)(2,1)S(1)} collective-permute-done((bf16[4,4,4,16,128]{4,3,2,1,0:T(8,128)(2,1)S(1)}, bf16[4,4,4,16,128]{4,3,2,1,0:T(8,128)(2,1)S(1)}, u32[]{:S(2)}, u32[]{:S(2)}) %collective-permute-start.16) | collective-permute-done | bytes 262176 | tf_op jit(solution)/shard_map/ppermute | solution.py:319
  128.4 5.5 %collective-permute-done.17.refs_3_ = bf16[4,4,4,16,128]{4,3,2,1,0:T(8,128)(2,1)S(1)} collective-permute-done((bf16[4,4,4,16,128]{4,3,2,1,0:T(8,128)(2,1)S(1)}, bf16[4,4,4,16,128]{4,3,2,1,0:T(8,128)(2,1)S(1)}, u32[]{:S(2)}, u32[]{:S(2)}) %collective-permute-start.17) | collective-permute-done | bytes 262176 | tf_op jit(solution)/shard_map/ppermute | solution.py:319
  134.7 3.7 %shard_map.83 = bf16[8,4,2,8,16,128]{5,4,3,2,1,0:T(8,128)(2,1)S(1)} custom-call(s32[6]{0:T(128)S(1)} %stack.27.pos, bf16[512,512]{1,0:T(8,128)(2,1)S(1)} %get-tuple-element.53.f1, bf16[4,2,4,4,64,128]{5,4,3,2,1,0:T(8,128)(2,1)S(1)} %bitcast.14), custom_call_target="tpu_custom_call" | custom-call | flops 1073741824 | bytes 4194304 | tf_op jit(solution)/shard_map/pallas_call | solution.py:324
  138.4 1.4 copy-done
  139.8 6.4 %all-to-all-start.2 = ((bf16[32,16,16,128]{3,2,1,0:T(8,128)(2,1)}), bf16[32,16,16,128]{3,2,1,0:T(8,128)(2,1)}, u32[]{:S(2)}, u32[]{:S(2)}) async-start(bf16[32,16,16,128]{3,2,1,0:T(8,128)(2,1)} %bitcast.16), calls=%async_computation.2 | async-start | bytes 4194304 | tf_op jit(solution)/shard_map/all_to_all | solution.py:327
  147.2 0.9 copy-done.17
  148.1 0.9 copy-done.19
  149.1 0.9 copy-done.21
  150.0 0.9 copy-done.23
  151.0 2.3 shard_map.84
  153.3 1.3 copy-done.6
  154.6 17.4 %all-to-all-done.2 = bf16[32,16,16,128]{3,2,1,0:T(8,128)(2,1)} async-done(((bf16[32,16,16,128]{3,2,1,0:T(8,128)(2,1)}), bf16[32,16,16,128]{3,2,1,0:T(8,128)(2,1)}, u32[]{:S(2)}, u32[]{:S(2)}) %all-to-all-start.2) | async-done | bytes 2097184 | tf_op jit(solution)/shard_map/all_to_all | solution.py:327
  172.1 10.6 %all-to-all-start.3 = ((bf16[32,4,64,128]{3,2,1,0:T(8,128)(2,1)}), bf16[32,4,64,128]{3,2,1,0:T(8,128)(2,1)}, u32[]{:S(2)}, u32[]{:S(2)}) async-start(bf16[32,4,64,128]{3,2,1,0:T(8,128)(2,1)} %bitcast.20), calls=%async_computation.3 | async-start | bytes 4194304 | tf_op jit(solution)/shard_map/all_to_all | solution.py:333
  182.7 1.6 copy-done.7
  184.3 4.1 %shard_map.85 = (f32[4,4,16,512]{3,2,1,0:T(8,128)S(1)}, f32[4,4,16,512]{3,2,1,0:T(8,128)S(1)}) custom-call(s32[6]{0:T(128)S(1)} %stack.27.pos, bf16[512,2048]{1,0:T(8,128)(2,1)S(1)} %copy-done.7, bf16[4,2,4,4,64,128]{5,4,3,2,1,0:T(8,128)(2,1)S(1)} %bitcast.15), custom_call_target="tpu_custom_call" | custom-call | flops 1073741824 | bytes 4194304 | tf_op jit(solution)/shard_map/pallas_call | solution.py:338
  188.5 6.3 %shard_map.86 = (f32[4,4,16,512]{3,2,1,0:T(8,128)S(1)}, f32[4,4,16,512]{3,2,1,0:T(8,128)S(1)}) custom-call(s32[6]{0:T(128)S(1)} %stack.27.pos, bf16[4,8,2,8,16,128]{5,4,3,2,1,0:T(8,128)(2,1)S(1)} %bitcast.18, bf16[8,4,2,8,16,128]{5,4,3,2,1,0:T(8,128)(2,1)} %bitcast.11.mixed), custom_call_target="tpu_custom_call" | custom-call | flops 1073741824 | bytes 4194304 | tf_op jit(solution)/shard_map/pallas_call | solution.py:335
  195.5 1.5 collective-permute-done.26.so
  198.3 1.7 collective-permute-start.28
  200.0 1.7 collective-permute-start.29
  201.7 11.4 %collective-permute-done.27.b = f32[4,2,16,512]{3,2,1,0:T(8,128)S(1)} collective-permute-done((f32[4,2,16,512]{3,2,1,0:T(8,128)S(1)}, f32[4,2,16,512]{3,2,1,0:T(8,128)S(1)}, u32[]{:S(2)}, u32[]{:S(2)}) %collective-permute-start.27) | collective-permute-done | bytes 262176 | tf_op jit(solution)/shard_map/ppermute | solution.py:344
  215.0 2.4 collective-permute-start.31
  217.4 1.6 collective-permute-done.30.b
  219.0 8.3 %collective-permute-done.31.c = f32[2,16,512]{2,1,0:T(8,128)S(1)} collective-permute-done((f32[2,16,512]{2,1,0:T(8,128)S(1)}, f32[2,16,512]{2,1,0:T(8,128)S(1)}, u32[]{:S(2)}, u32[]{:S(2)}) %collective-permute-start.31) | collective-permute-done | bytes 65568 | tf_op jit(solution)/shard_map/ppermute | solution.py:346
  227.3 1.2 shard_map.89
  228.5 3.0 %collective-permute-start.33 = (f32[2,16,512]{2,1,0:T(8,128)S(1)}, f32[2,16,512]{2,1,0:T(8,128)S(1)}, u32[]{:S(2)}, u32[]{:S(2)}) collective-permute-start(f32[2,16,512]{2,1,0:T(8,128)S(1)} %shard_map.89), channel_id=1, source_target_pairs={{0,0},{2,64},{4,128},{6,192},{64,2},{66,66},{68,130},{70,194},{128... | collective-permute-start | bytes 196616 | tf_op jit(solution)/shard_map/ppermute | solution.py:348
  231.5 9.5 %collective-permute-done.33 = f32[2,16,512]{2,1,0:T(8,128)S(1)} collective-permute-done((f32[2,16,512]{2,1,0:T(8,128)S(1)}, f32[2,16,512]{2,1,0:T(8,128)S(1)}, u32[]{:S(2)}, u32[]{:S(2)}) %collective-permute-start.33) | collective-permute-done | bytes 65568 | tf_op jit(solution)/shard_map/ppermute | solution.py:348
  241.0 3.2 %shard_map.90 = bf16[16,64,1024]{2,1,0:T(8,128)(2,1)} custom-call(s32[6]{0:T(128)S(1)} %stack.27.pos, bf16[4,4,2,4,64,128]{5,4,3,2,1,0:T(8,128)(2,1)} %bitcast.13.part), custom_call_target="tpu_custom_call" | custom-call | bytes 4194304 | tf_op jit(solution)/shard_map/pallas_call | solution.py:350
  (90 shorter events, 17.0 us)
Async XLA Ops:
  0.6 1.6 copy-start.5
  6.6 11.5 %copy-start.24 = (bf16[1,512,512]{2,1,0:T(8,128)(2,1)S(1)}, bf16[1,512,512]{2,1,0:T(8,128)(2,1)}, u32[]{:S(2)}) copy-start(bf16[1,512,512]{2,1,0:T(8,128)(2,1)} %param.8) | copy-start | bytes 1572868
  6.6 11.5 %copy-start.25 = (bf16[1,512,512]{2,1,0:T(8,128)(2,1)S(1)}, bf16[1,512,512]{2,1,0:T(8,128)(2,1)}, u32[]{:S(2)}) copy-start(bf16[1,512,512]{2,1,0:T(8,128)(2,1)} %param.9) | copy-start | bytes 1572868
  6.6 60.9 %all-to-all-start = ((bf16[64,8,16,128]{3,2,1,0:T(8,128)(2,1)}), bf16[64,8,16,128]{3,2,1,0:T(8,128)(2,1)S(1)}, u32[]{:S(2)}, u32[]{:S(2)}) async-start(bf16[64,8,16,128]{3,2,1,0:T(8,128)(2,1)} %bitcast.6), calls=%async_computation | async-start | bytes 4194304 | tf_op jit(solution)/shard_map/all_to_all | solution.py:287
  18.9 11.5 %collective-permute-start = (bf16[2,128,512]{2,1,0:T(8,128)(2,1)}, bf16[2,128,512]{2,1,0:T(8,128)(2,1)S(1)}, u32[]{:S(2)}, u32[]{:S(2)}) collective-permute-start(bf16[2,128,512]{2,1,0:T(8,128)(2,1)} %fusion), channel_id=1, source_target_pairs={{0,6},{66,64},{132,130},{198,196},{1,7},{67,65},{133,131},{199,197... | collective-permute-start | bytes 786440 | tf_op jit(solution)/shard_map/ppermute | solution.py:298
  19.5 16.3 %collective-permute-start.1 = (bf16[2,128,512]{2,1,0:T(8,128)(2,1)}, bf16[2,128,512]{2,1,0:T(8,128)(2,1)}, u32[]{:S(2)}, u32[]{:S(2)}) collective-permute-start(bf16[2,128,512]{2,1,0:T(8,128)(2,1)} %fusion), channel_id=1, source_target_pairs={{0,4},{66,70},{132,128},{198,194},{1,5},{67,71},{133,129},{199,195... | collective-permute-start | bytes 786440 | tf_op jit(solution)/shard_map/ppermute | solution.py:298
  20.8 15.0 %collective-permute-start.2 = (bf16[2,128,512]{2,1,0:T(8,128)(2,1)}, bf16[2,128,512]{2,1,0:T(8,128)(2,1)}, u32[]{:S(2)}, u32[]{:S(2)}) collective-permute-start(bf16[2,128,512]{2,1,0:T(8,128)(2,1)} %fusion), channel_id=1, source_target_pairs={{0,2},{66,68},{132,134},{198,192},{1,3},{67,69},{133,135},{199,193... | collective-permute-start | bytes 786440 | tf_op jit(solution)/shard_map/ppermute | solution.py:298
  24.9 26.3 %collective-permute-start.3 = (bf16[4,64,1024]{2,1,0:T(8,128)(2,1)}, bf16[4,64,1024]{2,1,0:T(8,128)(2,1)S(1)}, u32[]{:S(2)}, u32[]{:S(2)}) collective-permute-start(bf16[4,64,1024]{2,1,0:T(8,128)(2,1)} %get-tuple-element.102), channel_id=1, source_target_pairs={{0,2},{2,4},{4,6},{6,0},{1,3},{3,5},{5,7},{7,1},{8,10},{10,12},{12... | collective-permute-start | bytes 1572872 | tf_op jit(solution)/shard_map/ppermute | solution.py:291
  26.1 25.2 %collective-permute-start.4 = (bf16[4,64,1024]{2,1,0:T(8,128)(2,1)}, bf16[4,64,1024]{2,1,0:T(8,128)(2,1)}, u32[]{:S(2)}, u32[]{:S(2)}) collective-permute-start(bf16[4,64,1024]{2,1,0:T(8,128)(2,1)} %get-tuple-element.104), channel_id=1, source_target_pairs={{0,4},{2,6},{4,0},{6,2},{1,5},{3,7},{5,1},{7,3},{8,12},{10,14},{12... | collective-permute-start | bytes 1572872 | tf_op jit(solution)/shard_map/ppermute | solution.py:291
  30.4 27.0 %collective-permute-start.5 = (bf16[4,64,1024]{2,1,0:T(8,128)(2,1)}, bf16[4,64,1024]{2,1,0:T(8,128)(2,1)}, u32[]{:S(2)}, u32[]{:S(2)}) collective-permute-start(bf16[4,64,1024]{2,1,0:T(8,128)(2,1)} %get-tuple-element.101), channel_id=1, source_target_pairs={{0,6},{2,0},{4,2},{6,4},{1,7},{3,1},{5,3},{7,5},{8,14},{10,8},{12,... | collective-permute-start | bytes 1572872 | tf_op jit(solution)/shard_map/ppermute | solution.py:291
  37.0 1.7 copy-start.26
  37.1 1.7 collective-permute-start.6
  37.2 8.2 %collective-permute-start.7 = (bf16[1,128,512]{2,1,0:T(8,128)(2,1)S(1)}, bf16[1,128,512]{2,1,0:T(8,128)(2,1)S(1)}, u32[]{:S(2)}, u32[]{:S(2)}) collective-permute-start(bf16[1,128,512]{2,1,0:T(8,128)(2,1)S(1)} %slice.16.refs_0_), channel_id=1, source_target_pairs={{0,16},{8,24},{16,0},{24,8},{32,48},{40,56},{48,32},{56,40},{1,17}... | collective-permute-start | bytes 393224 | tf_op jit(solution)/shard_map/ppermute | solution.py:302
  38.7 10.5 %collective-permute-start.8 = (bf16[1,128,512]{2,1,0:T(8,128)(2,1)S(1)}, bf16[1,128,512]{2,1,0:T(8,128)(2,1)}, u32[]{:S(2)}, u32[]{:S(2)}) collective-permute-start(bf16[1,128,512]{2,1,0:T(8,128)(2,1)S(1)} %slice.16.refs_0_), channel_id=1, source_target_pairs={{0,24},{8,16},{16,8},{24,0},{32,56},{40,48},{48,40},{56,32},{1,25}... | collective-permute-start | bytes 393224 | tf_op jit(solution)/shard_map/ppermute | solution.py:302
  50.4 0.8 copy-start.8
  59.0 1.3 copy-start.4
  67.5 1.3 copy-start.1
  68.9 6.5 %copy-start.9 = (bf16[512,512]{1,0:T(8,128)(2,1)S(1)}, bf16[512,512]{1,0:T(8,128)(2,1)}, u32[]{:S(2)}) copy-start(bf16[512,512]{1,0:T(8,128)(2,1)} %copy-done.8) | copy-start | bytes 1572868
  68.9 65.8 %all-to-all-start.1 = ((bf16[8,16,64,128]{3,2,1,0:T(8,128)(2,1)}), bf16[8,16,64,128]{3,2,1,0:T(8,128)(2,1)S(1)}, u32[]{:S(2)}, u32[]{:S(2)}) async-start(bf16[8,16,64,128]{3,2,1,0:T(8,128)(2,1)} %bitcast.19), calls=%async_computation.1 | async-start | bytes 4194304 | tf_op jit(solution)/shard_map/all_to_all | solution.py:308
  75.4 1.6 copy-start.2
  77.0 25.6 %copy-start.27 = (bf16[2,128,512]{2,1,0:T(8,128)(2,1)S(1)}, bf16[2,128,512]{2,1,0:T(8,128)(2,1)}, u32[]{:S(2)}) copy-start(bf16[2,128,512]{2,1,0:T(8,128)(2,1)} %copy-done.26) | copy-start | bytes 786436
  80.9 13.6 %collective-permute-start.18 = (bf16[4,4,4,16,128]{4,3,2,1,0:T(8,128)(2,1)S(1)}, bf16[4,4,4,16,128]{4,3,2,1,0:T(8,128)(2,1)S(1)}, u32[]{:S(2)}, u32[]{:S(2)}) collective-permute-start(bf16[4,4,4,16,128]{4,3,2,1,0:T(8,128)(2,1)S(1)} %get-tuple-element.65), channel_id=1, source_target_pairs={{0,48},{8,56},{16,0},{24,8},{32,16},{40,24},{48,32},{56,40},{1,49}... | collective-permute-start | bytes 786440 | tf_op jit(solution)/shard_map/ppermute | solution.py:317
  82.1 12.4 %collective-permute-start.19 = (bf16[4,4,4,16,128]{4,3,2,1,0:T(8,128)(2,1)S(1)}, bf16[4,4,4,16,128]{4,3,2,1,0:T(8,128)(2,1)S(1)}, u32[]{:S(2)}, u32[]{:S(2)}) collective-permute-start(bf16[4,4,4,16,128]{4,3,2,1,0:T(8,128)(2,1)S(1)} %get-tuple-element.66), channel_id=1, source_target_pairs={{0,24},{8,32},{16,40},{24,48},{32,56},{40,0},{48,8},{56,16},{1,25}... | collective-permute-start | bytes 786440 | tf_op jit(solution)/shard_map/ppermute | solution.py:317
  82.1 15.1 %collective-permute-start.20 = (bf16[4,4,4,16,128]{4,3,2,1,0:T(8,128)(2,1)S(1)}, bf16[4,4,4,16,128]{4,3,2,1,0:T(8,128)(2,1)S(1)}, u32[]{:S(2)}, u32[]{:S(2)}) collective-permute-start(bf16[4,4,4,16,128]{4,3,2,1,0:T(8,128)(2,1)S(1)} %get-tuple-element.67), channel_id=1, source_target_pairs={{0,40},{8,48},{16,56},{24,0},{32,8},{40,16},{48,24},{56,32},{1,41}... | collective-permute-start | bytes 786440 | tf_op jit(solution)/shard_map/ppermute | solution.py:317
  85.4 15.8 %collective-permute-start.21 = (bf16[4,4,4,16,128]{4,3,2,1,0:T(8,128)(2,1)S(1)}, bf16[4,4,4,16,128]{4,3,2,1,0:T(8,128)(2,1)S(1)}, u32[]{:S(2)}, u32[]{:S(2)}) collective-permute-start(bf16[4,4,4,16,128]{4,3,2,1,0:T(8,128)(2,1)S(1)} %get-tuple-element.68), channel_id=1, source_target_pairs={{0,32},{8,40},{16,48},{24,56},{32,0},{40,8},{48,16},{56,24},{1,33}... | collective-permute-start | bytes 786440 | tf_op jit(solution)/shard_map/ppermute | solution.py:317
  87.2 17.7 %collective-permute-start.12 = (bf16[4,4,4,16,128]{4,3,2,1,0:T(8,128)(2,1)S(1)}, bf16[4,4,4,16,128]{4,3,2,1,0:T(8,128)(2,1)S(1)}, u32[]{:S(2)}, u32[]{:S(2)}) collective-permute-start(bf16[4,4,4,16,128]{4,3,2,1,0:T(8,128)(2,1)S(1)} %get-tuple-element.58), channel_id=1, source_target_pairs={{0,8},{8,16},{16,24},{24,32},{32,40},{40,48},{48,56},{56,0},{1,9},... | collective-permute-start | bytes 786440 | tf_op jit(solution)/shard_map/ppermute | solution.py:317
  94.5 11.2 %collective-permute-start.13 = (bf16[4,4,4,16,128]{4,3,2,1,0:T(8,128)(2,1)S(1)}, bf16[4,4,4,16,128]{4,3,2,1,0:T(8,128)(2,1)S(1)}, u32[]{:S(2)}, u32[]{:S(2)}) collective-permute-start(bf16[4,4,4,16,128]{4,3,2,1,0:T(8,128)(2,1)S(1)} %get-tuple-element.59), channel_id=1, source_target_pairs={{0,56},{8,0},{16,8},{24,16},{32,24},{40,32},{48,40},{56,48},{1,57}... | collective-permute-start | bytes 786440 | tf_op jit(solution)/shard_map/ppermute | solution.py:317
  94.5 11.9 %collective-permute-start.14 = (bf16[4,4,4,16,128]{4,3,2,1,0:T(8,128)(2,1)S(1)}, bf16[4,4,4,16,128]{4,3,2,1,0:T(8,128)(2,1)S(1)}, u32[]{:S(2)}, u32[]{:S(2)}) collective-permute-start(bf16[4,4,4,16,128]{4,3,2,1,0:T(8,128)(2,1)S(1)} %get-tuple-element.60), channel_id=1, source_target_pairs={{0,16},{8,24},{16,32},{24,40},{32,48},{40,56},{48,0},{56,8},{1,17}... | collective-permute-start | bytes 786440 | tf_op jit(solution)/shard_map/ppermute | solution.py:317
  101.8 13.9 %collective-permute-start.22 = (bf16[4,4,4,16,128]{4,3,2,1,0:T(8,128)(2,1)S(1)}, bf16[4,4,4,16,128]{4,3,2,1,0:T(8,128)(2,1)S(1)}, u32[]{:S(2)}, u32[]{:S(2)}) collective-permute-start(bf16[4,4,4,16,128]{4,3,2,1,0:T(8,128)(2,1)S(1)} %get-tuple-element.70), channel_id=1, source_target_pairs={{0,2},{2,4},{4,6},{6,0},{1,3},{3,5},{5,7},{7,1},{8,10},{10,12},{12... | collective-permute-start | bytes 786440 | tf_op jit(solution)/shard_map/ppermute | solution.py:319
  102.6 6.4 %collective-permute-start.10 = (bf16[1,128,512]{2,1,0:T(8,128)(2,1)S(1)}, bf16[1,128,512]{2,1,0:T(8,128)(2,1)S(1)}, u32[]{:S(2)}, u32[]{:S(2)}) collective-permute-start(bf16[1,128,512]{2,1,0:T(8,128)(2,1)S(1)} %slice.13.refs_0_), channel_id=1, source_target_pairs={{0,16},{8,24},{16,0},{24,8},{32,48},{40,56},{48,32},{56,40},{1,17}... | collective-permute-start | bytes 393224 | tf_op jit(solution)/shard_map/ppermute | solution.py:302
  104.9 7.2 %collective-permute-start.11 = (bf16[1,128,512]{2,1,0:T(8,128)(2,1)S(1)}, bf16[1,128,512]{2,1,0:T(8,128)(2,1)S(1)}, u32[]{:S(2)}, u32[]{:S(2)}) collective-permute-start(bf16[1,128,512]{2,1,0:T(8,128)(2,1)S(1)} %slice.13.refs_0_), channel_id=1, source_target_pairs={{0,24},{8,16},{16,8},{24,0},{32,56},{40,48},{48,40},{56,32},{1,25}... | collective-permute-start | bytes 393224 | tf_op jit(solution)/shard_map/ppermute | solution.py:302
  105.7 7.9 %collective-permute-start.9 = (bf16[1,128,512]{2,1,0:T(8,128)(2,1)S(1)}, bf16[1,128,512]{2,1,0:T(8,128)(2,1)S(1)}, u32[]{:S(2)}, u32[]{:S(2)}) collective-permute-start(bf16[1,128,512]{2,1,0:T(8,128)(2,1)S(1)} %slice.13.refs_0_), channel_id=1, source_target_pairs={{0,8},{8,0},{16,24},{24,16},{32,40},{40,32},{48,56},{56,48},{1,9},... | collective-permute-start | bytes 393224 | tf_op jit(solution)/shard_map/ppermute | solution.py:302
  106.4 10.4 %collective-permute-start.23 = (bf16[4,4,4,16,128]{4,3,2,1,0:T(8,128)(2,1)S(1)}, bf16[4,4,4,16,128]{4,3,2,1,0:T(8,128)(2,1)S(1)}, u32[]{:S(2)}, u32[]{:S(2)}) collective-permute-start(bf16[4,4,4,16,128]{4,3,2,1,0:T(8,128)(2,1)S(1)} %get-tuple-element.71), channel_id=1, source_target_pairs={{0,4},{2,6},{4,0},{6,2},{1,5},{3,7},{5,1},{7,3},{8,12},{10,14},{12... | collective-permute-start | bytes 786440 | tf_op jit(solution)/shard_map/ppermute | solution.py:319
  108.8 18.9 %copy-start.14 = (bf16[4,4,4,16,128]{4,3,2,1,0:T(8,128)(2,1)}, bf16[4,4,4,16,128]{4,3,2,1,0:T(8,128)(2,1)S(1)}, u32[]{:S(2)}) copy-start(bf16[4,4,4,16,128]{4,3,2,1,0:T(8,128)(2,1)S(1)} %get-tuple-element.75.refs_0_) | copy-start | bytes 786436
  109.0 14.5 %collective-permute-start.24 = (bf16[4,4,4,16,128]{4,3,2,1,0:T(8,128)(2,1)S(1)}, bf16[4,4,4,16,128]{4,3,2,1,0:T(8,128)(2,1)S(1)}, u32[]{:S(2)}, u32[]{:S(2)}) collective-permute-start(bf16[4,4,4,16,128]{4,3,2,1,0:T(8,128)(2,1)S(1)} %get-tuple-element.72), channel_id=1, source_target_pairs={{0,6},{2,0},{4,2},{6,4},{1,7},{3,1},{5,3},{7,5},{8,14},{10,8},{12,... | collective-permute-start | bytes 786440 | tf_op jit(solution)/shard_map/ppermute | solution.py:319
  112.1 12.1 %collective-permute-start.15 = (bf16[4,4,4,16,128]{4,3,2,1,0:T(8,128)(2,1)S(1)}, bf16[4,4,4,16,128]{4,3,2,1,0:T(8,128)(2,1)S(1)}, u32[]{:S(2)}, u32[]{:S(2)}) collective-permute-start(bf16[4,4,4,16,128]{4,3,2,1,0:T(8,128)(2,1)S(1)} %get-tuple-element.62), channel_id=1, source_target_pairs={{0,2},{2,4},{4,6},{6,0},{1,3},{3,5},{5,7},{7,1},{8,10},{10,12},{12... | collective-permute-start | bytes 786440 | tf_op jit(solution)/shard_map/ppermute | solution.py:319
  113.6 14.1 %collective-permute-start.16 = (bf16[4,4,4,16,128]{4,3,2,1,0:T(8,128)(2,1)S(1)}, bf16[4,4,4,16,128]{4,3,2,1,0:T(8,128)(2,1)S(1)}, u32[]{:S(2)}, u32[]{:S(2)}) collective-permute-start(bf16[4,4,4,16,128]{4,3,2,1,0:T(8,128)(2,1)S(1)} %get-tuple-element.63), channel_id=1, source_target_pairs={{0,4},{2,6},{4,0},{6,2},{1,5},{3,7},{5,1},{7,3},{8,12},{10,14},{12... | collective-permute-start | bytes 786440 | tf_op jit(solution)/shard_map/ppermute | solution.py:319
  115.7 12.0 %copy-start.10 = (bf16[4,4,4,16,128]{4,3,2,1,0:T(8,128)(2,1)}, bf16[4,4,4,16,128]{4,3,2,1,0:T(8,128)(2,1)S(1)}, u32[]{:S(2)}) copy-start(bf16[4,4,4,16,128]{4,3,2,1,0:T(8,128)(2,1)S(1)} %collective-permute-done.22.refs_5_) | copy-start | bytes 786436
  115.7 18.2 %collective-permute-start.17 = (bf16[4,4,4,16,128]{4,3,2,1,0:T(8,128)(2,1)S(1)}, bf16[4,4,4,16,128]{4,3,2,1,0:T(8,128)(2,1)S(1)}, u32[]{:S(2)}, u32[]{:S(2)}) collective-permute-start(bf16[4,4,4,16,128]{4,3,2,1,0:T(8,128)(2,1)S(1)} %get-tuple-element.64), channel_id=1, source_target_pairs={{0,6},{2,0},{4,2},{6,4},{1,7},{3,1},{5,3},{7,5},{8,14},{10,8},{12,... | collective-permute-start | bytes 786440 | tf_op jit(solution)/shard_map/ppermute | solution.py:319
  124.1 0.7 copy-start.18
  127.7 0.7 copy-start.20
  133.9 0.7 copy-start.22
  138.4 1.4 copy-start
  139.7 6.5 %copy-start.11 = (bf16[4,4,4,16,128]{4,3,2,1,0:T(8,128)(2,1)S(1)}, bf16[4,4,4,16,128]{4,3,2,1,0:T(8,128)(2,1)}, u32[]{:S(2)}) copy-start(bf16[4,4,4,16,128]{4,3,2,1,0:T(8,128)(2,1)} %copy-done.10) | copy-start | bytes 786436
  139.7 6.5 %copy-start.13 = (bf16[4,4,4,16,128]{4,3,2,1,0:T(8,128)(2,1)S(1)}, bf16[4,4,4,16,128]{4,3,2,1,0:T(8,128)(2,1)}, u32[]{:S(2)}) copy-start(bf16[4,4,4,16,128]{4,3,2,1,0:T(8,128)(2,1)} %copy-done.12) | copy-start | bytes 786436
  139.8 32.3 %all-to-all-start.2 = ((bf16[32,16,16,128]{3,2,1,0:T(8,128)(2,1)}), bf16[32,16,16,128]{3,2,1,0:T(8,128)(2,1)}, u32[]{:S(2)}, u32[]{:S(2)}) async-start(bf16[32,16,16,128]{3,2,1,0:T(8,128)(2,1)} %bitcast.16), calls=%async_computation.2 | async-start | bytes 4194304 | tf_op jit(solution)/shard_map/all_to_all | solution.py:327
  146.2 1.0 copy-start.15
  147.2 0.9 copy-start.17
  148.1 0.9 copy-start.19
  149.1 0.9 copy-start.21
  150.0 0.9 copy-start.23
  153.3 1.4 copy-start.6
  172.1 68.9 %all-to-all-start.3 = ((bf16[32,4,64,128]{3,2,1,0:T(8,128)(2,1)}), bf16[32,4,64,128]{3,2,1,0:T(8,128)(2,1)}, u32[]{:S(2)}, u32[]{:S(2)}) async-start(bf16[32,4,64,128]{3,2,1,0:T(8,128)(2,1)} %bitcast.20), calls=%async_computation.3 | async-start | bytes 4194304 | tf_op jit(solution)/shard_map/all_to_all | solution.py:333
  182.7 1.6 copy-start.7
  184.3 4.2 %copy-start.3 = (bf16[64,8,16,128]{3,2,1,0:T(8,128)(2,1)S(1)}, bf16[64,8,16,128]{3,2,1,0:T(8,128)(2,1)}, u32[]{:S(2)}) copy-start(bf16[64,8,16,128]{3,2,1,0:T(8,128)(2,1)} %copy-done.1) | copy-start | bytes 6291460
  188.4 7.1 %collective-permute-start.25 = (f32[4,4,16,512]{3,2,1,0:T(8,128)S(1)}, f32[4,4,16,512]{3,2,1,0:T(8,128)S(1)}, u32[]{:S(2)}, u32[]{:S(2)}) collective-permute-start(f32[4,4,16,512]{3,2,1,0:T(8,128)S(1)} %get-tuple-element.87), channel_id=1, source_target_pairs={{0,8},{8,0},{1,9},{9,1},{2,10},{10,2},{3,11},{11,3},{4,12},{12,4},... | collective-permute-start | bytes 1572872 | tf_op jit(solution)/shard_map/ppermute | solution.py:340
  194.8 2.2 collective-permute-start.26
  197.7 15.5 %collective-permute-start.27 = (f32[4,2,16,512]{3,2,1,0:T(8,128)S(1)}, f32[4,2,16,512]{3,2,1,0:T(8,128)S(1)}, u32[]{:S(2)}, u32[]{:S(2)}) collective-permute-start(f32[4,2,16,512]{3,2,1,0:T(8,128)S(1)} %get-tuple-element.92), channel_id=1, source_target_pairs={{0,16},{16,32},{32,48},{48,0},{1,17},{17,33},{33,49},{49,1},{2,18}... | collective-permute-start | bytes 786440 | tf_op jit(solution)/shard_map/ppermute | solution.py:344
  198.3 14.9 %collective-permute-start.28 = (f32[4,2,16,512]{3,2,1,0:T(8,128)S(1)}, f32[4,2,16,512]{3,2,1,0:T(8,128)S(1)}, u32[]{:S(2)}, u32[]{:S(2)}) collective-permute-start(f32[4,2,16,512]{3,2,1,0:T(8,128)S(1)} %get-tuple-element.93), channel_id=1, source_target_pairs={{0,32},{16,48},{32,0},{48,16},{1,33},{17,49},{33,1},{49,17},{2,34}... | collective-permute-start | bytes 786440 | tf_op jit(solution)/shard_map/ppermute | solution.py:344
  200.0 13.7 %collective-permute-start.29 = (f32[4,2,16,512]{3,2,1,0:T(8,128)S(1)}, f32[4,2,16,512]{3,2,1,0:T(8,128)S(1)}, u32[]{:S(2)}, u32[]{:S(2)}) collective-permute-start(f32[4,2,16,512]{3,2,1,0:T(8,128)S(1)} %get-tuple-element.94), channel_id=1, source_target_pairs={{0,48},{16,0},{32,16},{48,32},{1,49},{17,1},{33,17},{49,33},{2,50}... | collective-permute-start | bytes 786440 | tf_op jit(solution)/shard_map/ppermute | solution.py:344
  214.4 4.6 %collective-permute-start.30 = (f32[2,16,512]{2,1,0:T(8,128)S(1)}, f32[2,16,512]{2,1,0:T(8,128)S(1)}, u32[]{:S(2)}, u32[]{:S(2)}) collective-permute-start(f32[2,16,512]{2,1,0:T(8,128)S(1)} %get-tuple-element.96), channel_id=1, source_target_pairs={{0,2},{2,4},{4,6},{6,0},{1,3},{3,5},{5,7},{7,1},{8,10},{10,12},{12... | collective-permute-start | bytes 196616 | tf_op jit(solution)/shard_map/ppermute | solution.py:346
  215.0 12.3 %collective-permute-start.31 = (f32[2,16,512]{2,1,0:T(8,128)S(1)}, f32[2,16,512]{2,1,0:T(8,128)S(1)}, u32[]{:S(2)}, u32[]{:S(2)}) collective-permute-start(f32[2,16,512]{2,1,0:T(8,128)S(1)} %get-tuple-element.97), channel_id=1, source_target_pairs={{0,4},{2,6},{4,0},{6,2},{1,5},{3,7},{5,1},{7,3},{8,12},{10,14},{12... | collective-permute-start | bytes 196616 | tf_op jit(solution)/shard_map/ppermute | solution.py:346
  217.4 9.9 %collective-permute-start.32 = (f32[2,16,512]{2,1,0:T(8,128)S(1)}, f32[2,16,512]{2,1,0:T(8,128)S(1)}, u32[]{:S(2)}, u32[]{:S(2)}) collective-permute-start(f32[2,16,512]{2,1,0:T(8,128)S(1)} %get-tuple-element.98), channel_id=1, source_target_pairs={{0,6},{2,0},{4,2},{6,4},{1,7},{3,1},{5,3},{7,5},{8,14},{10,8},{12,... | collective-permute-start | bytes 196616 | tf_op jit(solution)/shard_map/ppermute | solution.py:346
  228.5 12.5 %collective-permute-start.33 = (f32[2,16,512]{2,1,0:T(8,128)S(1)}, f32[2,16,512]{2,1,0:T(8,128)S(1)}, u32[]{:S(2)}, u32[]{:S(2)}) collective-permute-start(f32[2,16,512]{2,1,0:T(8,128)S(1)} %shard_map.89), channel_id=1, source_target_pairs={{0,0},{2,64},{4,128},{6,192},{64,2},{66,66},{68,130},{70,194},{128... | collective-permute-start | bytes 196616 | tf_op jit(solution)/shard_map/ppermute | solution.py:348
  (2 other events, 1.4 us)

commit v4 on v3

--- a/solution.py
+++ b/solution.py
@@ -38,11 +38,12 @@
     return jax.ShapeDtypeStruct(dims, dtype)
 
 
-def gate_kernel(gate, up, out):
+def gate_kernel(gate, up, out, swap):
     for k in range(8):
         lanes = slice(k * SLAB, (k + 1) * SLAB)
-        prod = gate[:, :, lanes].astype(F32) * up[:, :, lanes].astype(F32)
-        out[k // 2, :, k % 2] = jnp.swapaxes(prod, 0, 1).astype(BF).reshape(2, 8, 16, SLAB)
+        for r in range(16):
+            swap[k, pl.ds(r, 16, stride=16), :] = gate[r, :, lanes].astype(F32) * up[r, :, lanes].astype(F32)
+        out[k // 2, :, k % 2] = swap[k].astype(BF).reshape(2, 8, 16, SLAB)
 
 
 def gate_call(gate, up):
@@ -52,6 +53,7 @@
         out_shape=shape(4, 8, 2, 8, 16, SLAB),
         in_specs=[pl.BlockSpec((16, 16, 1024), lambda c: (0, c, 0))] * 2,
         out_specs=pl.BlockSpec((4, 2, 2, 8, 16, SLAB), lambda c: (0, c, 0, 0, 0, 0)),
+        scratch_shapes=[pltpu.VMEM((8, 256, SLAB), F32)],
         compiler_params=PARAMS,
         cost_estimate=pl.CostEstimate(flops=1 << 20, bytes_accessed=6 << 20, transcendentals=0),
     )(gate, up)
@@ -83,28 +85,15 @@
     f1tp[...] = ordered.T.astype(BF)
 
 
-def bring(g, flat, sem):
-    copies = [
-        pltpu.make_async_copy(
-            g.at[:, :, k // 8, k % 8], flat.at[:, :, :, pl.ds(k * SLAB, SLAB)], sem.at[k]
-        )
-        for k in range(16)
-    ]
-    for copy in copies:
-        copy.start()
-    return copies
-
-
 def second_apply_kernel(pos, f2t, g, *refs):
-    outs, flat, swap, sem = refs[:8], refs[8], refs[9], refs[10]
-    for copy in bring(g, flat, sem):
-        copy.wait()
+    outs, flat, swap = refs[:8], refs[8], refs[9]
+    for k in range(16):
+        flat[:, k * SLAB : (k + 1) * SLAB] = g[:, :, k // 8, k % 8].reshape(ROWS, SLAB)
 
     def body(zh, _):
         rows = pl.ds(pl.multiple_of(zh * 128, 128), 128)
         for k in range(0, 16, 2):
-            right = flat[:, :, :, k * SLAB : (k + 2) * SLAB].reshape(ROWS, 2 * SLAB)
-            part = jnp.dot(f2t[rows, :], right, preferred_element_type=F32)
+            part = jnp.dot(f2t[rows, :], flat[:, k * SLAB : (k + 2) * SLAB], preferred_element_type=F32)
             swap[pl.ds(k, 128, stride=16), :] = part[:, :SLAB]
             swap[pl.ds(k + 1, 128, stride=16), :] = part[:, SLAB:]
         for t, out in enumerate(outs):
@@ -217,17 +206,14 @@
             put((give, keep))
 
 
-def second_kernel(pos, g, mixed, keep, give, flat, mixw, sem):
+def second_kernel(pos, flat, mixed, keep, give, mixw):
     core = pos[5]
-    copies = bring(g, flat, sem)
     for k in range(16):
         lanes = slice(k * SLAB, (k + 1) * SLAB)
         mixw[:, lanes] = mixed[:, :, k // 8, k % 8].reshape(ROWS, SLAB)
-    for copy in copies:
-        copy.wait()
     for zh in range(4):
         part = lax.dot_general(
-            flat[zh].reshape(128, 16 * SLAB), mixw[...], (((1,), (1,)), ((), ())), preferred_element_type=F32
+            flat[zh * 128 : (zh + 1) * 128, :], mixw[...], (((1,), (1,)), ((), ())), preferred_element_type=F32
         )
 
         def put(keep, give):
@@ -280,7 +266,6 @@
     four, eight = shifts(4), shifts(8)
     wide = pltpu.VMEM((ROWS, 16 * SLAB), BF)
     swap = pltpu.VMEM((128 * 16, SLAB), F32)
-    cols, dma = pltpu.VMEM((4, 8, 16, 16 * SLAB), BF), pltpu.SemaphoreType.DMA((16,))
     f32 = functools.partial(shape, dtype=F32)
 
     gated = gate_call(gate, upstream)
@@ -309,9 +294,13 @@
     f1, f1tp = call(first_factor_kernel, [shape(COLS, COLS)] * 2, [full], n_in=4, moved=1 << 20)(
         pos, *gathered(got[:1])
     )
-    mg = call(second_apply_kernel, [shape(4, 4, 4, 16, SLAB)] * 8, [cols, swap, dma], n_in=2, hbm=(1,), flops=1 << 30)(
-        pos, f2t, grad
-    )
+    *mg, flat = call(
+        second_apply_kernel,
+        [shape(4, 4, 4, 16, SLAB)] * 8 + [shape(ROWS, 16 * SLAB)],
+        [swap],
+        n_in=2,
+        flops=1 << 30,
+    )(pos, f2t, grad)
     crossed = []
     for steps in (NEAR, FAR):
         group = [mg[t] if t == 0 else lax.ppermute(mg[t], ("y", "core"), eight(t)) for t in steps]
@@ -322,20 +311,18 @@
 
     stage = pltpu.VMEM((4, 8, 2, 8, 16, SLAB), BF)
     mixed = call(
-        mix_kernel, shape(8, 4, 2, 8, 16, SLAB), [wide, swap, stage, dma], n_in=2, hbm=("out",), flops=1 << 30
+        mix_kernel, shape(8, 4, 2, 8, 16, SLAB), [wide, swap, stage, pltpu.SemaphoreType.DMA((4,))], n_in=2, hbm=("out",), flops=1 << 30
     )(pos, f1, tok)
     mixed = lax.all_to_all(mixed.reshape(32, 16, 16, SLAB), PLANE, 0, 0, tiled=True).reshape(8, 4, 2, 8, 16, SLAB)
     sent, mgw = call(
         first_apply_kernel, [shape(4, 4, 2, 4, 64, SLAB), shape(COLS, 16 * SLAB)], n_in=9, flops=1 << 30
     )(pos, f1tp, *mg)
-    mixed, sent = lax.optimization_barrier((mixed, sent))
+    halves = [f32(4, 4, 16, 512)] * 2
+    first = call(first_kernel, halves, [wide], n_in=2, flops=1 << 30)(pos, mgw, tok)
+    mixed, sent, (first_keep, first_give) = lax.optimization_barrier((mixed, sent, first))
 
     home = lax.all_to_all(sent.reshape(32, 4, 64, SLAB), ZX, 0, 0, tiled=True)
-    halves = [f32(4, 4, 16, 512)] * 2
-    second_keep, second_give = call(second_kernel, halves, [cols, wide, dma], n_in=2, hbm=(0,), flops=1 << 30)(
-        pos, grad, mixed
-    )
-    first_keep, first_give = call(first_kernel, halves, [wide], n_in=2, flops=1 << 30)(pos, mgw, tok)
+    second_keep, second_give = call(second_kernel, halves, [wide], n_in=2, flops=1 << 30)(pos, flat, mixed)
     other = [(0, 1), (1, 0)]
     first_came, second_came = lax.ppermute(first_give, "core", other), lax.ppermute(second_give, "core", other)
     sums = call(core_sum_kernel, [f32(4, 2, 16, 512)] * 4, n_in=4)(
@@ -346,14 +333,14 @@
     sums = [sums[0]] + [lax.ppermute(sums[s], "x", four(s)) for s in range(1, 4)]
     sums = call(sum_kernel, f32(2, 16, 512), n_in=4, moved=1 << 19)(pos, *sums)
     sums = lax.ppermute(sums, ("zh", "x"), [(a * 4 + b, b * 4 + a) for a in range(4) for b in range(4)])
-    home, sums = lax.optimization_barrier((home, sums))
+    home, first_grad, second_grad = lax.optimization_barrier((home, sums[:1], sums[1:]))
     token_grad = call(
         grad_join_kernel,
         shape(16, 64, 1024),
         [pltpu.VMEM((16, 64, 1024), BF), pltpu.SemaphoreType.DMA((4, 8)), pltpu.SemaphoreType.DMA((4,))],
         hbm=(0, "out"),
     )(pos, home.reshape(4, 4, 2, 4, 64, SLAB))
-    return token_grad, sums[:1], sums[1:]
+    return token_grad, first_grad, second_grad
 
 
 def solution(mesh):

time: 246 us -> 240 us (0.976)
  waiting for transfers between devices: 107 us -> 100 us
    all_to_all x1, waiting for transfers between devices: 17.4 us -> 11.9 us  [local(): lax.all_to_all(mixed.reshape(32, 16, 16, SLAB), PLANE, 0, 0, tiled=True)]
    ppermute x3, waiting for transfers between devices: 9.92 us -> 6.19 us  [local(): lax.ppermute(sums[s], 'x', four(s))]
    unnamed x56 -> x50, local copies, waits for them, and re-layouts: 19.2 us -> 18.5 us
  transfers between devices with their start and end apart: 38 -> 38, of which waited for: 21 -> 23; matrix products, arithmetic and copies ran while one was open for 2% -> 2% of each run, Pallas kernels for 10% -> 9%
where the time goes in v4:
time: 240 us; the launch traced here: 237 us
  waiting for transfers between devices  100 us (42%)
  starting transfers between devices  78.8 us (33%)
  Pallas kernels  33.1 us (14%)
  local copies, waits for them, and re-layouts  21.9 us (9%)
    unnamed x50, local copies, waits for them, and re-layouts  18.5 us
    ppermute x6, waiting for transfers between devices, local(): lax.ppermute(group[s], 'x', four(s))  14.3 us
    ppermute x7, waiting for transfers between devices, local(): lax.ppermute(mg[t], ('y', 'core'), eight(t))  13.8 us
    all_to_all x1, waiting for transfers between devices, local(): lax.all_to_all(mixed.reshape(32, 16, 16, SLAB), PLANE, 0, 0, tiled=True)  11.9 us
    ppermute x3, waiting for transfers between devices, local(): lax.ppermute(sums[t], 'y', four(t))  11.8 us
    all_to_all x1, starting transfers between devices, local(): lax.all_to_all(gated.reshape(64, 8, 16, SLAB), ZYC, 0, 0, tiled=True)  11.6 us
    ppermute x6, waiting for transfers between devices, gathered(): lax.ppermute(own, ('y', 'core'), [(k, k ^ s) for k in range(8)])  11 us
    all_to_all x1, starting transfers between devices, local(): home = lax.all_to_all(sent.reshape(32, 4, 64, SLAB), ZX, 0, 0, tiled=True)  10.7 us
  transfers between devices with their start and end apart: 38, of which 23 were waited for; matrix products, arithmetic and copies ran while one was open for 2% of the time, Pallas kernels for 9%

profile of v4, /device:TPU:70, one launch (start us, length us, event | category | flops | bytes accessed | tf_op | source)
XLA Modules:
  0.0 236.8 jit_solution(7568877486214829004)
XLA Ops:
  0.6 1.6 copy-done.2
  2.2 4.7 %shard_map.77 = bf16[4,8,2,8,16,128]{5,4,3,2,1,0:T(8,128)(2,1)} custom-call(bf16[16,64,1024]{2,1,0:T(8,128)(2,1)S(1)} %copy-done.2, bf16[16,64,1024]{2,1,0:T(8,128)(2,1)} %up.1), custom_call_target="tpu_custom_call" | custom-call | flops 1048576 | bytes 6291456 | tf_op jit(solution)/shard_map/pallas_call | solution.py:50
  6.9 11.6 %all-to-all-start = ((bf16[64,8,16,128]{3,2,1,0:T(8,128)(2,1)}), bf16[64,8,16,128]{3,2,1,0:T(8,128)(2,1)}, u32[]{:S(2)}, u32[]{:S(2)}) async-start(bf16[64,8,16,128]{3,2,1,0:T(8,128)(2,1)} %bitcast.6), calls=%async_computation | async-start | bytes 4194304 | tf_op jit(solution)/shard_map/all_to_all | solution.py:272
  20.0 1.3 collective-permute-start.1
  21.3 1.4 collective-permute-start.2
  22.7 2.7 %constant_dynamic-slice_fusion = (bf16[4,64,1024]{2,1,0:T(8,128)(2,1)}, bf16[4,64,1024]{2,1,0:T(8,128)(2,1)}, bf16[4,64,1024]{2,1,0:T(8,128)(2,1)S(1)}, bf16[4,64,1024]{2,1,0:T(8,128)(2,1)}) fusion(bf16[16,64,1024]{2,1,0:T(8,128)(2,1)} %param.5, s32[]{:T(128)S(6)} %select_n.88, s32[]{:T(128)S(6)} %select_n.84, s32[]{:T(128)S(6)} %select_n.82, s32[]{:T(128)S(6)} %select_n.86), kind=kLoop, calls=%fused_computation.4 | loop fusion | bytes 4194320 | tf_op jit(solution)/shard_map/dynamic_slice | solution.py:275
  25.4 1.2 collective-permute-start.3
  26.5 4.3 %collective-permute-start.4 = (bf16[4,64,1024]{2,1,0:T(8,128)(2,1)}, bf16[4,64,1024]{2,1,0:T(8,128)(2,1)S(1)}, u32[]{:S(2)}, u32[]{:S(2)}) collective-permute-start(bf16[4,64,1024]{2,1,0:T(8,128)(2,1)} %get-tuple-element.112), channel_id=1, source_target_pairs={{0,4},{2,6},{4,0},{6,2},{1,5},{3,7},{5,1},{7,3},{8,12},{10,14},{12... | collective-permute-start | bytes 1572872 | tf_op jit(solution)/shard_map/ppermute | solution.py:276
  30.8 1.4 collective-permute-start.5
  32.3 4.0 %collective-permute-done.1 = bf16[2,128,512]{2,1,0:T(8,128)(2,1)} collective-permute-done((bf16[2,128,512]{2,1,0:T(8,128)(2,1)}, bf16[2,128,512]{2,1,0:T(8,128)(2,1)}, u32[]{:S(2)}, u32[]{:S(2)}) %collective-permute-start.1) | collective-permute-done | bytes 262176 | tf_op jit(solution)/shard_map/ppermute | solution.py:283
  36.3 1.1 select_select_fusion
  37.5 1.6 collective-permute-start.7
  39.1 1.0 collective-permute-start.8
  40.1 5.5 %collective-permute-done.7.refs_2_ = bf16[1,128,512]{2,1,0:T(8,128)(2,1)S(1)} collective-permute-done((bf16[1,128,512]{2,1,0:T(8,128)(2,1)S(1)}, bf16[1,128,512]{2,1,0:T(8,128)(2,1)S(1)}, u32[]{:S(2)}, u32[]{:S(2)}) %collective-permute-start.7) | collective-permute-done | bytes 131104 | tf_op jit(solution)/shard_map/ppermute | solution.py:287
  45.6 3.8 %collective-permute-done.8.refs_3_ = bf16[1,128,512]{2,1,0:T(8,128)(2,1)S(1)} collective-permute-done((bf16[1,128,512]{2,1,0:T(8,128)(2,1)S(1)}, bf16[1,128,512]{2,1,0:T(8,128)(2,1)S(1)}, u32[]{:S(2)}, u32[]{:S(2)}) %collective-permute-start.8) | collective-permute-done | bytes 131104 | tf_op jit(solution)/shard_map/ppermute | solution.py:287
  50.3 7.4 %collective-permute-done.5.x3 = bf16[4,64,1024]{2,1,0:T(8,128)(2,1)S(1)} collective-permute-done((bf16[4,64,1024]{2,1,0:T(8,128)(2,1)}, bf16[4,64,1024]{2,1,0:T(8,128)(2,1)S(1)}, u32[]{:S(2)}, u32[]{:S(2)}) %collective-permute-start.5) | collective-permute-done | bytes 524320 | tf_op jit(solution)/shard_map/ppermute | solution.py:276
  58.7 1.4 copy-done.1
  60.0 7.9 %all-to-all-done = bf16[64,8,16,128]{3,2,1,0:T(8,128)(2,1)} async-done(((bf16[64,8,16,128]{3,2,1,0:T(8,128)(2,1)}), bf16[64,8,16,128]{3,2,1,0:T(8,128)(2,1)}, u32[]{:S(2)}, u32[]{:S(2)}) %all-to-all-start) | async-done | bytes 2097184 | tf_op jit(solution)/shard_map/all_to_all | solution.py:272
  67.9 6.4 %all-to-all-start.1 = ((bf16[8,16,64,128]{3,2,1,0:T(8,128)(2,1)}), bf16[8,16,64,128]{3,2,1,0:T(8,128)(2,1)S(1)}, u32[]{:S(2)}, u32[]{:S(2)}) async-start(bf16[8,16,64,128]{3,2,1,0:T(8,128)(2,1)} %bitcast.17), calls=%async_computation.1 | async-start | bytes 4194304 | tf_op jit(solution)/shard_map/all_to_all | solution.py:293
  74.3 4.7 %shard_map.80 = (bf16[4,4,4,16,128]{4,3,2,1,0:T(8,128)(2,1)S(1)}, bf16[4,4,4,16,128]{4,3,2,1,0:T(8,128)(2,1)S(1)}, bf16[4,4,4,16,128]{4,3,2,1,0:T(8,128)(2,1)S(1...) custom-call(s32[6]{0:T(128)S(1)} %stack.27.pos, ...), custom_call_target="tpu_custom_call" | custom-call | flops 1073741824 | bytes 4194304 | tf_op jit(solution)/shard_map/pallas_call | solution.py:297
  79.0 1.3 copy-done.3
  80.3 1.1 collective-permute-start.18
  81.5 3.2 %collective-permute-start.20 = (bf16[4,4,4,16,128]{4,3,2,1,0:T(8,128)(2,1)S(1)}, bf16[4,4,4,16,128]{4,3,2,1,0:T(8,128)(2,1)S(1)}, u32[]{:S(2)}, u32[]{:S(2)}) collective-permute-start(bf16[4,4,4,16,128]{4,3,2,1,0:T(8,128)(2,1)S(1)} %get-tuple-element.71), channel_id=1, source_target_pairs={{0,40},{8,48},{16,56},{24,0},{32,8},{40,16},{48,24},{56,32},{1,41}... | collective-permute-start | bytes 786440 | tf_op jit(solution)/shard_map/ppermute | solution.py:306
  84.7 1.8 collective-permute-start.21
  86.5 7.3 %collective-permute-done.18.a = bf16[4,4,4,16,128]{4,3,2,1,0:T(8,128)(2,1)S(1)} collective-permute-done((bf16[4,4,4,16,128]{4,3,2,1,0:T(8,128)(2,1)S(1)}, bf16[4,4,4,16,128]{4,3,2,1,0:T(8,128)(2,1)S(1)}, u32[]{:S(2)}, u32[]{:S(2)}) %collective-permute-start.18) | collective-permute-done | bytes 262176 | tf_op jit(solution)/shard_map/ppermute | solution.py:306
  94.7 1.8 collective-permute-done.20.c
  96.5 4.0 %collective-permute-done.21.d = bf16[4,4,4,16,128]{4,3,2,1,0:T(8,128)(2,1)S(1)} collective-permute-done((bf16[4,4,4,16,128]{4,3,2,1,0:T(8,128)(2,1)S(1)}, bf16[4,4,4,16,128]{4,3,2,1,0:T(8,128)(2,1)S(1)}, u32[]{:S(2)}, u32[]{:S(2)}) %collective-permute-start.21) | collective-permute-done | bytes 262176 | tf_op jit(solution)/shard_map/ppermute | solution.py:306
  102.0 2.3 collective-permute-start.10
  105.8 1.8 collective-permute-start.23
  108.3 1.5 collective-permute-start.24
  109.9 1.5 collective-permute-done.11.refs_3_
  111.4 1.5 collective-permute-start.15
  112.9 2.1 collective-permute-start.16
  116.8 5.9 %collective-permute-done.24.refs_7_ = bf16[4,4,4,16,128]{4,3,2,1,0:T(8,128)(2,1)S(1)} collective-permute-done((bf16[4,4,4,16,128]{4,3,2,1,0:T(8,128)(2,1)S(1)}, bf16[4,4,4,16,128]{4,3,2,1,0:T(8,128)(2,1)S(1)}, u32[]{:S(2)}, u32[]{:S(2)}) %collective-permute-start.24) | collective-permute-done | bytes 262176 | tf_op jit(solution)/shard_map/ppermute | solution.py:308
  124.2 2.8 %collective-permute-done.16.refs_2_ = bf16[4,4,4,16,128]{4,3,2,1,0:T(8,128)(2,1)S(1)} collective-permute-done((bf16[4,4,4,16,128]{4,3,2,1,0:T(8,128)(2,1)S(1)}, bf16[4,4,4,16,128]{4,3,2,1,0:T(8,128)(2,1)S(1)}, u32[]{:S(2)}, u32[]{:S(2)}) %collective-permute-start.16) | collective-permute-done | bytes 262176 | tf_op jit(solution)/shard_map/ppermute | solution.py:308
  127.7 5.5 %collective-permute-done.17.refs_3_ = bf16[4,4,4,16,128]{4,3,2,1,0:T(8,128)(2,1)S(1)} collective-permute-done((bf16[4,4,4,16,128]{4,3,2,1,0:T(8,128)(2,1)S(1)}, bf16[4,4,4,16,128]{4,3,2,1,0:T(8,128)(2,1)S(1)}, u32[]{:S(2)}, u32[]{:S(2)}) %collective-permute-start.17) | collective-permute-done | bytes 262176 | tf_op jit(solution)/shard_map/ppermute | solution.py:308
  134.0 3.5 %shard_map.83 = bf16[8,4,2,8,16,128]{5,4,3,2,1,0:T(8,128)(2,1)S(1)} custom-call(s32[6]{0:T(128)S(1)} %stack.27.pos, bf16[512,512]{1,0:T(8,128)(2,1)S(1)} %get-tuple-element.57.f1, bf16[4,2,4,4,64,128]{5,4,3,2,1,0:T(8,128)(2,1)S(1)} %bitcast.14), custom_call_target="tpu_custom_call" | custom-call | flops 1073741824 | bytes 4194304 | tf_op jit(solution)/shard_map/pallas_call | solution.py:313
  137.5 1.3 copy-done
  138.9 6.4 %all-to-all-start.2 = ((bf16[32,16,16,128]{3,2,1,0:T(8,128)(2,1)}), bf16[32,16,16,128]{3,2,1,0:T(8,128)(2,1)}, u32[]{:S(2)}, u32[]{:S(2)}) async-start(bf16[32,16,16,128]{3,2,1,0:T(8,128)(2,1)} %bitcast.16), calls=%async_computation.2 | async-start | bytes 4194304 | tf_op jit(solution)/shard_map/all_to_all | solution.py:316
  145.3 0.9 copy-done.12
  146.3 0.9 copy-done.14
  147.2 0.9 copy-done.16
  148.2 0.9 copy-done.18
  149.1 0.9 copy-done.20
  150.1 2.2 shard_map.84
  152.3 1.4 copy-done.5
  153.8 1.6 copy-done.6
  155.3 3.9 %shard_map.85 = (f32[4,4,16,512]{3,2,1,0:T(8,128)S(1)}, f32[4,4,16,512]{3,2,1,0:T(8,128)S(1)}) custom-call(s32[6]{0:T(128)S(1)} %stack.27.pos, bf16[512,2048]{1,0:T(8,128)(2,1)S(1)} %copy-done.6, bf16[4,2,4,4,64,128]{5,4,3,2,1,0:T(8,128)(2,1)S(1)} %bitcast.15), custom_call_target="tpu_custom_call" | custom-call | flops 1073741824 | bytes 4194304 | tf_op jit(solution)/shard_map/pallas_call | solution.py:321
  159.3 11.9 %all-to-all-done.2 = bf16[32,16,16,128]{3,2,1,0:T(8,128)(2,1)} async-done(((bf16[32,16,16,128]{3,2,1,0:T(8,128)(2,1)}), bf16[32,16,16,128]{3,2,1,0:T(8,128)(2,1)}, u32[]{:S(2)}, u32[]{:S(2)}) %all-to-all-start.2) | async-done | bytes 2097184 | tf_op jit(solution)/shard_map/all_to_all | solution.py:316
  171.2 10.7 %all-to-all-start.3 = ((bf16[32,4,64,128]{3,2,1,0:T(8,128)(2,1)}), bf16[32,4,64,128]{3,2,1,0:T(8,128)(2,1)S(1)}, u32[]{:S(2)}, u32[]{:S(2)}) async-start(bf16[32,4,64,128]{3,2,1,0:T(8,128)(2,1)} %bitcast.19), calls=%async_computation.3 | async-start | bytes 4194304 | tf_op jit(solution)/shard_map/all_to_all | solution.py:324
  181.9 1.6 copy-done.4
  183.5 5.0 %shard_map.86 = (f32[4,4,16,512]{3,2,1,0:T(8,128)S(1)}, f32[4,4,16,512]{3,2,1,0:T(8,128)S(1)}) custom-call(s32[6]{0:T(128)S(1)} %stack.27.pos, bf16[512,2048]{1,0:T(8,128)(2,1)S(1)} %copy-done.4, bf16[8,4,2,8,16,128]{5,4,3,2,1,0:T(8,128)(2,1)} %bitcast.11.mixed), custom_call_target="tpu_custom_call" | custom-call | flops 1073741824 | bytes 4194304 | tf_op jit(solution)/shard_map/pallas_call | solution.py:325
  189.1 1.4 collective-permute-done.26.so
  192.6 1.7 collective-permute-start.28
  194.3 1.7 collective-permute-start.29
  196.0 11.2 %collective-permute-done.27.b = f32[4,2,16,512]{3,2,1,0:T(8,128)S(1)} collective-permute-done((f32[4,2,16,512]{3,2,1,0:T(8,128)S(1)}, f32[4,2,16,512]{3,2,1,0:T(8,128)S(1)}, u32[]{:S(2)}, u32[]{:S(2)}) %collective-permute-start.27) | collective-permute-done | bytes 262176 | tf_op jit(solution)/shard_map/ppermute | solution.py:331
  209.0 2.4 collective-permute-start.31
  211.4 2.6 %collective-permute-done.30.b = f32[2,16,512]{2,1,0:T(8,128)S(1)} collective-permute-done((f32[2,16,512]{2,1,0:T(8,128)S(1)}, f32[2,16,512]{2,1,0:T(8,128)S(1)}, u32[]{:S(2)}, u32[]{:S(2)}) %collective-permute-start.30) | collective-permute-done | bytes 65568 | tf_op jit(solution)/shard_map/ppermute | solution.py:333
  214.0 1.1 collective-permute-done.31.c
  215.1 2.5 %collective-permute-done.32.d = f32[2,16,512]{2,1,0:T(8,128)S(1)} collective-permute-done((f32[2,16,512]{2,1,0:T(8,128)S(1)}, f32[2,16,512]{2,1,0:T(8,128)S(1)}, u32[]{:S(2)}, u32[]{:S(2)}) %collective-permute-start.32) | collective-permute-done | bytes 65568 | tf_op jit(solution)/shard_map/ppermute | solution.py:333
  217.6 1.2 shard_map.89
  218.8 4.9 %collective-permute-start.33 = (f32[2,16,512]{2,1,0:T(8,128)S(1)}, f32[2,16,512]{2,1,0:T(8,128)S(1)}, u32[]{:S(2)}, u32[]{:S(2)}) collective-permute-start(f32[2,16,512]{2,1,0:T(8,128)S(1)} %shard_map.89), channel_id=1, source_target_pairs={{0,0},{2,64},{4,128},{6,192},{64,2},{66,66},{68,130},{70,194},{128... | collective-permute-start | bytes 196616 | tf_op jit(solution)/shard_map/ppermute | solution.py:335
  223.7 9.5 %collective-permute-done.33 = f32[2,16,512]{2,1,0:T(8,128)S(1)} collective-permute-done((f32[2,16,512]{2,1,0:T(8,128)S(1)}, f32[2,16,512]{2,1,0:T(8,128)S(1)}, u32[]{:S(2)}, u32[]{:S(2)}) %collective-permute-start.33) | collective-permute-done | bytes 65568 | tf_op jit(solution)/shard_map/ppermute | solution.py:335
  233.9 2.8 %shard_map.90 = bf16[16,64,1024]{2,1,0:T(8,128)(2,1)} custom-call(s32[6]{0:T(128)S(1)} %stack.27.pos, bf16[4,4,2,4,64,128]{5,4,3,2,1,0:T(8,128)(2,1)S(1)} %bitcast.18), custom_call_target="tpu_custom_call" | custom-call | bytes 4194304 | tf_op jit(solution)/shard_map/pallas_call | solution.py:337
  (84 shorter events, 17.6 us)
Async XLA Ops:
  0.6 1.6 copy-start.2
  6.9 11.7 %copy-start.21 = (bf16[1,512,512]{2,1,0:T(8,128)(2,1)S(1)}, bf16[1,512,512]{2,1,0:T(8,128)(2,1)}, u32[]{:S(2)}) copy-start(bf16[1,512,512]{2,1,0:T(8,128)(2,1)} %param.8) | copy-start | bytes 1572868
  6.9 11.7 %copy-start.22 = (bf16[1,512,512]{2,1,0:T(8,128)(2,1)S(1)}, bf16[1,512,512]{2,1,0:T(8,128)(2,1)}, u32[]{:S(2)}) copy-start(bf16[1,512,512]{2,1,0:T(8,128)(2,1)} %param.9) | copy-start | bytes 1572868
  6.9 61.0 %all-to-all-start = ((bf16[64,8,16,128]{3,2,1,0:T(8,128)(2,1)}), bf16[64,8,16,128]{3,2,1,0:T(8,128)(2,1)}, u32[]{:S(2)}, u32[]{:S(2)}) async-start(bf16[64,8,16,128]{3,2,1,0:T(8,128)(2,1)} %bitcast.6), calls=%async_computation | async-start | bytes 4194304 | tf_op jit(solution)/shard_map/all_to_all | solution.py:272
  19.3 11.5 %collective-permute-start = (bf16[2,128,512]{2,1,0:T(8,128)(2,1)}, bf16[2,128,512]{2,1,0:T(8,128)(2,1)S(1)}, u32[]{:S(2)}, u32[]{:S(2)}) collective-permute-start(bf16[2,128,512]{2,1,0:T(8,128)(2,1)} %fusion), channel_id=1, source_target_pairs={{0,6},{66,64},{132,130},{198,196},{1,7},{67,65},{133,131},{199,197... | collective-permute-start | bytes 786440 | tf_op jit(solution)/shard_map/ppermute | solution.py:283
  20.0 16.3 %collective-permute-start.1 = (bf16[2,128,512]{2,1,0:T(8,128)(2,1)}, bf16[2,128,512]{2,1,0:T(8,128)(2,1)}, u32[]{:S(2)}, u32[]{:S(2)}) collective-permute-start(bf16[2,128,512]{2,1,0:T(8,128)(2,1)} %fusion), channel_id=1, source_target_pairs={{0,4},{66,70},{132,128},{198,194},{1,5},{67,71},{133,129},{199,195... | collective-permute-start | bytes 786440 | tf_op jit(solution)/shard_map/ppermute | solution.py:283
  21.3 15.0 %collective-permute-start.2 = (bf16[2,128,512]{2,1,0:T(8,128)(2,1)}, bf16[2,128,512]{2,1,0:T(8,128)(2,1)}, u32[]{:S(2)}, u32[]{:S(2)}) collective-permute-start(bf16[2,128,512]{2,1,0:T(8,128)(2,1)} %fusion), channel_id=1, source_target_pairs={{0,2},{66,68},{132,134},{198,192},{1,3},{67,69},{133,135},{199,193... | collective-permute-start | bytes 786440 | tf_op jit(solution)/shard_map/ppermute | solution.py:283
  25.4 24.9 %collective-permute-start.3 = (bf16[4,64,1024]{2,1,0:T(8,128)(2,1)}, bf16[4,64,1024]{2,1,0:T(8,128)(2,1)S(1)}, u32[]{:S(2)}, u32[]{:S(2)}) collective-permute-start(bf16[4,64,1024]{2,1,0:T(8,128)(2,1)} %get-tuple-element.110), channel_id=1, source_target_pairs={{0,2},{2,4},{4,6},{6,0},{1,3},{3,5},{5,7},{7,1},{8,10},{10,12},{12... | collective-permute-start | bytes 1572872 | tf_op jit(solution)/shard_map/ppermute | solution.py:276
  26.5 23.8 %collective-permute-start.4 = (bf16[4,64,1024]{2,1,0:T(8,128)(2,1)}, bf16[4,64,1024]{2,1,0:T(8,128)(2,1)S(1)}, u32[]{:S(2)}, u32[]{:S(2)}) collective-permute-start(bf16[4,64,1024]{2,1,0:T(8,128)(2,1)} %get-tuple-element.112), channel_id=1, source_target_pairs={{0,4},{2,6},{4,0},{6,2},{1,5},{3,7},{5,1},{7,3},{8,12},{10,14},{12... | collective-permute-start | bytes 1572872 | tf_op jit(solution)/shard_map/ppermute | solution.py:276
  30.8 26.9 %collective-permute-start.5 = (bf16[4,64,1024]{2,1,0:T(8,128)(2,1)}, bf16[4,64,1024]{2,1,0:T(8,128)(2,1)S(1)}, u32[]{:S(2)}, u32[]{:S(2)}) collective-permute-start(bf16[4,64,1024]{2,1,0:T(8,128)(2,1)} %get-tuple-element.109), channel_id=1, source_target_pairs={{0,6},{2,0},{4,2},{6,4},{1,7},{3,1},{5,3},{7,5},{8,14},{10,8},{12,... | collective-permute-start | bytes 1572872 | tf_op jit(solution)/shard_map/ppermute | solution.py:276
  37.4 1.7 copy-start.23
  37.4 1.7 collective-permute-start.6
  37.5 8.1 %collective-permute-start.7 = (bf16[1,128,512]{2,1,0:T(8,128)(2,1)S(1)}, bf16[1,128,512]{2,1,0:T(8,128)(2,1)S(1)}, u32[]{:S(2)}, u32[]{:S(2)}) collective-permute-start(bf16[1,128,512]{2,1,0:T(8,128)(2,1)S(1)} %slice.16.refs_0_), channel_id=1, source_target_pairs={{0,16},{8,24},{16,0},{24,8},{32,48},{40,56},{48,32},{56,40},{1,17}... | collective-permute-start | bytes 393224 | tf_op jit(solution)/shard_map/ppermute | solution.py:287
  39.1 10.4 %collective-permute-start.8 = (bf16[1,128,512]{2,1,0:T(8,128)(2,1)S(1)}, bf16[1,128,512]{2,1,0:T(8,128)(2,1)S(1)}, u32[]{:S(2)}, u32[]{:S(2)}) collective-permute-start(bf16[1,128,512]{2,1,0:T(8,128)(2,1)S(1)} %slice.16.refs_0_), channel_id=1, source_target_pairs={{0,24},{8,16},{16,8},{24,0},{32,56},{40,48},{48,40},{56,32},{1,25}... | collective-permute-start | bytes 393224 | tf_op jit(solution)/shard_map/ppermute | solution.py:287
  58.7 1.4 copy-start.1
  67.9 66.1 %all-to-all-start.1 = ((bf16[8,16,64,128]{3,2,1,0:T(8,128)(2,1)}), bf16[8,16,64,128]{3,2,1,0:T(8,128)(2,1)S(1)}, u32[]{:S(2)}, u32[]{:S(2)}) async-start(bf16[8,16,64,128]{3,2,1,0:T(8,128)(2,1)} %bitcast.17), calls=%async_computation.1 | async-start | bytes 4194304 | tf_op jit(solution)/shard_map/all_to_all | solution.py:293
  74.3 27.7 %copy-start.24 = (bf16[2,128,512]{2,1,0:T(8,128)(2,1)S(1)}, bf16[2,128,512]{2,1,0:T(8,128)(2,1)}, u32[]{:S(2)}) copy-start(bf16[2,128,512]{2,1,0:T(8,128)(2,1)} %copy-done.23) | copy-start | bytes 786436
  79.0 1.3 copy-start.3
  80.3 13.5 %collective-permute-start.18 = (bf16[4,4,4,16,128]{4,3,2,1,0:T(8,128)(2,1)S(1)}, bf16[4,4,4,16,128]{4,3,2,1,0:T(8,128)(2,1)S(1)}, u32[]{:S(2)}, u32[]{:S(2)}) collective-permute-start(bf16[4,4,4,16,128]{4,3,2,1,0:T(8,128)(2,1)S(1)} %get-tuple-element.69), channel_id=1, source_target_pairs={{0,48},{8,56},{16,0},{24,8},{32,16},{40,24},{48,32},{56,40},{1,49}... | collective-permute-start | bytes 786440 | tf_op jit(solution)/shard_map/ppermute | solution.py:306
  81.5 12.4 %collective-permute-start.19 = (bf16[4,4,4,16,128]{4,3,2,1,0:T(8,128)(2,1)S(1)}, bf16[4,4,4,16,128]{4,3,2,1,0:T(8,128)(2,1)S(1)}, u32[]{:S(2)}, u32[]{:S(2)}) collective-permute-start(bf16[4,4,4,16,128]{4,3,2,1,0:T(8,128)(2,1)S(1)} %get-tuple-element.70), channel_id=1, source_target_pairs={{0,24},{8,32},{16,40},{24,48},{32,56},{40,0},{48,8},{56,16},{1,25}... | collective-permute-start | bytes 786440 | tf_op jit(solution)/shard_map/ppermute | solution.py:306
  81.5 15.1 %collective-permute-start.20 = (bf16[4,4,4,16,128]{4,3,2,1,0:T(8,128)(2,1)S(1)}, bf16[4,4,4,16,128]{4,3,2,1,0:T(8,128)(2,1)S(1)}, u32[]{:S(2)}, u32[]{:S(2)}) collective-permute-start(bf16[4,4,4,16,128]{4,3,2,1,0:T(8,128)(2,1)S(1)} %get-tuple-element.71), channel_id=1, source_target_pairs={{0,40},{8,48},{16,56},{24,0},{32,8},{40,16},{48,24},{56,32},{1,41}... | collective-permute-start | bytes 786440 | tf_op jit(solution)/shard_map/ppermute | solution.py:306
  84.7 15.9 %collective-permute-start.21 = (bf16[4,4,4,16,128]{4,3,2,1,0:T(8,128)(2,1)S(1)}, bf16[4,4,4,16,128]{4,3,2,1,0:T(8,128)(2,1)S(1)}, u32[]{:S(2)}, u32[]{:S(2)}) collective-permute-start(bf16[4,4,4,16,128]{4,3,2,1,0:T(8,128)(2,1)S(1)} %get-tuple-element.72), channel_id=1, source_target_pairs={{0,32},{8,40},{16,48},{24,56},{32,0},{40,8},{48,16},{56,24},{1,33}... | collective-permute-start | bytes 786440 | tf_op jit(solution)/shard_map/ppermute | solution.py:306
  86.5 17.7 %collective-permute-start.12 = (bf16[4,4,4,16,128]{4,3,2,1,0:T(8,128)(2,1)S(1)}, bf16[4,4,4,16,128]{4,3,2,1,0:T(8,128)(2,1)S(1)}, u32[]{:S(2)}, u32[]{:S(2)}) collective-permute-start(bf16[4,4,4,16,128]{4,3,2,1,0:T(8,128)(2,1)S(1)} %get-tuple-element.62), channel_id=1, source_target_pairs={{0,8},{8,16},{16,24},{24,32},{32,40},{40,48},{48,56},{56,0},{1,9},... | collective-permute-start | bytes 786440 | tf_op jit(solution)/shard_map/ppermute | solution.py:306
  93.8 11.2 %collective-permute-start.13 = (bf16[4,4,4,16,128]{4,3,2,1,0:T(8,128)(2,1)S(1)}, bf16[4,4,4,16,128]{4,3,2,1,0:T(8,128)(2,1)S(1)}, u32[]{:S(2)}, u32[]{:S(2)}) collective-permute-start(bf16[4,4,4,16,128]{4,3,2,1,0:T(8,128)(2,1)S(1)} %get-tuple-element.63), channel_id=1, source_target_pairs={{0,56},{8,0},{16,8},{24,16},{32,24},{40,32},{48,40},{56,48},{1,57}... | collective-permute-start | bytes 786440 | tf_op jit(solution)/shard_map/ppermute | solution.py:306
  93.9 11.9 %collective-permute-start.14 = (bf16[4,4,4,16,128]{4,3,2,1,0:T(8,128)(2,1)S(1)}, bf16[4,4,4,16,128]{4,3,2,1,0:T(8,128)(2,1)S(1)}, u32[]{:S(2)}, u32[]{:S(2)}) collective-permute-start(bf16[4,4,4,16,128]{4,3,2,1,0:T(8,128)(2,1)S(1)} %get-tuple-element.64), channel_id=1, source_target_pairs={{0,16},{8,24},{16,32},{24,40},{32,48},{40,56},{48,0},{56,8},{1,17}... | collective-permute-start | bytes 786440 | tf_op jit(solution)/shard_map/ppermute | solution.py:306
  101.2 13.9 %collective-permute-start.22 = (bf16[4,4,4,16,128]{4,3,2,1,0:T(8,128)(2,1)S(1)}, bf16[4,4,4,16,128]{4,3,2,1,0:T(8,128)(2,1)S(1)}, u32[]{:S(2)}, u32[]{:S(2)}) collective-permute-start(bf16[4,4,4,16,128]{4,3,2,1,0:T(8,128)(2,1)S(1)} %get-tuple-element.74), channel_id=1, source_target_pairs={{0,2},{2,4},{4,6},{6,0},{1,3},{3,5},{5,7},{7,1},{8,10},{10,12},{12... | collective-permute-start | bytes 786440 | tf_op jit(solution)/shard_map/ppermute | solution.py:308
  102.0 6.4 %collective-permute-start.10 = (bf16[1,128,512]{2,1,0:T(8,128)(2,1)S(1)}, bf16[1,128,512]{2,1,0:T(8,128)(2,1)S(1)}, u32[]{:S(2)}, u32[]{:S(2)}) collective-permute-start(bf16[1,128,512]{2,1,0:T(8,128)(2,1)S(1)} %slice.13.refs_0_), channel_id=1, source_target_pairs={{0,16},{8,24},{16,0},{24,8},{32,48},{40,56},{48,32},{56,40},{1,17}... | collective-permute-start | bytes 393224 | tf_op jit(solution)/shard_map/ppermute | solution.py:287
  104.3 7.2 %collective-permute-start.11 = (bf16[1,128,512]{2,1,0:T(8,128)(2,1)S(1)}, bf16[1,128,512]{2,1,0:T(8,128)(2,1)S(1)}, u32[]{:S(2)}, u32[]{:S(2)}) collective-permute-start(bf16[1,128,512]{2,1,0:T(8,128)(2,1)S(1)} %slice.13.refs_0_), channel_id=1, source_target_pairs={{0,24},{8,16},{16,8},{24,0},{32,56},{40,48},{48,40},{56,32},{1,25}... | collective-permute-start | bytes 393224 | tf_op jit(solution)/shard_map/ppermute | solution.py:287
  105.0 7.9 %collective-permute-start.9 = (bf16[1,128,512]{2,1,0:T(8,128)(2,1)S(1)}, bf16[1,128,512]{2,1,0:T(8,128)(2,1)S(1)}, u32[]{:S(2)}, u32[]{:S(2)}) collective-permute-start(bf16[1,128,512]{2,1,0:T(8,128)(2,1)S(1)} %slice.13.refs_0_), channel_id=1, source_target_pairs={{0,8},{8,0},{16,24},{24,16},{32,40},{40,32},{48,56},{56,48},{1,9},... | collective-permute-start | bytes 393224 | tf_op jit(solution)/shard_map/ppermute | solution.py:287
  105.8 10.3 %collective-permute-start.23 = (bf16[4,4,4,16,128]{4,3,2,1,0:T(8,128)(2,1)S(1)}, bf16[4,4,4,16,128]{4,3,2,1,0:T(8,128)(2,1)S(1)}, u32[]{:S(2)}, u32[]{:S(2)}) collective-permute-start(bf16[4,4,4,16,128]{4,3,2,1,0:T(8,128)(2,1)S(1)} %get-tuple-element.75), channel_id=1, source_target_pairs={{0,4},{2,6},{4,0},{6,2},{1,5},{3,7},{5,1},{7,3},{8,12},{10,14},{12... | collective-permute-start | bytes 786440 | tf_op jit(solution)/shard_map/ppermute | solution.py:308
  108.2 18.9 %copy-start.11 = (bf16[4,4,4,16,128]{4,3,2,1,0:T(8,128)(2,1)}, bf16[4,4,4,16,128]{4,3,2,1,0:T(8,128)(2,1)S(1)}, u32[]{:S(2)}) copy-start(bf16[4,4,4,16,128]{4,3,2,1,0:T(8,128)(2,1)S(1)} %get-tuple-element.79.refs_0_) | copy-start | bytes 786436
  108.3 14.4 %collective-permute-start.24 = (bf16[4,4,4,16,128]{4,3,2,1,0:T(8,128)(2,1)S(1)}, bf16[4,4,4,16,128]{4,3,2,1,0:T(8,128)(2,1)S(1)}, u32[]{:S(2)}, u32[]{:S(2)}) collective-permute-start(bf16[4,4,4,16,128]{4,3,2,1,0:T(8,128)(2,1)S(1)} %get-tuple-element.76), channel_id=1, source_target_pairs={{0,6},{2,0},{4,2},{6,4},{1,7},{3,1},{5,3},{7,5},{8,14},{10,8},{12,... | collective-permute-start | bytes 786440 | tf_op jit(solution)/shard_map/ppermute | solution.py:308
  111.4 12.1 %collective-permute-start.15 = (bf16[4,4,4,16,128]{4,3,2,1,0:T(8,128)(2,1)S(1)}, bf16[4,4,4,16,128]{4,3,2,1,0:T(8,128)(2,1)S(1)}, u32[]{:S(2)}, u32[]{:S(2)}) collective-permute-start(bf16[4,4,4,16,128]{4,3,2,1,0:T(8,128)(2,1)S(1)} %get-tuple-element.66), channel_id=1, source_target_pairs={{0,2},{2,4},{4,6},{6,0},{1,3},{3,5},{5,7},{7,1},{8,10},{10,12},{12... | collective-permute-start | bytes 786440 | tf_op jit(solution)/shard_map/ppermute | solution.py:308
  112.9 14.1 %collective-permute-start.16 = (bf16[4,4,4,16,128]{4,3,2,1,0:T(8,128)(2,1)S(1)}, bf16[4,4,4,16,128]{4,3,2,1,0:T(8,128)(2,1)S(1)}, u32[]{:S(2)}, u32[]{:S(2)}) collective-permute-start(bf16[4,4,4,16,128]{4,3,2,1,0:T(8,128)(2,1)S(1)} %get-tuple-element.67), channel_id=1, source_target_pairs={{0,4},{2,6},{4,0},{6,2},{1,5},{3,7},{5,1},{7,3},{8,12},{10,14},{12... | collective-permute-start | bytes 786440 | tf_op jit(solution)/shard_map/ppermute | solution.py:308
  115.1 12.0 %copy-start.7 = (bf16[4,4,4,16,128]{4,3,2,1,0:T(8,128)(2,1)}, bf16[4,4,4,16,128]{4,3,2,1,0:T(8,128)(2,1)S(1)}, u32[]{:S(2)}) copy-start(bf16[4,4,4,16,128]{4,3,2,1,0:T(8,128)(2,1)S(1)} %collective-permute-done.22.refs_5_) | copy-start | bytes 786436
  115.1 18.2 %collective-permute-start.17 = (bf16[4,4,4,16,128]{4,3,2,1,0:T(8,128)(2,1)S(1)}, bf16[4,4,4,16,128]{4,3,2,1,0:T(8,128)(2,1)S(1)}, u32[]{:S(2)}, u32[]{:S(2)}) collective-permute-start(bf16[4,4,4,16,128]{4,3,2,1,0:T(8,128)(2,1)S(1)} %get-tuple-element.68), channel_id=1, source_target_pairs={{0,6},{2,0},{4,2},{6,4},{1,7},{3,1},{5,3},{7,5},{8,14},{10,8},{12,... | collective-permute-start | bytes 786440 | tf_op jit(solution)/shard_map/ppermute | solution.py:308
  116.1 0.7 copy-start.9
  122.8 0.7 copy-start.13
  123.5 0.7 copy-start.15
  127.0 0.7 copy-start.17
  133.3 0.7 copy-start.19
  137.5 1.4 copy-start
  138.9 6.4 %copy-start.8 = (bf16[4,4,4,16,128]{4,3,2,1,0:T(8,128)(2,1)S(1)}, bf16[4,4,4,16,128]{4,3,2,1,0:T(8,128)(2,1)}, u32[]{:S(2)}) copy-start(bf16[4,4,4,16,128]{4,3,2,1,0:T(8,128)(2,1)} %copy-done.7) | copy-start | bytes 786436
  138.9 6.4 %copy-start.10 = (bf16[4,4,4,16,128]{4,3,2,1,0:T(8,128)(2,1)S(1)}, bf16[4,4,4,16,128]{4,3,2,1,0:T(8,128)(2,1)}, u32[]{:S(2)}) copy-start(bf16[4,4,4,16,128]{4,3,2,1,0:T(8,128)(2,1)} %copy-done.9) | copy-start | bytes 786436
  138.9 32.3 %all-to-all-start.2 = ((bf16[32,16,16,128]{3,2,1,0:T(8,128)(2,1)}), bf16[32,16,16,128]{3,2,1,0:T(8,128)(2,1)}, u32[]{:S(2)}, u32[]{:S(2)}) async-start(bf16[32,16,16,128]{3,2,1,0:T(8,128)(2,1)} %bitcast.16), calls=%async_computation.2 | async-start | bytes 4194304 | tf_op jit(solution)/shard_map/all_to_all | solution.py:316
  145.3 1.0 copy-start.12
  146.3 0.9 copy-start.14
  147.2 0.9 copy-start.16
  148.2 0.9 copy-start.18
  149.1 0.9 copy-start.20
  152.3 1.4 copy-start.5
  153.7 1.6 copy-start.6
  171.2 62.7 %all-to-all-start.3 = ((bf16[32,4,64,128]{3,2,1,0:T(8,128)(2,1)}), bf16[32,4,64,128]{3,2,1,0:T(8,128)(2,1)S(1)}, u32[]{:S(2)}, u32[]{:S(2)}) async-start(bf16[32,4,64,128]{3,2,1,0:T(8,128)(2,1)} %bitcast.19), calls=%async_computation.3 | async-start | bytes 4194304 | tf_op jit(solution)/shard_map/all_to_all | solution.py:324
  181.9 1.6 copy-start.4
  188.5 2.0 collective-permute-start.26
  188.6 2.6 %collective-permute-start.25 = (f32[4,4,16,512]{3,2,1,0:T(8,128)S(1)}, f32[4,4,16,512]{3,2,1,0:T(8,128)S(1)}, u32[]{:S(2)}, u32[]{:S(2)}) collective-permute-start(f32[4,4,16,512]{3,2,1,0:T(8,128)S(1)} %get-tuple-element.93), channel_id=1, source_target_pairs={{0,8},{8,0},{1,9},{9,1},{2,10},{10,2},{3,11},{11,3},{4,12},{12,4},... | collective-permute-start | bytes 1572872 | tf_op jit(solution)/shard_map/ppermute | solution.py:327
  191.9 15.3 %collective-permute-start.27 = (f32[4,2,16,512]{3,2,1,0:T(8,128)S(1)}, f32[4,2,16,512]{3,2,1,0:T(8,128)S(1)}, u32[]{:S(2)}, u32[]{:S(2)}) collective-permute-start(f32[4,2,16,512]{3,2,1,0:T(8,128)S(1)} %get-tuple-element.99), channel_id=1, source_target_pairs={{0,16},{16,32},{32,48},{48,0},{1,17},{17,33},{33,49},{49,1},{2,18}... | collective-permute-start | bytes 786440 | tf_op jit(solution)/shard_map/ppermute | solution.py:331
  192.6 14.6 %collective-permute-start.28 = (f32[4,2,16,512]{3,2,1,0:T(8,128)S(1)}, f32[4,2,16,512]{3,2,1,0:T(8,128)S(1)}, u32[]{:S(2)}, u32[]{:S(2)}) collective-permute-start(f32[4,2,16,512]{3,2,1,0:T(8,128)S(1)} %get-tuple-element.100), channel_id=1, source_target_pairs={{0,32},{16,48},{32,0},{48,16},{1,33},{17,49},{33,1},{49,17},{2,34}... | collective-permute-start | bytes 786440 | tf_op jit(solution)/shard_map/ppermute | solution.py:331
  194.3 13.5 %collective-permute-start.29 = (f32[4,2,16,512]{3,2,1,0:T(8,128)S(1)}, f32[4,2,16,512]{3,2,1,0:T(8,128)S(1)}, u32[]{:S(2)}, u32[]{:S(2)}) collective-permute-start(f32[4,2,16,512]{3,2,1,0:T(8,128)S(1)} %get-tuple-element.101), channel_id=1, source_target_pairs={{0,48},{16,0},{32,16},{48,32},{1,49},{17,1},{33,17},{49,33},{2,50}... | collective-permute-start | bytes 786440 | tf_op jit(solution)/shard_map/ppermute | solution.py:331
  208.4 5.6 %collective-permute-start.30 = (f32[2,16,512]{2,1,0:T(8,128)S(1)}, f32[2,16,512]{2,1,0:T(8,128)S(1)}, u32[]{:S(2)}, u32[]{:S(2)}) collective-permute-start(f32[2,16,512]{2,1,0:T(8,128)S(1)} %get-tuple-element.103), channel_id=1, source_target_pairs={{0,2},{2,4},{4,6},{6,0},{1,3},{3,5},{5,7},{7,1},{8,10},{10,12},{12... | collective-permute-start | bytes 196616 | tf_op jit(solution)/shard_map/ppermute | solution.py:333
  209.0 6.1 %collective-permute-start.31 = (f32[2,16,512]{2,1,0:T(8,128)S(1)}, f32[2,16,512]{2,1,0:T(8,128)S(1)}, u32[]{:S(2)}, u32[]{:S(2)}) collective-permute-start(f32[2,16,512]{2,1,0:T(8,128)S(1)} %get-tuple-element.104), channel_id=1, source_target_pairs={{0,4},{2,6},{4,0},{6,2},{1,5},{3,7},{5,1},{7,3},{8,12},{10,14},{12... | collective-permute-start | bytes 196616 | tf_op jit(solution)/shard_map/ppermute | solution.py:333
  211.4 6.2 %collective-permute-start.32 = (f32[2,16,512]{2,1,0:T(8,128)S(1)}, f32[2,16,512]{2,1,0:T(8,128)S(1)}, u32[]{:S(2)}, u32[]{:S(2)}) collective-permute-start(f32[2,16,512]{2,1,0:T(8,128)S(1)} %get-tuple-element.105), channel_id=1, source_target_pairs={{0,6},{2,0},{4,2},{6,4},{1,7},{3,1},{5,3},{7,5},{8,14},{10,8},{12,... | collective-permute-start | bytes 196616 | tf_op jit(solution)/shard_map/ppermute | solution.py:333
  218.8 14.4 %collective-permute-start.33 = (f32[2,16,512]{2,1,0:T(8,128)S(1)}, f32[2,16,512]{2,1,0:T(8,128)S(1)}, u32[]{:S(2)}, u32[]{:S(2)}) collective-permute-start(f32[2,16,512]{2,1,0:T(8,128)S(1)} %shard_map.89), channel_id=1, source_target_pairs={{0,0},{2,64},{4,128},{6,192},{64,2},{66,66},{68,130},{70,194},{128... | collective-permute-start | bytes 196616 | tf_op jit(solution)/shard_map/ppermute | solution.py:335

commit v5 on v4

--- a/solution.py
+++ b/solution.py
@@ -288,11 +288,12 @@
 
     full = pltpu.VMEM((COLS, COLS), F32)
     f2t = call(second_factor_kernel, shape(ROWS, ROWS), [full], n_in=4, moved=1 << 20)(pos, *gathered(got[1:]))
-    got, sent, grad, f2t = lax.optimization_barrier((got, sent, grad, f2t))
+    first_quarters = gathered(got[:1])
+    first_quarters, sent, grad, f2t = lax.optimization_barrier((first_quarters, sent, grad, f2t))
 
     tok = lax.all_to_all(sent.reshape(8, 16, 64, SLAB), ("zh", "zl"), 0, 0, tiled=True).reshape(4, 2, 4, 4, 64, SLAB)
     f1, f1tp = call(first_factor_kernel, [shape(COLS, COLS)] * 2, [full], n_in=4, moved=1 << 20)(
-        pos, *gathered(got[:1])
+        pos, *first_quarters
     )
     *mg, flat = call(
         second_apply_kernel,
@@ -311,7 +312,7 @@
 
     stage = pltpu.VMEM((4, 8, 2, 8, 16, SLAB), BF)
     mixed = call(
-        mix_kernel, shape(8, 4, 2, 8, 16, SLAB), [wide, swap, stage, pltpu.SemaphoreType.DMA((4,))], n_in=2, hbm=("out",), flops=1 << 30
+        mix_kernel, pltpu.HBM((8, 4, 2, 8, 16, SLAB), BF), [wide, swap, stage, pltpu.SemaphoreType.DMA((4,))], n_in=2, hbm=("out",), flops=1 << 30
     )(pos, f1, tok)
     mixed = lax.all_to_all(mixed.reshape(32, 16, 16, SLAB), PLANE, 0, 0, tiled=True).reshape(8, 4, 2, 8, 16, SLAB)
     sent, mgw = call(

time: 240 us -> 236 us (0.983)
  waiting for transfers between devices: 100 us -> 93.8 us
  local copies, waits for them, and re-layouts: 21.9 us -> 24.3 us
    ppermute x6, waiting for transfers between devices: 11 us -> 8.33 us  [gathered(): lax.ppermute(own, ('y', 'core'), [(k, k ^ s) for k in range(8)])]
    all_to_all x1, starting transfers between devices: 6.41 us -> 9.08 us  [local(): lax.all_to_all(mixed.reshape(32, 16, 16, SLAB), PLANE, 0, 0, tiled=True)]
    unnamed x50 -> x52, local copies, waits for them, and re-layouts: 18.5 us -> 20.9 us
  transfers between devices with their start and end apart: 38 -> 38, of which waited for: 23 -> 24; matrix products, arithmetic and copies ran while one was open for 2% -> 2% of each run, Pallas kernels for 9% -> 10%
where the time goes in v5:
time: 236 us; the launch traced here: 233 us
  waiting for transfers between devices  93.8 us (40%)
  starting transfers between devices  78.4 us (33%)
  Pallas kernels  33.3 us (14%)
  local copies, waits for them, and re-layouts  24.3 us (10%)
    unnamed x52, local copies, waits for them, and re-layouts  20.9 us
    ppermute x7, waiting for transfers between devices, local(): lax.ppermute(mg[t], ('y', 'core'), eight(t))  14.7 us
    ppermute x6, waiting for transfers between devices, local(): lax.ppermute(group[s], 'x', four(s))  12.1 us
    all_to_all x1, waiting for transfers between devices, local(): lax.all_to_all(mixed.reshape(32, 16, 16, SLAB), PLANE, 0, 0, tiled=True)  11.9 us
    ppermute x3, waiting for transfers between devices, local(): lax.ppermute(sums[t], 'y', four(t))  11.8 us
    all_to_all x1, starting transfers between devices, local(): lax.all_to_all(gated.reshape(64, 8, 16, SLAB), ZYC, 0, 0, tiled=True)  11.6 us
    all_to_all x1, starting transfers between devices, local(): home = lax.all_to_all(sent.reshape(32, 4, 64, SLAB), ZX, 0, 0, tiled=True)  10.4 us
    ppermute x1, waiting for transfers between devices, local(): lax.ppermute(sums, ('zh', 'x'), [(a * 4 + b, b * 4 + a) for a in range(4)...  9.51 us
  transfers between devices with their start and end apart: 38, of which 24 were waited for; matrix products, arithmetic and copies ran while one was open for 2% of the time, Pallas kernels for 10%

profile of v5, /device:TPU:70, one launch (start us, length us, event | category | flops | bytes accessed | tf_op | source)
XLA Modules:
  0.0 232.8 jit_solution(5061756216051339087)
XLA Ops:
  0.6 1.6 copy-done.1
  2.2 4.7 %shard_map.77 = bf16[4,8,2,8,16,128]{5,4,3,2,1,0:T(8,128)(2,1)} custom-call(bf16[16,64,1024]{2,1,0:T(8,128)(2,1)S(1)} %copy-done.1, bf16[16,64,1024]{2,1,0:T(8,128)(2,1)} %up.1), custom_call_target="tpu_custom_call" | custom-call | flops 1048576 | bytes 6291456 | tf_op jit(solution)/shard_map/pallas_call | solution.py:50
  6.9 11.6 %all-to-all-start = ((bf16[64,8,16,128]{3,2,1,0:T(8,128)(2,1)}), bf16[64,8,16,128]{3,2,1,0:T(8,128)(2,1)}, u32[]{:S(2)}, u32[]{:S(2)}) async-start(bf16[64,8,16,128]{3,2,1,0:T(8,128)(2,1)} %bitcast.6), calls=%async_computation | async-start | bytes 4194304 | tf_op jit(solution)/shard_map/all_to_all | solution.py:272
  20.0 1.3 collective-permute-start.1
  21.3 1.4 collective-permute-start.2
  22.7 2.7 %constant_dynamic-slice_fusion = (bf16[4,64,1024]{2,1,0:T(8,128)(2,1)}, bf16[4,64,1024]{2,1,0:T(8,128)(2,1)}, bf16[4,64,1024]{2,1,0:T(8,128)(2,1)S(1)}, bf16[4,64,1024]{2,1,0:T(8,128)(2,1)}) fusion(bf16[16,64,1024]{2,1,0:T(8,128)(2,1)} %param.5, s32[]{:T(128)S(6)} %select_n.88, s32[]{:T(128)S(6)} %select_n.84, s32[]{:T(128)S(6)} %select_n.82, s32[]{:T(128)S(6)} %select_n.86), kind=kLoop, calls=%fused_computation.4 | loop fusion | bytes 4194320 | tf_op jit(solution)/shard_map/dynamic_slice | solution.py:275
  25.4 1.2 collective-permute-start.6
  26.5 4.3 %collective-permute-start.7 = (bf16[4,64,1024]{2,1,0:T(8,128)(2,1)}, bf16[4,64,1024]{2,1,0:T(8,128)(2,1)S(1)}, u32[]{:S(2)}, u32[]{:S(2)}) collective-permute-start(bf16[4,64,1024]{2,1,0:T(8,128)(2,1)} %get-tuple-element.118), channel_id=1, source_target_pairs={{0,4},{2,6},{4,0},{6,2},{1,5},{3,7},{5,1},{7,3},{8,12},{10,14},{12... | collective-permute-start | bytes 1572872 | tf_op jit(solution)/shard_map/ppermute | solution.py:276
  30.9 1.4 collective-permute-start.8
  32.3 4.0 %collective-permute-done.1 = bf16[2,128,512]{2,1,0:T(8,128)(2,1)} collective-permute-done((bf16[2,128,512]{2,1,0:T(8,128)(2,1)}, bf16[2,128,512]{2,1,0:T(8,128)(2,1)}, u32[]{:S(2)}, u32[]{:S(2)}) %collective-permute-start.1) | collective-permute-done | bytes 262176 | tf_op jit(solution)/shard_map/ppermute | solution.py:283
  36.3 1.1 select_select_fusion
  37.4 1.6 collective-permute-start.10
  39.0 6.0 %collective-permute-done.10.refs_2_ = bf16[1,128,512]{2,1,0:T(8,128)(2,1)S(1)} collective-permute-done((bf16[1,128,512]{2,1,0:T(8,128)(2,1)S(1)}, bf16[1,128,512]{2,1,0:T(8,128)(2,1)S(1)}, u32[]{:S(2)}, u32[]{:S(2)}) %collective-permute-start.10) | collective-permute-done | bytes 131104 | tf_op jit(solution)/shard_map/ppermute | solution.py:287
  45.0 1.7 collective-permute-done.11.refs_3_
  46.7 1.0 collective-permute-start.3
  48.4 1.7 collective-permute-start.4
  51.9 5.8 %collective-permute-done.8.x3 = bf16[4,64,1024]{2,1,0:T(8,128)(2,1)S(1)} collective-permute-done((bf16[4,64,1024]{2,1,0:T(8,128)(2,1)}, bf16[4,64,1024]{2,1,0:T(8,128)(2,1)S(1)}, u32[]{:S(2)}, u32[]{:S(2)}) %collective-permute-start.8) | collective-permute-done | bytes 524320 | tf_op jit(solution)/shard_map/ppermute | solution.py:276
  57.8 0.9 shard_map.76
  58.7 1.4 copy-done
  60.6 7.2 %all-to-all-done = bf16[64,8,16,128]{3,2,1,0:T(8,128)(2,1)} async-done(((bf16[64,8,16,128]{3,2,1,0:T(8,128)(2,1)}), bf16[64,8,16,128]{3,2,1,0:T(8,128)(2,1)}, u32[]{:S(2)}, u32[]{:S(2)}) %all-to-all-start) | async-done | bytes 2097184 | tf_op jit(solution)/shard_map/all_to_all | solution.py:272
  67.9 6.4 %all-to-all-start.1 = ((bf16[8,16,64,128]{3,2,1,0:T(8,128)(2,1)}), bf16[8,16,64,128]{3,2,1,0:T(8,128)(2,1)S(1)}, u32[]{:S(2)}, u32[]{:S(2)}) async-start(bf16[8,16,64,128]{3,2,1,0:T(8,128)(2,1)} %bitcast.16), calls=%async_computation.1 | async-start | bytes 4194304 | tf_op jit(solution)/shard_map/all_to_all | solution.py:294
  74.3 4.7 %shard_map.80 = (bf16[4,4,4,16,128]{4,3,2,1,0:T(8,128)(2,1)S(1)}, bf16[4,4,4,16,128]{4,3,2,1,0:T(8,128)(2,1)S(1)}, bf16[4,4,4,16,128]{4,3,2,1,0:T(8,128)(2,1)S(1...) custom-call(s32[6]{0:T(128)S(1)} %stack.27.pos, ...), custom_call_target="tpu_custom_call" | custom-call | flops 1073741824 | bytes 4194304 | tf_op jit(solution)/shard_map/pallas_call | solution.py:298
  79.0 1.3 copy-done.2
  80.3 1.1 collective-permute-start.18
  81.4 3.2 %collective-permute-start.20 = (bf16[4,4,4,16,128]{4,3,2,1,0:T(8,128)(2,1)S(1)}, bf16[4,4,4,16,128]{4,3,2,1,0:T(8,128)(2,1)S(1)}, u32[]{:S(2)}, u32[]{:S(2)}) collective-permute-start(bf16[4,4,4,16,128]{4,3,2,1,0:T(8,128)(2,1)S(1)} %get-tuple-element.77), channel_id=1, source_target_pairs={{0,40},{8,48},{16,56},{24,0},{32,8},{40,16},{48,24},{56,32},{1,41}... | collective-permute-start | bytes 786440 | tf_op jit(solution)/shard_map/ppermute | solution.py:307
  84.7 1.8 collective-permute-start.21
  86.5 7.3 %collective-permute-done.18.a = bf16[4,4,4,16,128]{4,3,2,1,0:T(8,128)(2,1)S(1)} collective-permute-done((bf16[4,4,4,16,128]{4,3,2,1,0:T(8,128)(2,1)S(1)}, bf16[4,4,4,16,128]{4,3,2,1,0:T(8,128)(2,1)S(1)}, u32[]{:S(2)}, u32[]{:S(2)}) %collective-permute-start.18) | collective-permute-done | bytes 262176 | tf_op jit(solution)/shard_map/ppermute | solution.py:307
  94.7 1.8 collective-permute-done.20.c
  96.5 4.0 %collective-permute-done.21.d = bf16[4,4,4,16,128]{4,3,2,1,0:T(8,128)(2,1)S(1)} collective-permute-done((bf16[4,4,4,16,128]{4,3,2,1,0:T(8,128)(2,1)S(1)}, bf16[4,4,4,16,128]{4,3,2,1,0:T(8,128)(2,1)S(1)}, u32[]{:S(2)}, u32[]{:S(2)}) %collective-permute-start.21) | collective-permute-done | bytes 262176 | tf_op jit(solution)/shard_map/ppermute | solution.py:307
  101.7 2.5 %collective-permute-start.23 = (bf16[4,4,4,16,128]{4,3,2,1,0:T(8,128)(2,1)S(1)}, bf16[4,4,4,16,128]{4,3,2,1,0:T(8,128)(2,1)S(1)}, u32[]{:S(2)}, u32[]{:S(2)}) collective-permute-start(bf16[4,4,4,16,128]{4,3,2,1,0:T(8,128)(2,1)S(1)} %get-tuple-element.81), channel_id=1, source_target_pairs={{0,4},{2,6},{4,0},{6,2},{1,5},{3,7},{5,1},{7,3},{8,12},{10,14},{12... | collective-permute-start | bytes 786440 | tf_op jit(solution)/shard_map/ppermute | solution.py:309
  104.2 1.5 collective-permute-done.14.d
  107.0 1.7 collective-permute-start.15
  108.7 1.2 collective-permute-start.16
  114.3 3.8 %collective-permute-done.24.refs_7_ = bf16[4,4,4,16,128]{4,3,2,1,0:T(8,128)(2,1)S(1)} collective-permute-done((bf16[4,4,4,16,128]{4,3,2,1,0:T(8,128)(2,1)S(1)}, bf16[4,4,4,16,128]{4,3,2,1,0:T(8,128)(2,1)S(1)}, u32[]{:S(2)}, u32[]{:S(2)}) %collective-permute-start.24) | collective-permute-done | bytes 262176 | tf_op jit(solution)/shard_map/ppermute | solution.py:309
  118.9 2.8 %collective-permute-done.15.refs_1_ = bf16[4,4,4,16,128]{4,3,2,1,0:T(8,128)(2,1)S(1)} collective-permute-done((bf16[4,4,4,16,128]{4,3,2,1,0:T(8,128)(2,1)S(1)}, bf16[4,4,4,16,128]{4,3,2,1,0:T(8,128)(2,1)S(1)}, u32[]{:S(2)}, u32[]{:S(2)}) %collective-permute-start.15) | collective-permute-done | bytes 262176 | tf_op jit(solution)/shard_map/ppermute | solution.py:309
  122.4 1.4 collective-permute-done.16.refs_2_
  124.4 3.6 %collective-permute-done.17.refs_3_ = bf16[4,4,4,16,128]{4,3,2,1,0:T(8,128)(2,1)S(1)} collective-permute-done((bf16[4,4,4,16,128]{4,3,2,1,0:T(8,128)(2,1)S(1)}, bf16[4,4,4,16,128]{4,3,2,1,0:T(8,128)(2,1)S(1)}, u32[]{:S(2)}, u32[]{:S(2)}) %collective-permute-start.17) | collective-permute-done | bytes 262176 | tf_op jit(solution)/shard_map/ppermute | solution.py:309
  128.7 3.7 %shard_map.83 = bf16[8,4,2,8,16,128]{5,4,3,2,1,0:T(8,128)(2,1)} custom-call(s32[6]{0:T(128)S(1)} %stack.27.pos, bf16[512,512]{1,0:T(8,128)(2,1)S(1)} %get-tuple-element.63.f1, bf16[4,2,4,4,64,128]{5,4,3,2,1,0:T(8,128)(2,1)S(1)} %bitcast.14), custom_call_target="tpu_custom_call" | custom-call | flops 1073741824 | bytes 4194304 | tf_op jit(solution)/shard_map/pallas_call | solution.py:314
  132.5 9.1 %all-to-all-start.2 = ((bf16[32,16,16,128]{3,2,1,0:T(8,128)(2,1)}), bf16[32,16,16,128]{3,2,1,0:T(8,128)(2,1)}, u32[]{:S(2)}, u32[]{:S(2)}) async-start(bf16[32,16,16,128]{3,2,1,0:T(8,128)(2,1)} %bitcast.19), calls=%async_computation.2 | async-start | bytes 4194304 | tf_op jit(solution)/shard_map/all_to_all | solution.py:317
  141.6 0.9 copy-done.15
  142.6 0.9 copy-done.17
  143.5 0.9 copy-done.19
  144.5 0.9 copy-done.21
  145.4 0.9 copy-done.23
  146.4 2.2 shard_map.84
  148.6 1.4 copy-done.4
  150.0 1.6 copy-done.5
  151.6 3.9 %shard_map.85 = (f32[4,4,16,512]{3,2,1,0:T(8,128)S(1)}, f32[4,4,16,512]{3,2,1,0:T(8,128)S(1)}) custom-call(s32[6]{0:T(128)S(1)} %stack.27.pos, bf16[512,2048]{1,0:T(8,128)(2,1)S(1)} %copy-done.5, bf16[4,2,4,4,64,128]{5,4,3,2,1,0:T(8,128)(2,1)S(1)} %bitcast.15), custom_call_target="tpu_custom_call" | custom-call | flops 1073741824 | bytes 4194304 | tf_op jit(solution)/shard_map/pallas_call | solution.py:322
  155.6 11.9 %all-to-all-done.2 = bf16[32,16,16,128]{3,2,1,0:T(8,128)(2,1)} async-done(((bf16[32,16,16,128]{3,2,1,0:T(8,128)(2,1)}), bf16[32,16,16,128]{3,2,1,0:T(8,128)(2,1)}, u32[]{:S(2)}, u32[]{:S(2)}) %all-to-all-start.2) | async-done | bytes 2097184 | tf_op jit(solution)/shard_map/all_to_all | solution.py:317
  167.5 10.4 %all-to-all-start.3 = ((bf16[32,4,64,128]{3,2,1,0:T(8,128)(2,1)}), bf16[32,4,64,128]{3,2,1,0:T(8,128)(2,1)S(1)}, u32[]{:S(2)}, u32[]{:S(2)}) async-start(bf16[32,4,64,128]{3,2,1,0:T(8,128)(2,1)} %bitcast.18), calls=%async_computation.3 | async-start | bytes 4194304 | tf_op jit(solution)/shard_map/all_to_all | solution.py:325
  177.9 1.6 copy-done.3
  179.5 5.0 %shard_map.86 = (f32[4,4,16,512]{3,2,1,0:T(8,128)S(1)}, f32[4,4,16,512]{3,2,1,0:T(8,128)S(1)}) custom-call(s32[6]{0:T(128)S(1)} %stack.27.pos, bf16[512,2048]{1,0:T(8,128)(2,1)S(1)} %copy-done.3, bf16[8,4,2,8,16,128]{5,4,3,2,1,0:T(8,128)(2,1)} %bitcast.11.mixed), custom_call_target="tpu_custom_call" | custom-call | flops 1073741824 | bytes 4194304 | tf_op jit(solution)/shard_map/pallas_call | solution.py:326
  185.1 1.4 collective-permute-done.26.so
  188.5 1.7 collective-permute-start.28
  190.3 1.7 collective-permute-start.29
  192.0 11.2 %collective-permute-done.27.b = f32[4,2,16,512]{3,2,1,0:T(8,128)S(1)} collective-permute-done((f32[4,2,16,512]{3,2,1,0:T(8,128)S(1)}, f32[4,2,16,512]{3,2,1,0:T(8,128)S(1)}, u32[]{:S(2)}, u32[]{:S(2)}) %collective-permute-start.27) | collective-permute-done | bytes 262176 | tf_op jit(solution)/shard_map/ppermute | solution.py:332
  205.0 2.4 %collective-permute-start.31 = (f32[2,16,512]{2,1,0:T(8,128)S(1)}, f32[2,16,512]{2,1,0:T(8,128)S(1)}, u32[]{:S(2)}, u32[]{:S(2)}) collective-permute-start(f32[2,16,512]{2,1,0:T(8,128)S(1)} %get-tuple-element.110), channel_id=1, source_target_pairs={{0,4},{2,6},{4,0},{6,2},{1,5},{3,7},{5,1},{7,3},{8,12},{10,14},{12... | collective-permute-start | bytes 196616 | tf_op jit(solution)/shard_map/ppermute | solution.py:334
  207.4 2.6 %collective-permute-done.30.b = f32[2,16,512]{2,1,0:T(8,128)S(1)} collective-permute-done((f32[2,16,512]{2,1,0:T(8,128)S(1)}, f32[2,16,512]{2,1,0:T(8,128)S(1)}, u32[]{:S(2)}, u32[]{:S(2)}) %collective-permute-start.30) | collective-permute-done | bytes 65568 | tf_op jit(solution)/shard_map/ppermute | solution.py:334
  210.0 1.1 collective-permute-done.31.c
  211.1 2.5 %collective-permute-done.32.d = f32[2,16,512]{2,1,0:T(8,128)S(1)} collective-permute-done((f32[2,16,512]{2,1,0:T(8,128)S(1)}, f32[2,16,512]{2,1,0:T(8,128)S(1)}, u32[]{:S(2)}, u32[]{:S(2)}) %collective-permute-start.32) | collective-permute-done | bytes 65568 | tf_op jit(solution)/shard_map/ppermute | solution.py:334
  213.6 1.2 shard_map.89
  214.8 4.9 %collective-permute-start.33 = (f32[2,16,512]{2,1,0:T(8,128)S(1)}, f32[2,16,512]{2,1,0:T(8,128)S(1)}, u32[]{:S(2)}, u32[]{:S(2)}) collective-permute-start(f32[2,16,512]{2,1,0:T(8,128)S(1)} %shard_map.89), channel_id=1, source_target_pairs={{0,0},{2,64},{4,128},{6,192},{64,2},{66,66},{68,130},{70,194},{128... | collective-permute-start | bytes 196616 | tf_op jit(solution)/shard_map/ppermute | solution.py:336
  219.7 9.5 %collective-permute-done.33 = f32[2,16,512]{2,1,0:T(8,128)S(1)} collective-permute-done((f32[2,16,512]{2,1,0:T(8,128)S(1)}, f32[2,16,512]{2,1,0:T(8,128)S(1)}, u32[]{:S(2)}, u32[]{:S(2)}) %collective-permute-start.33) | collective-permute-done | bytes 65568 | tf_op jit(solution)/shard_map/ppermute | solution.py:336
  229.9 2.8 %shard_map.90 = bf16[16,64,1024]{2,1,0:T(8,128)(2,1)} custom-call(s32[6]{0:T(128)S(1)} %stack.27.pos, bf16[4,4,2,4,64,128]{5,4,3,2,1,0:T(8,128)(2,1)S(1)} %bitcast.17), custom_call_target="tpu_custom_call" | custom-call | bytes 4194304 | tf_op jit(solution)/shard_map/pallas_call | solution.py:338
  (85 shorter events, 20.3 us)
Async XLA Ops:
  0.6 1.6 copy-start.1
  6.9 11.7 %copy-start.24 = (bf16[1,512,512]{2,1,0:T(8,128)(2,1)S(1)}, bf16[1,512,512]{2,1,0:T(8,128)(2,1)}, u32[]{:S(2)}) copy-start(bf16[1,512,512]{2,1,0:T(8,128)(2,1)} %param.8) | copy-start | bytes 1572868
  6.9 11.7 %copy-start.25 = (bf16[1,512,512]{2,1,0:T(8,128)(2,1)S(1)}, bf16[1,512,512]{2,1,0:T(8,128)(2,1)}, u32[]{:S(2)}) copy-start(bf16[1,512,512]{2,1,0:T(8,128)(2,1)} %param.9) | copy-start | bytes 1572868
  6.9 61.0 %all-to-all-start = ((bf16[64,8,16,128]{3,2,1,0:T(8,128)(2,1)}), bf16[64,8,16,128]{3,2,1,0:T(8,128)(2,1)}, u32[]{:S(2)}, u32[]{:S(2)}) async-start(bf16[64,8,16,128]{3,2,1,0:T(8,128)(2,1)} %bitcast.6), calls=%async_computation | async-start | bytes 4194304 | tf_op jit(solution)/shard_map/all_to_all | solution.py:272
  19.3 11.6 %collective-permute-start = (bf16[2,128,512]{2,1,0:T(8,128)(2,1)}, bf16[2,128,512]{2,1,0:T(8,128)(2,1)S(1)}, u32[]{:S(2)}, u32[]{:S(2)}) collective-permute-start(bf16[2,128,512]{2,1,0:T(8,128)(2,1)} %fusion), channel_id=1, source_target_pairs={{0,6},{66,64},{132,130},{198,196},{1,7},{67,65},{133,131},{199,197... | collective-permute-start | bytes 786440 | tf_op jit(solution)/shard_map/ppermute | solution.py:283
  20.0 16.3 %collective-permute-start.1 = (bf16[2,128,512]{2,1,0:T(8,128)(2,1)}, bf16[2,128,512]{2,1,0:T(8,128)(2,1)}, u32[]{:S(2)}, u32[]{:S(2)}) collective-permute-start(bf16[2,128,512]{2,1,0:T(8,128)(2,1)} %fusion), channel_id=1, source_target_pairs={{0,4},{66,70},{132,128},{198,194},{1,5},{67,71},{133,129},{199,195... | collective-permute-start | bytes 786440 | tf_op jit(solution)/shard_map/ppermute | solution.py:283
  21.3 15.0 %collective-permute-start.2 = (bf16[2,128,512]{2,1,0:T(8,128)(2,1)}, bf16[2,128,512]{2,1,0:T(8,128)(2,1)}, u32[]{:S(2)}, u32[]{:S(2)}) collective-permute-start(bf16[2,128,512]{2,1,0:T(8,128)(2,1)} %fusion), channel_id=1, source_target_pairs={{0,2},{66,68},{132,134},{198,192},{1,3},{67,69},{133,135},{199,193... | collective-permute-start | bytes 786440 | tf_op jit(solution)/shard_map/ppermute | solution.py:283
  25.4 24.7 %collective-permute-start.6 = (bf16[4,64,1024]{2,1,0:T(8,128)(2,1)}, bf16[4,64,1024]{2,1,0:T(8,128)(2,1)S(1)}, u32[]{:S(2)}, u32[]{:S(2)}) collective-permute-start(bf16[4,64,1024]{2,1,0:T(8,128)(2,1)} %get-tuple-element.116), channel_id=1, source_target_pairs={{0,2},{2,4},{4,6},{6,0},{1,3},{3,5},{5,7},{7,1},{8,10},{10,12},{12... | collective-permute-start | bytes 1572872 | tf_op jit(solution)/shard_map/ppermute | solution.py:276
  26.5 25.4 %collective-permute-start.7 = (bf16[4,64,1024]{2,1,0:T(8,128)(2,1)}, bf16[4,64,1024]{2,1,0:T(8,128)(2,1)S(1)}, u32[]{:S(2)}, u32[]{:S(2)}) collective-permute-start(bf16[4,64,1024]{2,1,0:T(8,128)(2,1)} %get-tuple-element.118), channel_id=1, source_target_pairs={{0,4},{2,6},{4,0},{6,2},{1,5},{3,7},{5,1},{7,3},{8,12},{10,14},{12... | collective-permute-start | bytes 1572872 | tf_op jit(solution)/shard_map/ppermute | solution.py:276
  30.9 26.9 %collective-permute-start.8 = (bf16[4,64,1024]{2,1,0:T(8,128)(2,1)}, bf16[4,64,1024]{2,1,0:T(8,128)(2,1)S(1)}, u32[]{:S(2)}, u32[]{:S(2)}) collective-permute-start(bf16[4,64,1024]{2,1,0:T(8,128)(2,1)} %get-tuple-element.115), channel_id=1, source_target_pairs={{0,6},{2,0},{4,2},{6,4},{1,7},{3,1},{5,3},{7,5},{8,14},{10,8},{12,... | collective-permute-start | bytes 1572872 | tf_op jit(solution)/shard_map/ppermute | solution.py:276
  37.4 7.6 %collective-permute-start.10 = (bf16[1,128,512]{2,1,0:T(8,128)(2,1)S(1)}, bf16[1,128,512]{2,1,0:T(8,128)(2,1)S(1)}, u32[]{:S(2)}, u32[]{:S(2)}) collective-permute-start(bf16[1,128,512]{2,1,0:T(8,128)(2,1)S(1)} %get-tuple-element.119.refs_0_), channel_id=1, source_target_pairs={{0,16},{8,24},{16,0},{24,8},{32,48},{40,56},{48,32},{56,40},{1,17}... | collective-permute-start | bytes 393224 | tf_op jit(solution)/shard_map/ppermute | solution.py:287
  39.0 7.7 %collective-permute-start.11 = (bf16[1,128,512]{2,1,0:T(8,128)(2,1)S(1)}, bf16[1,128,512]{2,1,0:T(8,128)(2,1)S(1)}, u32[]{:S(2)}, u32[]{:S(2)}) collective-permute-start(bf16[1,128,512]{2,1,0:T(8,128)(2,1)S(1)} %get-tuple-element.119.refs_0_), channel_id=1, source_target_pairs={{0,24},{8,16},{16,8},{24,0},{32,56},{40,48},{48,40},{56,32},{1,25}... | collective-permute-start | bytes 393224 | tf_op jit(solution)/shard_map/ppermute | solution.py:287
  45.0 2.7 %collective-permute-start.9 = (bf16[1,128,512]{2,1,0:T(8,128)(2,1)S(1)}, bf16[1,128,512]{2,1,0:T(8,128)(2,1)S(1)}, u32[]{:S(2)}, u32[]{:S(2)}) collective-permute-start(bf16[1,128,512]{2,1,0:T(8,128)(2,1)S(1)} %get-tuple-element.119.refs_0_), channel_id=1, source_target_pairs={{0,8},{8,0},{16,24},{24,16},{32,40},{40,32},{48,56},{56,48},{1,9},... | collective-permute-start | bytes 393224 | tf_op jit(solution)/shard_map/ppermute | solution.py:287
  46.7 13.3 %collective-permute-start.3 = (bf16[1,128,512]{2,1,0:T(8,128)(2,1)S(1)}, bf16[1,128,512]{2,1,0:T(8,128)(2,1)S(1)}, u32[]{:S(2)}, u32[]{:S(2)}) collective-permute-start(bf16[1,128,512]{2,1,0:T(8,128)(2,1)S(1)} %get-tuple-element.59.refs_0_), channel_id=1, source_target_pairs={{0,8},{8,0},{16,24},{24,16},{32,40},{40,32},{48,56},{56,48},{1,9},... | collective-permute-start | bytes 393224 | tf_op jit(solution)/shard_map/ppermute | solution.py:287
  47.7 0.7 copy-start.6
  48.4 11.7 %collective-permute-start.4 = (bf16[1,128,512]{2,1,0:T(8,128)(2,1)S(1)}, bf16[1,128,512]{2,1,0:T(8,128)(2,1)S(1)}, u32[]{:S(2)}, u32[]{:S(2)}) collective-permute-start(bf16[1,128,512]{2,1,0:T(8,128)(2,1)S(1)} %get-tuple-element.59.refs_0_), channel_id=1, source_target_pairs={{0,16},{8,24},{16,0},{24,8},{32,48},{40,56},{48,32},{56,40},{1,17}... | collective-permute-start | bytes 393224 | tf_op jit(solution)/shard_map/ppermute | solution.py:287
  50.1 10.5 %collective-permute-start.5 = (bf16[1,128,512]{2,1,0:T(8,128)(2,1)S(1)}, bf16[1,128,512]{2,1,0:T(8,128)(2,1)S(1)}, u32[]{:S(2)}, u32[]{:S(2)}) collective-permute-start(bf16[1,128,512]{2,1,0:T(8,128)(2,1)S(1)} %get-tuple-element.59.refs_0_), channel_id=1, source_target_pairs={{0,24},{8,16},{16,8},{24,0},{32,56},{40,48},{48,40},{56,32},{1,25}... | collective-permute-start | bytes 393224 | tf_op jit(solution)/shard_map/ppermute | solution.py:287
  50.2 0.9 copy-start.7
  58.7 1.4 copy-start
  67.9 60.8 %all-to-all-start.1 = ((bf16[8,16,64,128]{3,2,1,0:T(8,128)(2,1)}), bf16[8,16,64,128]{3,2,1,0:T(8,128)(2,1)S(1)}, u32[]{:S(2)}, u32[]{:S(2)}) async-start(bf16[8,16,64,128]{3,2,1,0:T(8,128)(2,1)} %bitcast.16), calls=%async_computation.1 | async-start | bytes 4194304 | tf_op jit(solution)/shard_map/all_to_all | solution.py:294
  79.0 1.3 copy-start.2
  80.3 13.5 %collective-permute-start.18 = (bf16[4,4,4,16,128]{4,3,2,1,0:T(8,128)(2,1)S(1)}, bf16[4,4,4,16,128]{4,3,2,1,0:T(8,128)(2,1)S(1)}, u32[]{:S(2)}, u32[]{:S(2)}) collective-permute-start(bf16[4,4,4,16,128]{4,3,2,1,0:T(8,128)(2,1)S(1)} %get-tuple-element.75), channel_id=1, source_target_pairs={{0,48},{8,56},{16,0},{24,8},{32,16},{40,24},{48,32},{56,40},{1,49}... | collective-permute-start | bytes 786440 | tf_op jit(solution)/shard_map/ppermute | solution.py:307
  81.4 12.4 %collective-permute-start.19 = (bf16[4,4,4,16,128]{4,3,2,1,0:T(8,128)(2,1)S(1)}, bf16[4,4,4,16,128]{4,3,2,1,0:T(8,128)(2,1)S(1)}, u32[]{:S(2)}, u32[]{:S(2)}) collective-permute-start(bf16[4,4,4,16,128]{4,3,2,1,0:T(8,128)(2,1)S(1)} %get-tuple-element.76), channel_id=1, source_target_pairs={{0,24},{8,32},{16,40},{24,48},{32,56},{40,0},{48,8},{56,16},{1,25}... | collective-permute-start | bytes 786440 | tf_op jit(solution)/shard_map/ppermute | solution.py:307
  81.4 15.1 %collective-permute-start.20 = (bf16[4,4,4,16,128]{4,3,2,1,0:T(8,128)(2,1)S(1)}, bf16[4,4,4,16,128]{4,3,2,1,0:T(8,128)(2,1)S(1)}, u32[]{:S(2)}, u32[]{:S(2)}) collective-permute-start(bf16[4,4,4,16,128]{4,3,2,1,0:T(8,128)(2,1)S(1)} %get-tuple-element.77), channel_id=1, source_target_pairs={{0,40},{8,48},{16,56},{24,0},{32,8},{40,16},{48,24},{56,32},{1,41}... | collective-permute-start | bytes 786440 | tf_op jit(solution)/shard_map/ppermute | solution.py:307
  84.7 15.8 %collective-permute-start.21 = (bf16[4,4,4,16,128]{4,3,2,1,0:T(8,128)(2,1)S(1)}, bf16[4,4,4,16,128]{4,3,2,1,0:T(8,128)(2,1)S(1)}, u32[]{:S(2)}, u32[]{:S(2)}) collective-permute-start(bf16[4,4,4,16,128]{4,3,2,1,0:T(8,128)(2,1)S(1)} %get-tuple-element.78), channel_id=1, source_target_pairs={{0,32},{8,40},{16,48},{24,56},{32,0},{40,8},{48,16},{56,24},{1,33}... | collective-permute-start | bytes 786440 | tf_op jit(solution)/shard_map/ppermute | solution.py:307
  86.5 17.7 %collective-permute-start.12 = (bf16[4,4,4,16,128]{4,3,2,1,0:T(8,128)(2,1)S(1)}, bf16[4,4,4,16,128]{4,3,2,1,0:T(8,128)(2,1)S(1)}, u32[]{:S(2)}, u32[]{:S(2)}) collective-permute-start(bf16[4,4,4,16,128]{4,3,2,1,0:T(8,128)(2,1)S(1)} %get-tuple-element.68), channel_id=1, source_target_pairs={{0,8},{8,16},{16,24},{24,32},{32,40},{40,48},{48,56},{56,0},{1,9},... | collective-permute-start | bytes 786440 | tf_op jit(solution)/shard_map/ppermute | solution.py:307
  93.8 10.4 %collective-permute-start.13 = (bf16[4,4,4,16,128]{4,3,2,1,0:T(8,128)(2,1)S(1)}, bf16[4,4,4,16,128]{4,3,2,1,0:T(8,128)(2,1)S(1)}, u32[]{:S(2)}, u32[]{:S(2)}) collective-permute-start(bf16[4,4,4,16,128]{4,3,2,1,0:T(8,128)(2,1)S(1)} %get-tuple-element.69), channel_id=1, source_target_pairs={{0,56},{8,0},{16,8},{24,16},{32,24},{40,32},{48,40},{56,48},{1,57}... | collective-permute-start | bytes 786440 | tf_op jit(solution)/shard_map/ppermute | solution.py:307
  93.8 11.9 %collective-permute-start.14 = (bf16[4,4,4,16,128]{4,3,2,1,0:T(8,128)(2,1)S(1)}, bf16[4,4,4,16,128]{4,3,2,1,0:T(8,128)(2,1)S(1)}, u32[]{:S(2)}, u32[]{:S(2)}) collective-permute-start(bf16[4,4,4,16,128]{4,3,2,1,0:T(8,128)(2,1)S(1)} %get-tuple-element.70), channel_id=1, source_target_pairs={{0,16},{8,24},{16,32},{24,40},{32,48},{40,56},{48,0},{56,8},{1,17}... | collective-permute-start | bytes 786440 | tf_op jit(solution)/shard_map/ppermute | solution.py:307
  101.1 9.2 %collective-permute-start.22 = (bf16[4,4,4,16,128]{4,3,2,1,0:T(8,128)(2,1)S(1)}, bf16[4,4,4,16,128]{4,3,2,1,0:T(8,128)(2,1)S(1)}, u32[]{:S(2)}, u32[]{:S(2)}) collective-permute-start(bf16[4,4,4,16,128]{4,3,2,1,0:T(8,128)(2,1)S(1)} %get-tuple-element.80), channel_id=1, source_target_pairs={{0,2},{2,4},{4,6},{6,0},{1,3},{3,5},{5,7},{7,1},{8,10},{10,12},{12... | collective-permute-start | bytes 786440 | tf_op jit(solution)/shard_map/ppermute | solution.py:309
  101.7 11.9 %collective-permute-start.23 = (bf16[4,4,4,16,128]{4,3,2,1,0:T(8,128)(2,1)S(1)}, bf16[4,4,4,16,128]{4,3,2,1,0:T(8,128)(2,1)S(1)}, u32[]{:S(2)}, u32[]{:S(2)}) collective-permute-start(bf16[4,4,4,16,128]{4,3,2,1,0:T(8,128)(2,1)S(1)} %get-tuple-element.81), channel_id=1, source_target_pairs={{0,4},{2,6},{4,0},{6,2},{1,5},{3,7},{5,1},{7,3},{8,12},{10,14},{12... | collective-permute-start | bytes 786440 | tf_op jit(solution)/shard_map/ppermute | solution.py:309
  104.2 14.0 %collective-permute-start.24 = (bf16[4,4,4,16,128]{4,3,2,1,0:T(8,128)(2,1)S(1)}, bf16[4,4,4,16,128]{4,3,2,1,0:T(8,128)(2,1)S(1)}, u32[]{:S(2)}, u32[]{:S(2)}) collective-permute-start(bf16[4,4,4,16,128]{4,3,2,1,0:T(8,128)(2,1)S(1)} %get-tuple-element.82), channel_id=1, source_target_pairs={{0,6},{2,0},{4,2},{6,4},{1,7},{3,1},{5,3},{7,5},{8,14},{10,8},{12,... | collective-permute-start | bytes 786440 | tf_op jit(solution)/shard_map/ppermute | solution.py:309
  106.3 0.7 copy-start.16
  107.0 14.6 %collective-permute-start.15 = (bf16[4,4,4,16,128]{4,3,2,1,0:T(8,128)(2,1)S(1)}, bf16[4,4,4,16,128]{4,3,2,1,0:T(8,128)(2,1)S(1)}, u32[]{:S(2)}, u32[]{:S(2)}) collective-permute-start(bf16[4,4,4,16,128]{4,3,2,1,0:T(8,128)(2,1)S(1)} %get-tuple-element.72), channel_id=1, source_target_pairs={{0,2},{2,4},{4,6},{6,0},{1,3},{3,5},{5,7},{7,1},{8,10},{10,12},{12... | collective-permute-start | bytes 786440 | tf_op jit(solution)/shard_map/ppermute | solution.py:309
  108.7 15.0 %collective-permute-start.16 = (bf16[4,4,4,16,128]{4,3,2,1,0:T(8,128)(2,1)S(1)}, bf16[4,4,4,16,128]{4,3,2,1,0:T(8,128)(2,1)S(1)}, u32[]{:S(2)}, u32[]{:S(2)}) collective-permute-start(bf16[4,4,4,16,128]{4,3,2,1,0:T(8,128)(2,1)S(1)} %get-tuple-element.73), channel_id=1, source_target_pairs={{0,4},{2,6},{4,0},{6,2},{1,5},{3,7},{5,1},{7,3},{8,12},{10,14},{12... | collective-permute-start | bytes 786440 | tf_op jit(solution)/shard_map/ppermute | solution.py:309
  110.4 0.7 copy-start.10
  111.1 16.9 %collective-permute-start.17 = (bf16[4,4,4,16,128]{4,3,2,1,0:T(8,128)(2,1)S(1)}, bf16[4,4,4,16,128]{4,3,2,1,0:T(8,128)(2,1)S(1)}, u32[]{:S(2)}, u32[]{:S(2)}) collective-permute-start(bf16[4,4,4,16,128]{4,3,2,1,0:T(8,128)(2,1)S(1)} %get-tuple-element.74), channel_id=1, source_target_pairs={{0,6},{2,0},{4,2},{6,4},{1,7},{3,1},{5,3},{7,5},{8,14},{10,8},{12,... | collective-permute-start | bytes 786440 | tf_op jit(solution)/shard_map/ppermute | solution.py:309
  112.8 0.8 copy-start.8
  113.6 0.7 copy-start.12
  118.1 0.7 copy-start.14
  121.7 0.7 copy-start.18
  123.7 0.7 copy-start.20
  128.0 0.7 copy-start.22
  132.5 9.1 %copy-start.9 = (bf16[512,512]{1,0:T(8,128)(2,1)S(1)}, bf16[512,512]{1,0:T(8,128)(2,1)}, u32[]{:S(2)}) copy-start(bf16[512,512]{1,0:T(8,128)(2,1)} %copy-done.8) | copy-start | bytes 1572868
  132.5 9.1 %copy-start.11 = (bf16[4,4,4,16,128]{4,3,2,1,0:T(8,128)(2,1)S(1)}, bf16[4,4,4,16,128]{4,3,2,1,0:T(8,128)(2,1)}, u32[]{:S(2)}) copy-start(bf16[4,4,4,16,128]{4,3,2,1,0:T(8,128)(2,1)} %copy-done.10) | copy-start | bytes 786436
  132.5 9.1 %copy-start.13 = (bf16[4,4,4,16,128]{4,3,2,1,0:T(8,128)(2,1)S(1)}, bf16[4,4,4,16,128]{4,3,2,1,0:T(8,128)(2,1)}, u32[]{:S(2)}) copy-start(bf16[4,4,4,16,128]{4,3,2,1,0:T(8,128)(2,1)} %copy-done.12) | copy-start | bytes 786436
  132.5 35.0 %all-to-all-start.2 = ((bf16[32,16,16,128]{3,2,1,0:T(8,128)(2,1)}), bf16[32,16,16,128]{3,2,1,0:T(8,128)(2,1)}, u32[]{:S(2)}, u32[]{:S(2)}) async-start(bf16[32,16,16,128]{3,2,1,0:T(8,128)(2,1)} %bitcast.19), calls=%async_computation.2 | async-start | bytes 4194304 | tf_op jit(solution)/shard_map/all_to_all | solution.py:317
  141.6 1.0 copy-start.15
  142.6 0.9 copy-start.17
  143.5 0.9 copy-start.19
  144.5 0.9 copy-start.21
  145.4 0.9 copy-start.23
  148.6 1.4 copy-start.4
  150.0 1.6 copy-start.5
  167.5 62.4 %all-to-all-start.3 = ((bf16[32,4,64,128]{3,2,1,0:T(8,128)(2,1)}), bf16[32,4,64,128]{3,2,1,0:T(8,128)(2,1)S(1)}, u32[]{:S(2)}, u32[]{:S(2)}) async-start(bf16[32,4,64,128]{3,2,1,0:T(8,128)(2,1)} %bitcast.18), calls=%async_computation.3 | async-start | bytes 4194304 | tf_op jit(solution)/shard_map/all_to_all | solution.py:325
  177.9 1.6 copy-start.3
  184.5 2.0 collective-permute-start.26
  184.6 2.6 %collective-permute-start.25 = (f32[4,4,16,512]{3,2,1,0:T(8,128)S(1)}, f32[4,4,16,512]{3,2,1,0:T(8,128)S(1)}, u32[]{:S(2)}, u32[]{:S(2)}) collective-permute-start(f32[4,4,16,512]{3,2,1,0:T(8,128)S(1)} %get-tuple-element.99), channel_id=1, source_target_pairs={{0,8},{8,0},{1,9},{9,1},{2,10},{10,2},{3,11},{11,3},{4,12},{12,4},... | collective-permute-start | bytes 1572872 | tf_op jit(solution)/shard_map/ppermute | solution.py:328
  187.9 15.3 %collective-permute-start.27 = (f32[4,2,16,512]{3,2,1,0:T(8,128)S(1)}, f32[4,2,16,512]{3,2,1,0:T(8,128)S(1)}, u32[]{:S(2)}, u32[]{:S(2)}) collective-permute-start(f32[4,2,16,512]{3,2,1,0:T(8,128)S(1)} %get-tuple-element.105), channel_id=1, source_target_pairs={{0,16},{16,32},{32,48},{48,0},{1,17},{17,33},{33,49},{49,1},{2,18}... | collective-permute-start | bytes 786440 | tf_op jit(solution)/shard_map/ppermute | solution.py:332
  188.5 14.6 %collective-permute-start.28 = (f32[4,2,16,512]{3,2,1,0:T(8,128)S(1)}, f32[4,2,16,512]{3,2,1,0:T(8,128)S(1)}, u32[]{:S(2)}, u32[]{:S(2)}) collective-permute-start(f32[4,2,16,512]{3,2,1,0:T(8,128)S(1)} %get-tuple-element.106), channel_id=1, source_target_pairs={{0,32},{16,48},{32,0},{48,16},{1,33},{17,49},{33,1},{49,17},{2,34}... | collective-permute-start | bytes 786440 | tf_op jit(solution)/shard_map/ppermute | solution.py:332
  190.3 13.5 %collective-permute-start.29 = (f32[4,2,16,512]{3,2,1,0:T(8,128)S(1)}, f32[4,2,16,512]{3,2,1,0:T(8,128)S(1)}, u32[]{:S(2)}, u32[]{:S(2)}) collective-permute-start(f32[4,2,16,512]{3,2,1,0:T(8,128)S(1)} %get-tuple-element.107), channel_id=1, source_target_pairs={{0,48},{16,0},{32,16},{48,32},{1,49},{17,1},{33,17},{49,33},{2,50}... | collective-permute-start | bytes 786440 | tf_op jit(solution)/shard_map/ppermute | solution.py:332
  204.4 5.6 %collective-permute-start.30 = (f32[2,16,512]{2,1,0:T(8,128)S(1)}, f32[2,16,512]{2,1,0:T(8,128)S(1)}, u32[]{:S(2)}, u32[]{:S(2)}) collective-permute-start(f32[2,16,512]{2,1,0:T(8,128)S(1)} %get-tuple-element.109), channel_id=1, source_target_pairs={{0,2},{2,4},{4,6},{6,0},{1,3},{3,5},{5,7},{7,1},{8,10},{10,12},{12... | collective-permute-start | bytes 196616 | tf_op jit(solution)/shard_map/ppermute | solution.py:334
  205.0 6.1 %collective-permute-start.31 = (f32[2,16,512]{2,1,0:T(8,128)S(1)}, f32[2,16,512]{2,1,0:T(8,128)S(1)}, u32[]{:S(2)}, u32[]{:S(2)}) collective-permute-start(f32[2,16,512]{2,1,0:T(8,128)S(1)} %get-tuple-element.110), channel_id=1, source_target_pairs={{0,4},{2,6},{4,0},{6,2},{1,5},{3,7},{5,1},{7,3},{8,12},{10,14},{12... | collective-permute-start | bytes 196616 | tf_op jit(solution)/shard_map/ppermute | solution.py:334
  207.4 6.2 %collective-permute-start.32 = (f32[2,16,512]{2,1,0:T(8,128)S(1)}, f32[2,16,512]{2,1,0:T(8,128)S(1)}, u32[]{:S(2)}, u32[]{:S(2)}) collective-permute-start(f32[2,16,512]{2,1,0:T(8,128)S(1)} %get-tuple-element.111), channel_id=1, source_target_pairs={{0,6},{2,0},{4,2},{6,4},{1,7},{3,1},{5,3},{7,5},{8,14},{10,8},{12,... | collective-permute-start | bytes 196616 | tf_op jit(solution)/shard_map/ppermute | solution.py:334
  214.8 14.4 %collective-permute-start.33 = (f32[2,16,512]{2,1,0:T(8,128)S(1)}, f32[2,16,512]{2,1,0:T(8,128)S(1)}, u32[]{:S(2)}, u32[]{:S(2)}) collective-permute-start(f32[2,16,512]{2,1,0:T(8,128)S(1)} %shard_map.89), channel_id=1, source_target_pairs={{0,0},{2,64},{4,128},{6,192},{64,2},{66,66},{68,130},{70,194},{128... | collective-permute-start | bytes 196616 | tf_op jit(solution)/shard_map/ppermute | solution.py:336
